TPU v7x, 256 devices: a whole 4x4x8 slice. The times are simulated.
256 devices in a mesh: row: 4 (over x), col: 4 (over y), depth: 16 (over z, core).
Axes of the slice: x: 4, y: 4, z: 8, core: 2. Of those that a mesh axis runs over, the one named last changes fastest.
Arguments:
- three_center: bfloat16 [8192, 8192], P('col', ('row', 'depth')), may hold values from -6 to 6
- three_mask: int32 [256, 256], P('col', ('row', 'depth')), may hold values from 0 to 1, as said below
- density: bfloat16 [8192, 8192], P(('col', 'depth'), 'row'), may hold values from -0.375 to 0.375
- density_mask: int32 [256, 256], P(('col', 'depth'), 'row'), may hold values from 0 to 1, as said below
- nu_sizes: int32 [256], P(('row', 'depth')), may hold values from 5 to 32
Outputs:
- contracted: bfloat16 [8192, 8192], P('col', ('row', 'depth'))
Inputs may be any that keep to these rules, and one draw needn't show every extreme that they name: `three_mask`: 1 marks an occupied tile. `density_mask`: 1 marks an occupied tile.
All inputs are finite; a program needn't handle non-finite values.
Results may differ from a plain program's by a relative error of at most 0.022.
Values may be sent and summed in bfloat16 or wider, within the bound.
No kernel may reach another device: no remote copies, remote signals or barrier semaphores. Data moves between devices by JAX's collectives and lax.ppermute only.
A program may use at most 128 MiB of HBM per device.

v0:
```python
import jax
import jax.numpy as jnp
from jax import lax
from jax.sharding import PartitionSpec as P

BS = 32


def shifted(block, axis, distance):
    devices = range(lax.axis_size(axis))
    route = [((i - distance) % len(devices), i) for i in devices]
    return lax.ppermute(block, axis, route)


def mask_three(three_center, three_mask, nu_sizes):
    row_blocks = three_center.shape[0] // BS
    col_blocks = three_center.shape[1] // BS
    inside = (jnp.arange(BS)[None, :] < nu_sizes[:, None]).astype(jnp.int32)
    keep_mask = (three_mask[:, None, :, None] * inside[None, None, :, :]).astype(jnp.bfloat16)
    shaped = three_center.reshape(row_blocks, BS, col_blocks, BS) * keep_mask
    return shaped.reshape(three_center.shape)


def mask_density(density, density_mask):
    row_blocks = density.shape[0] // BS
    col_blocks = density.shape[1] // BS
    keep_mask = density_mask[:, None, :, None].astype(jnp.bfloat16)
    shaped = density.reshape(row_blocks, BS, col_blocks, BS) * keep_mask
    return shaped.reshape(density.shape)


def on_device(three_center, three_mask, density, density_mask, nu_sizes):
    live_tile = mask_three(three_center, three_mask, nu_sizes)
    dens_tile = mask_density(density, density_mask)
    empty_sum = jnp.zeros((live_tile.shape[0], dens_tile.shape[1]), jnp.float32)
    loop_size = lax.axis_size("row")
    bit_count = loop_size.bit_length() - 1
    row_index = lax.axis_index("row")
    col_index = lax.axis_index("col")
    for bit_index in range(bit_count):
        arrived = shifted(live_tile, "row", -(1 << bit_index))
        live_tile = jnp.where(col_index >> bit_index & 1 == 1, arrived, live_tile)
    for bit_index in range(bit_count):
        arrived = shifted(dens_tile, "col", -(1 << bit_index))
        dens_tile = jnp.where(row_index >> bit_index & 1 == 1, arrived, dens_tile)
    accum_sum = empty_sum
    for step_index in range(loop_size):
        accum_sum = accum_sum + jnp.dot(live_tile, dens_tile, preferred_element_type=jnp.float32)
        if step_index + 1 < loop_size:
            live_tile = shifted(live_tile, "row", -1)
            dens_tile = shifted(dens_tile, "col", -1)
    layered = lax.psum_scatter(
        accum_sum.astype(jnp.bfloat16), "depth", scatter_dimension=1, tiled=True
    )
    return layered


def solution(mesh):
    in_specs = (
        P("col", ("row", "depth")),
        P("col", ("row", "depth")),
        P(("col", "depth"), "row"),
        P(("col", "depth"), "row"),
        P(("row", "depth")),
    )
    out_specs = P("col", ("row", "depth"))
    return jax.shard_map(
        on_device, mesh=mesh, in_specs=in_specs, out_specs=out_specs, check_vma=False
    )
```

profile of v0, /device:TPU:24, one launch (start us, length us, event | category | flops | bytes accessed | tf_op | source)
XLA Modules:
  0.0 192.3 jit_solution(11909767397350880086)
XLA Ops:
  6.5 0.0 reduce-scatter.4.cloned.1.call-start
  6.5 0.7 fusion
  7.3 1.2 copy.8
  8.5 0.8 multiply_convert_fusion
  9.3 1.3 mul.43
  10.5 2.3 %mul.44 = bf16[2048,128]{0,1:T(8,128)(2,1)S(1)} reshape(bf16[64,32,4,32]{1,0,3,2:T(8,128)(2,1)S(1)} %mul.43) | data formatting | bytes 1048576 | tf_op jit(solution)/shard_map/mul | solution.py:20
  12.8 0.1 mul.45
  12.9 2.8 %collective-permute-start = (bf16[2048,128]{0,1:T(8,128)(2,1)S(1)}, bf16[2048,128]{0,1:T(8,128)(2,1)}, u32[]{:S(2)}, u32[]{:S(2)}) collective-permute-start(bf16[2048,128]{0,1:T(8,128)(2,1)S(1)} %mul.45), channel_id=1, source_target_pairs={{64,0},{128,64},{192,128},{0,192},{65,1},{129,65},{193,129},{1,193... | collective-permute-start | bytes 1572872 | tf_op jit(solution)/shard_map/ppermute | solution.py:12
  15.8 0.7 convert_element_type.24
  16.5 0.6 mul.46
  17.1 2.3 %mul.47 = bf16[128,2048]{1,0:T(8,128)(2,1)S(1)} reshape(bf16[4,32,64,32]{3,2,1,0:T(8,128)(2,1)S(1)} %mul.46) | data formatting | bytes 1048576 | tf_op jit(solution)/shard_map/mul | solution.py:28
  19.3 1.2 mul.48
  20.5 0.8 collective-permute-start.2
  21.3 5.6 %collective-permute-done = bf16[2048,128]{0,1:T(8,128)(2,1)} collective-permute-done((bf16[2048,128]{0,1:T(8,128)(2,1)S(1)}, bf16[2048,128]{0,1:T(8,128)(2,1)}, u32[]{:S(2)}, u32[]{:S(2)}) %collective-permute-start) | collective-permute-done | bytes 524320 | tf_op jit(solution)/shard_map/ppermute | solution.py:12
  27.0 1.1 broadcast_select_fusion.2
  28.1 2.9 %collective-permute-start.1 = (bf16[2048,128]{0,1:T(8,128)(2,1)S(1)}, bf16[2048,128]{0,1:T(8,128)(2,1)S(1)}, u32[]{:S(2)}, u32[]{:S(2)}) collective-permute-start(bf16[2048,128]{0,1:T(8,128)(2,1)S(1)} %broadcast_select_fusion.2), channel_id=1, source_target_pairs={{128,0},{192,64},{0,128},{64,192},{129,1},{193,65},{1,129},{65,193... | collective-permute-start | bytes 1572872 | tf_op jit(solution)/shard_map/ppermute | solution.py:12
  31.0 4.2 %collective-permute-done.2 = bf16[128,2048]{1,0:T(8,128)(2,1)S(1)} collective-permute-done((bf16[128,2048]{1,0:T(8,128)(2,1)S(1)}, bf16[128,2048]{1,0:T(8,128)(2,1)S(1)}, u32[]{:S(2)}, u32[]{:S(2)}) %collective-permute-start.2) | collective-permute-done | bytes 524320 | tf_op jit(solution)/shard_map/ppermute | solution.py:12
  35.2 0.1 broadcast_select_fusion
  35.2 0.1 collective-permute-start.3
  35.4 7.1 %collective-permute-done.1 = bf16[2048,128]{0,1:T(8,128)(2,1)S(1)} collective-permute-done((bf16[2048,128]{0,1:T(8,128)(2,1)S(1)}, bf16[2048,128]{0,1:T(8,128)(2,1)S(1)}, u32[]{:S(2)}, u32[]{:S(2)}) %collective-permute-start.1) | collective-permute-done | bytes 524320 | tf_op jit(solution)/shard_map/ppermute | solution.py:12
  42.4 0.1 broadcast_select_fusion.3
  42.5 4.2 %collective-permute-start.4 = (bf16[2048,128]{0,1:T(8,128)(2,1)S(1)}, bf16[2048,128]{0,1:T(8,128)(2,1)S(1)}, u32[]{:S(2)}, u32[]{:S(2)}) collective-permute-start(bf16[2048,128]{0,1:T(8,128)(2,1)S(1)} %broadcast_select_fusion.3), channel_id=1, source_target_pairs={{64,0},{128,64},{192,128},{0,192},{65,1},{129,65},{193,129},{1,193... | collective-permute-start | bytes 1572872 | tf_op jit(solution)/shard_map/ppermute | solution.py:12
  46.7 3.1 %collective-permute-done.3 = bf16[128,2048]{1,0:T(8,128)(2,1)S(1)} collective-permute-done((bf16[128,2048]{1,0:T(8,128)(2,1)S(1)}, bf16[128,2048]{1,0:T(8,128)(2,1)S(1)}, u32[]{:S(2)}, u32[]{:S(2)}) %collective-permute-start.3) | collective-permute-done | bytes 524320 | tf_op jit(solution)/shard_map/ppermute | solution.py:12
  49.8 0.1 broadcast_select_fusion.1
  49.9 0.1 collective-permute-start.5
  50.0 2.4 %fusion.1 = f32[2048,2048]{1,0:T(8,128)S(1)} fusion(bf16[2048,128]{0,1:T(8,128)(2,1)S(1)} %broadcast_select_fusion.3, bf16[128,2048]{1,0:T(8,128)(2,1)S(1)} %broadcast_select_fusion.1), kind=kOutput, calls=%fused_computation.8 | convolution fusion | flops 1073741824 | bytes 17825792 | tf_op jit(solution)/shard_map/dot_general | solution.py:48
  52.3 3.5 %collective-permute-done.4 = bf16[2048,128]{0,1:T(8,128)(2,1)S(1)} collective-permute-done((bf16[2048,128]{0,1:T(8,128)(2,1)S(1)}, bf16[2048,128]{0,1:T(8,128)(2,1)S(1)}, u32[]{:S(2)}, u32[]{:S(2)}) %collective-permute-start.4) | collective-permute-done | bytes 524320 | tf_op jit(solution)/shard_map/ppermute | solution.py:12
  55.8 3.7 %collective-permute-start.6 = (bf16[2048,128]{0,1:T(8,128)(2,1)S(1)}, bf16[2048,128]{0,1:T(8,128)(2,1)S(1)}, u32[]{:S(2)}, u32[]{:S(2)}) collective-permute-start(bf16[2048,128]{0,1:T(8,128)(2,1)S(1)} %collective-permute-done.4), channel_id=1, source_target_pairs={{64,0},{128,64},{192,128},{0,192},{65,1},{129,65},{193,129},{1,193... | collective-permute-start | bytes 1572872 | tf_op jit(solution)/shard_map/ppermute | solution.py:12
  59.5 2.7 %collective-permute-done.5 = bf16[128,2048]{1,0:T(8,128)(2,1)S(1)} collective-permute-done((bf16[128,2048]{1,0:T(8,128)(2,1)S(1)}, bf16[128,2048]{1,0:T(8,128)(2,1)S(1)}, u32[]{:S(2)}, u32[]{:S(2)}) %collective-permute-start.5) | collective-permute-done | bytes 524320 | tf_op jit(solution)/shard_map/ppermute | solution.py:12
  62.2 0.0 collective-permute-start.7
  62.2 8.1 %fusion.2 = f32[2048,2048]{1,0:T(8,128)} fusion(bf16[2048,128]{0,1:T(8,128)(2,1)S(1)} %collective-permute-done.4, bf16[128,2048]{1,0:T(8,128)(2,1)S(1)} %collective-permute-done.5), kind=kOutput, calls=%fused_computation.9 | convolution fusion | flops 1073741824 | bytes 17825792 | tf_op jit(solution)/shard_map/dot_general | solution.py:48
  70.3 0.0 collective-permute-done.6
  70.3 1.0 collective-permute-start.8
  71.3 2.9 %collective-permute-done.7 = bf16[128,2048]{1,0:T(8,128)(2,1)S(1)} collective-permute-done((bf16[128,2048]{1,0:T(8,128)(2,1)S(1)}, bf16[128,2048]{1,0:T(8,128)(2,1)S(1)}, u32[]{:S(2)}, u32[]{:S(2)}) %collective-permute-start.7) | collective-permute-done | bytes 524320 | tf_op jit(solution)/shard_map/ppermute | solution.py:12
  74.3 0.0 collective-permute-start.9
  74.3 8.1 %fusion.3 = f32[2048,2048]{1,0:T(8,128)} fusion(bf16[2048,128]{0,1:T(8,128)(2,1)S(1)} %collective-permute-done.6, bf16[128,2048]{1,0:T(8,128)(2,1)S(1)} %collective-permute-done.7), kind=kOutput, calls=%fused_computation.10 | convolution fusion | flops 1073741824 | bytes 17825792 | tf_op jit(solution)/shard_map/dot_general | solution.py:48
  82.4 0.0 collective-permute-done.8
  82.4 2.4 %collective-permute-done.9 = bf16[128,2048]{1,0:T(8,128)(2,1)S(1)} collective-permute-done((bf16[128,2048]{1,0:T(8,128)(2,1)S(1)}, bf16[128,2048]{1,0:T(8,128)(2,1)S(1)}, u32[]{:S(2)}, u32[]{:S(2)}) %collective-permute-start.9) | collective-permute-done | bytes 524320 | tf_op jit(solution)/shard_map/ppermute | solution.py:12
  84.8 15.3 %add_convert_fusion = bf16[2048,2048]{1,0:T(8,128)(2,1)} fusion(f32[2048,2048]{1,0:T(8,128)} %fusion.3, f32[2048,2048]{1,0:T(8,128)S(1)} %fusion.1, f32[2048,2048]{1,0:T(8,128)} %fusion.2, bf16[2048,128]{0,1:T(8,128)(2,1)S(1)} %collective-permute-done.8, bf16[128,2048]{1,0:T(8,128)(2,1)S(1)} %collective-permute-done.9), kind=kOutput, calls=%fused_computation | convolution fusion | flops 1090519040 | bytes 59768832 | tf_op jit(solution)/shard_map/dot_general | solution.py:48
  100.1 12.3 %copy.9 = bf16[2048,2048]{0,1:T(8,128)(2,1)} copy(bf16[2048,2048]{1,0:T(8,128)(2,1)} %add_convert_fusion) | data formatting | bytes 16777216
  112.4 0.0 reduce-scatter.4.cloned.1.call-update
  112.4 71.0 %reduce-scatter.4.cloned.1.call-done = bf16[128,2048]{1,0:T(8,128)(2,1)} async-done(((bf16[2048,2048]{1,0:T(8,128)(2,1)}), bf16[128,2048]{1,0:T(8,128)(2,1)}) %reduce-scatter.4.cloned.1.call-update) | async-done | bytes 524304
  183.4 2.0 %copy.10 = bf16[2048,128]{1,0:T(8,128)(2,1)} copy(bf16[2048,128]{0,1:T(8,128)(2,1)} %bitcast.17) | data formatting | bytes 1048576
Async XLA Ops:
  6.5 176.8 %reduce-scatter.4.cloned.1.call-start = ((), (), s32[]{:S(2)}) async-start(), calls=%async_computation.1 | async-start | bytes 8912896
  12.9 14.0 %collective-permute-start = (bf16[2048,128]{0,1:T(8,128)(2,1)S(1)}, bf16[2048,128]{0,1:T(8,128)(2,1)}, u32[]{:S(2)}, u32[]{:S(2)}) collective-permute-start(bf16[2048,128]{0,1:T(8,128)(2,1)S(1)} %mul.45), channel_id=1, source_target_pairs={{64,0},{128,64},{192,128},{0,192},{65,1},{129,65},{193,129},{1,193... | collective-permute-start | bytes 1572872 | tf_op jit(solution)/shard_map/ppermute | solution.py:12
  20.5 14.7 %collective-permute-start.2 = (bf16[128,2048]{1,0:T(8,128)(2,1)S(1)}, bf16[128,2048]{1,0:T(8,128)(2,1)S(1)}, u32[]{:S(2)}, u32[]{:S(2)}) collective-permute-start(bf16[128,2048]{1,0:T(8,128)(2,1)S(1)} %mul.48), channel_id=1, source_target_pairs={{16,0},{32,16},{48,32},{0,48},{17,1},{33,17},{49,33},{1,49},{18,2}... | collective-permute-start | bytes 1572872 | tf_op jit(solution)/shard_map/ppermute | solution.py:12
  28.1 14.4 %collective-permute-start.1 = (bf16[2048,128]{0,1:T(8,128)(2,1)S(1)}, bf16[2048,128]{0,1:T(8,128)(2,1)S(1)}, u32[]{:S(2)}, u32[]{:S(2)}) collective-permute-start(bf16[2048,128]{0,1:T(8,128)(2,1)S(1)} %broadcast_select_fusion.2), channel_id=1, source_target_pairs={{128,0},{192,64},{0,128},{64,192},{129,1},{193,65},{1,129},{65,193... | collective-permute-start | bytes 1572872 | tf_op jit(solution)/shard_map/ppermute | solution.py:12
  35.2 14.6 %collective-permute-start.3 = (bf16[128,2048]{1,0:T(8,128)(2,1)S(1)}, bf16[128,2048]{1,0:T(8,128)(2,1)S(1)}, u32[]{:S(2)}, u32[]{:S(2)}) collective-permute-start(bf16[128,2048]{1,0:T(8,128)(2,1)S(1)} %broadcast_select_fusion), channel_id=1, source_target_pairs={{32,0},{48,16},{0,32},{16,48},{33,1},{49,17},{1,33},{17,49},{34,2}... | collective-permute-start | bytes 1572872 | tf_op jit(solution)/shard_map/ppermute | solution.py:12
  42.5 13.3 %collective-permute-start.4 = (bf16[2048,128]{0,1:T(8,128)(2,1)S(1)}, bf16[2048,128]{0,1:T(8,128)(2,1)S(1)}, u32[]{:S(2)}, u32[]{:S(2)}) collective-permute-start(bf16[2048,128]{0,1:T(8,128)(2,1)S(1)} %broadcast_select_fusion.3), channel_id=1, source_target_pairs={{64,0},{128,64},{192,128},{0,192},{65,1},{129,65},{193,129},{1,193... | collective-permute-start | bytes 1572872 | tf_op jit(solution)/shard_map/ppermute | solution.py:12
  49.9 12.3 %collective-permute-start.5 = (bf16[128,2048]{1,0:T(8,128)(2,1)S(1)}, bf16[128,2048]{1,0:T(8,128)(2,1)S(1)}, u32[]{:S(2)}, u32[]{:S(2)}) collective-permute-start(bf16[128,2048]{1,0:T(8,128)(2,1)S(1)} %broadcast_select_fusion.1), channel_id=1, source_target_pairs={{16,0},{32,16},{48,32},{0,48},{17,1},{33,17},{49,33},{1,49},{18,2}... | collective-permute-start | bytes 1572872 | tf_op jit(solution)/shard_map/ppermute | solution.py:12
  55.8 14.5 %collective-permute-start.6 = (bf16[2048,128]{0,1:T(8,128)(2,1)S(1)}, bf16[2048,128]{0,1:T(8,128)(2,1)S(1)}, u32[]{:S(2)}, u32[]{:S(2)}) collective-permute-start(bf16[2048,128]{0,1:T(8,128)(2,1)S(1)} %collective-permute-done.4), channel_id=1, source_target_pairs={{64,0},{128,64},{192,128},{0,192},{65,1},{129,65},{193,129},{1,193... | collective-permute-start | bytes 1572872 | tf_op jit(solution)/shard_map/ppermute | solution.py:12
  62.2 12.1 %collective-permute-start.7 = (bf16[128,2048]{1,0:T(8,128)(2,1)S(1)}, bf16[128,2048]{1,0:T(8,128)(2,1)S(1)}, u32[]{:S(2)}, u32[]{:S(2)}) collective-permute-start(bf16[128,2048]{1,0:T(8,128)(2,1)S(1)} %collective-permute-done.5), channel_id=1, source_target_pairs={{16,0},{32,16},{48,32},{0,48},{17,1},{33,17},{49,33},{1,49},{18,2}... | collective-permute-start | bytes 1572872 | tf_op jit(solution)/shard_map/ppermute | solution.py:12
  70.3 12.1 %collective-permute-start.8 = (bf16[2048,128]{0,1:T(8,128)(2,1)S(1)}, bf16[2048,128]{0,1:T(8,128)(2,1)S(1)}, u32[]{:S(2)}, u32[]{:S(2)}) collective-permute-start(bf16[2048,128]{0,1:T(8,128)(2,1)S(1)} %collective-permute-done.6), channel_id=1, source_target_pairs={{64,0},{128,64},{192,128},{0,192},{65,1},{129,65},{193,129},{1,193... | collective-permute-start | bytes 1572872 | tf_op jit(solution)/shard_map/ppermute | solution.py:12
  74.3 10.5 %collective-permute-start.9 = (bf16[128,2048]{1,0:T(8,128)(2,1)S(1)}, bf16[128,2048]{1,0:T(8,128)(2,1)S(1)}, u32[]{:S(2)}, u32[]{:S(2)}) collective-permute-start(bf16[128,2048]{1,0:T(8,128)(2,1)S(1)} %collective-permute-done.7), channel_id=1, source_target_pairs={{16,0},{32,16},{48,32},{0,48},{17,1},{33,17},{49,33},{1,49},{18,2}... | collective-permute-start | bytes 1572872 | tf_op jit(solution)/shard_map/ppermute | solution.py:12
Sparse Core Ops, SparseCore 0:
  112.5 70.8 reduce-scatter.3
where the time goes:
time: 193 us; the launch traced here: 192 us
  waiting for transfers between devices  103 us (53%)
  matrix products  33.9 us (18%)
  local copies, waits for them, and re-layouts  21.9 us (11%)
  starting transfers between devices  15.7 us (8%)
  between operations  13.5 us (7%)
  other arithmetic  4.73 us (2%)
    unnamed x2, waiting for transfers between devices  71 us
    dot_general x4, matrix products, on_device(): jnp.dot(live_tile, dens_tile, preferred_element_type=jnp.float32)  33.9 us
    ppermute x10, waiting for transfers between devices, shifted(): return lax.ppermute(block, axis, route)  31.6 us
    ppermute x10, starting transfers between devices, shifted(): return lax.ppermute(block, axis, route)  15.7 us
    unnamed x3, local copies, waits for them, and re-layouts  15.6 us
  transfers between devices with their start and end apart: 11, of which 9 were waited for; matrix products, arithmetic and copies ran while one was open for 13% of the time, Pallas kernels for 0%

commit v1 on v0

v1 whole, which is shorter than its diff:
```python
import functools

import jax
import jax.numpy as jnp
from jax import lax
from jax.experimental import pallas as pl
from jax.experimental.pallas import tpu as pltpu
from jax.sharding import PartitionSpec as P

BS = 32
CHUNKS = 2
EARLY = (4, 3, 5)
LATE = (2, 6, 1, 7, 0)
VMEM_BYTES = 32 * 1024 * 1024

vmem = functools.partial(pl.BlockSpec, memory_space=pltpu.VMEM)
smem = functools.partial(pl.BlockSpec, memory_space=pltpu.SMEM)


def call(kernel, outs, operands, in_specs, scratch=(), flops=0):
    moved = sum(a.size * a.dtype.itemsize for a in operands)
    moved += sum(o.size * o.dtype.itemsize for o in outs)
    return pl.pallas_call(
        kernel,
        out_shape=outs,
        in_specs=in_specs,
        out_specs=[vmem()] * len(outs),
        scratch_shapes=list(scratch),
        compiler_params=pltpu.CompilerParams(vmem_limit_bytes=VMEM_BYTES),
        cost_estimate=pl.CostEstimate(flops=flops, bytes_accessed=moved, transcendentals=0),
    )(*operands)


def mask_three(three_center, three_mask, nu_sizes):
    rows, cols = three_center.shape
    part = rows // CHUNKS
    tiles = part // BS

    def kernel(sizes_ref, mask_ref, three_ref, *outs):
        lane = lax.broadcasted_iota(jnp.int32, (rows // BS, cols), 1)
        size = jnp.zeros_like(lane)
        keep = jnp.zeros_like(lane)
        for j in range(cols // BS):
            here = lane // BS == j
            size = jnp.where(here, sizes_ref[j], size)
            keep = jnp.where(here, mask_ref[:, j : j + 1], keep)
        keep = jnp.where(lane % BS < size, keep, 0).astype(jnp.float32)
        for h in range(CHUNKS):
            for t in range(tiles):
                g = h * tiles + t
                wide = jnp.broadcast_to(keep[g : g + 1, :], (BS, cols)).astype(jnp.bfloat16)
                outs[h][t * BS : (t + 1) * BS, :] = three_ref[g * BS : (g + 1) * BS, :] * wide

    return call(
        kernel,
        [jax.ShapeDtypeStruct((part, cols), jnp.bfloat16)] * CHUNKS,
        (nu_sizes, three_mask, three_center),
        [smem(), vmem(), vmem()],
    )


def mask_density(place, density, density_mask):
    rows, cols = density.shape
    row_tiles, col_tiles = density_mask.shape
    share = 128
    count = cols // (2 * share)

    def kernel(place_ref, mask_ref, dens_ref, own_ref, other_ref, held):
        z, c = place_ref[0], place_ref[1]
        spread = (
            lax.broadcasted_iota(jnp.int32, (col_tiles, cols), 1) // BS
            == lax.broadcasted_iota(jnp.int32, (col_tiles, cols), 0)
        ).astype(jnp.bfloat16)
        keep = jnp.dot(
            mask_ref[...].astype(jnp.float32).astype(jnp.bfloat16), spread, preferred_element_type=jnp.float32
        )
        for i in range(row_tiles):
            wide = jnp.broadcast_to(keep[i : i + 1, :], (BS, cols)).astype(jnp.bfloat16)
            held[i * BS : (i + 1) * BS, :] = dens_ref[i * BS : (i + 1) * BS, :] * wide
        for j in range(count):
            first = lax.rem(z + j, count) * 2
            own = pl.multiple_of((first + c) * share, share)
            other = pl.multiple_of((first + 1 - c) * share, share)
            own_ref[j] = held[:, pl.ds(own, share)]
            other_ref[j] = held[:, pl.ds(other, share)]

    return call(
        kernel,
        [jax.ShapeDtypeStruct((count, rows, share), jnp.bfloat16)] * 2,
        (place, density_mask, density),
        [smem(), vmem(), vmem()],
        [pltpu.VMEM((rows, cols), jnp.bfloat16)],
        flops=2 * row_tiles * col_tiles * cols,
    )


def dots(place, three, dens, groups, kinds):
    part, deep = three[0].shape
    pieces = len(dens)
    k_piece = dens[0].shape[1]
    share = dens[0].shape[2]
    tile = 256

    def kernel(place_ref, *refs):
        a_refs, b_refs = refs[: len(three)], refs[len(three) : len(three) + pieces]
        outs = refs[len(three) + pieces : -1]
        held = refs[-1]
        turn = place_ref[2]
        for s in range(pieces):
            at = pl.multiple_of(lax.rem(s + turn, pieces) * k_piece, k_piece)
            first = 0
            for group in groups:
                for n, j in enumerate(group):
                    held[pl.ds(at, k_piece), (first + n) * share : (first + n + 1) * share] = b_refs[s][j]
                first += len(group)
        first = 0
        for group, out in zip(groups, outs):
            width = len(group) * share
            right = held[:, first * share : first * share + width]
            for m in range(0, part, tile):
                left = jnp.concatenate([a[m : m + tile, :] for a in a_refs], axis=1)
                out[m : m + tile, :] = jnp.dot(left, right, preferred_element_type=jnp.float32).astype(out.dtype)
            first += len(group)

    total = sum(len(g) for g in groups)
    return call(
        kernel,
        [jax.ShapeDtypeStruct((part, len(g) * share), kind) for g, kind in zip(groups, kinds)],
        (place, *three, *dens),
        [smem()] + [vmem()] * (len(three) + pieces),
        [pltpu.VMEM((pieces * k_piece, total * share), jnp.bfloat16)],
        flops=2 * part * deep * len(three) * total * share,
    )


def shifted(block, axis, distance):
    count = lax.axis_size(axis)
    return lax.ppermute(block, axis, [((i + distance) % count, i) for i in range(count)])


def along_z(block, distance):
    count = lax.axis_size("depth") // 2
    route = [(z * 2 + c, (z + distance) % count * 2 + c) for z in range(count) for c in range(2)]
    return lax.ppermute(block, "depth", route)


def other_core(block):
    return lax.ppermute(block, "depth", [(i, i ^ 1) for i in range(lax.axis_size("depth"))])


def gathered(block, axis):
    up, down, far = shifted(block, axis, 1), shifted(block, axis, 3), shifted(block, axis, 2)
    return [block, up, far, down]


def on_device(three_center, three_mask, density, density_mask, nu_sizes):
    row, col, depth = lax.axis_index("row"), lax.axis_index("col"), lax.axis_index("depth")
    place = jnp.stack([depth // 2, depth % 2, (col - row) % 4]).astype(jnp.int32)

    chunks = mask_three(three_center, three_mask, nu_sizes)
    own, other = mask_density(place, density, density_mask)
    arrived = other_core(other)
    both = jnp.concatenate([own, arrived], axis=1)
    early = gathered(jnp.stack([both[j] for j in EARLY]), "col")
    late = gathered(jnp.stack([both[j] for j in LATE]), "col")

    outs = []
    for chunk in chunks:
        blocks = gathered(chunk, "row")
        three = []
        for block in blocks:
            three += [block, other_core(block)]
        half = chunk.shape[0] // 2
        far, near3 = dots(place, three, early, ((0,), (1, 2)), (jnp.bfloat16, jnp.float32))
        to_right, to_left = along_z(far[:half], 1), along_z(far[half:], -1)
        near2, near1, near0 = dots(place, three, late, ((0, 1), (2, 3), (4,)), (jnp.float32,) * 3)
        share = far.shape[1]
        none = jnp.zeros((half, share), jnp.float32)
        to_right = jnp.concatenate([to_right.astype(jnp.float32), none])
        to_left = jnp.concatenate([none, to_left.astype(jnp.float32)])
        for near in (near3, near2, near1):
            to_right = along_z((near[:, :share] + to_right).astype(jnp.bfloat16), 1).astype(jnp.float32)
            to_left = along_z((near[:, share:] + to_left).astype(jnp.bfloat16), -1).astype(jnp.float32)
        outs.append((near0 + to_right + to_left).astype(jnp.bfloat16))
    return jnp.concatenate(outs)


def solution(mesh):
    in_specs = (
        P("col", ("row", "depth")),
        P("col", ("row", "depth")),
        P(("col", "depth"), "row"),
        P(("col", "depth"), "row"),
        P(("row", "depth")),
    )
    out_specs = P("col", ("row", "depth"))
    return jax.shard_map(
        on_device, mesh=mesh, in_specs=in_specs, out_specs=out_specs, check_vma=False
    )
```

time: 193 us -> 107 us (0.55)
  the two profiles are of different devices: /device:TPU:24 before, /device:TPU:6 now
where the time goes in v1:
time: 107 us
  starting transfers between devices  58.5 us (55%)
  waiting for transfers between devices  33.3 us (31%)
  Pallas kernels  10.4 us (10%)
  local copies, waits for them, and re-layouts  2.48 us (2%)
  other arithmetic  1.71 us (2%)
    ppermute x16, starting transfers between devices, along_z(): return lax.ppermute(block, 'depth', route)  35.3 us
    ppermute x12, starting transfers between devices, shifted(): lax.ppermute(block, axis, [((i + distance) % count, i) for i in range(cou...  21.4 us
    ppermute x12, waiting for transfers between devices, shifted(): lax.ppermute(block, axis, [((i + distance) % count, i) for i in range(cou...  18.2 us
    ppermute x16, waiting for transfers between devices, along_z(): return lax.ppermute(block, 'depth', route)  15.1 us
    pallas_call x6, Pallas kernels, call(): pl.pallas_call(kernel, out_shape=outs, in_specs=in_specs, out_specs=[vmem...  10.4 us
    unnamed x16, local copies, waits for them, and re-layouts  2.38 us
  transfers between devices with their start and end apart: 37, of which 15 were waited for; matrix products, arithmetic and copies ran while one was open for 1% of the time, Pallas kernels for 9%

profile of v1, /device:TPU:6, one launch (start us, length us, event | category | flops | bytes accessed | tf_op | source)
XLA Modules:
  0.0 106.6 jit_solution(2837917991220919941)
XLA Ops:
  0.1 1.1 %copy-done.1 = bf16[128,2048]{1,0:T(8,128)(2,1)S(1)} copy-done((bf16[128,2048]{1,0:T(8,128)(2,1)S(1)}, bf16[128,2048]{1,0:T(8,128)(2,1)}, u32[]{:S(2)}) %copy-start.1) | copy-done | bytes 524312
  1.2 0.7 copy-done.2
  1.9 0.9 shard_map.56
  2.9 0.4 copy-done.3
  3.4 0.7 shard_map.55
  4.2 0.9 collective-permute-start.23
  5.1 2.8 %collective-permute-start.25 = (bf16[1024,128]{1,0:T(8,128)(2,1)S(1)}, bf16[1024,128]{1,0:T(8,128)(2,1)S(1)}, u32[]{:S(2)}, u32[]{:S(2)}) collective-permute-start(bf16[1024,128]{1,0:T(8,128)(2,1)S(1)} %get-tuple-element.27.refs_0_), channel_id=1, source_target_pairs={{128,0},{192,64},{0,128},{64,192},{129,1},{193,65},{1,129},{65,193... | collective-permute-start | bytes 786440 | tf_op jit(solution)/shard_map/ppermute | solution.py:138
  8.3 1.7 %collective-permute-start.1 = (bf16[1024,128]{1,0:T(8,128)(2,1)S(1)}, bf16[1024,128]{1,0:T(8,128)(2,1)S(1)}, u32[]{:S(2)}, u32[]{:S(2)}) collective-permute-start(bf16[1024,128]{1,0:T(8,128)(2,1)S(1)} %get-tuple-element.19.refs_0_), channel_id=1, source_target_pairs={{64,0},{128,64},{192,128},{0,192},{65,1},{129,65},{193,129},{1,193... | collective-permute-start | bytes 786440 | tf_op jit(solution)/shard_map/ppermute | solution.py:138
  10.2 0.8 collective-permute-start.3
  11.0 4.1 %collective-permute-done.23.refs_2_ = bf16[1024,128]{1,0:T(8,128)(2,1)S(1)} collective-permute-done((bf16[1024,128]{1,0:T(8,128)(2,1)S(1)}, bf16[1024,128]{1,0:T(8,128)(2,1)S(1)}, u32[]{:S(2)}, u32[]{:S(2)}) %collective-permute-start.23) | collective-permute-done | bytes 262176 | tf_op jit(solution)/shard_map/ppermute | solution.py:138
  15.1 0.5 collective-permute-start.5
  15.6 5.1 %collective-permute-done.25.refs_4_ = bf16[1024,128]{1,0:T(8,128)(2,1)S(1)} collective-permute-done((bf16[1024,128]{1,0:T(8,128)(2,1)S(1)}, bf16[1024,128]{1,0:T(8,128)(2,1)S(1)}, u32[]{:S(2)}, u32[]{:S(2)}) %collective-permute-start.25) | collective-permute-done | bytes 262176 | tf_op jit(solution)/shard_map/ppermute | solution.py:138
  20.7 2.6 %collective-permute-start.11 = (bf16[3,256,128]{2,1,0:T(8,128)(2,1)S(1)}, bf16[3,256,128]{2,1,0:T(8,128)(2,1)S(1)}, u32[]{:S(2)}, u32[]{:S(2)}) collective-permute-start(bf16[3,256,128]{2,1,0:T(8,128)(2,1)S(1)} %pad_maximum_fusion.1.refs_8_), channel_id=1, source_target_pairs={{16,0},{32,16},{48,32},{0,48},{17,1},{33,17},{49,33},{1,49},{18,2}... | collective-permute-start | bytes 589832 | tf_op jit(solution)/shard_map/ppermute | solution.py:138
  23.3 1.0 collective-permute-start.12
  24.3 1.0 collective-permute-done.1.refs_2_
  25.4 7.2 %collective-permute-start.13 = (bf16[3,256,128]{2,1,0:T(8,128)(2,1)S(1)}, bf16[3,256,128]{2,1,0:T(8,128)(2,1)S(1)}, u32[]{:S(2)}, u32[]{:S(2)}) collective-permute-start(bf16[3,256,128]{2,1,0:T(8,128)(2,1)S(1)} %pad_maximum_fusion.1.refs_8_), channel_id=1, source_target_pairs={{48,0},{0,16},{16,32},{32,48},{49,1},{1,17},{17,33},{33,49},{50,2}... | collective-permute-start | bytes 589832 | tf_op jit(solution)/shard_map/ppermute | solution.py:138
  32.6 0.5 collective-permute-start.26
  33.2 0.4 collective-permute-start
  33.6 5.1 %collective-permute-done.13.refs_11_ = bf16[3,256,128]{2,1,0:T(8,128)(2,1)S(1)} collective-permute-done((bf16[3,256,128]{2,1,0:T(8,128)(2,1)S(1)}, bf16[3,256,128]{2,1,0:T(8,128)(2,1)S(1)}, u32[]{:S(2)}, u32[]{:S(2)}) %collective-permute-start.13) | collective-permute-done | bytes 196640 | tf_op jit(solution)/shard_map/ppermute | solution.py:138
  38.7 1.7 %collective-permute-start.8 = (bf16[5,256,128]{2,1,0:T(8,128)(2,1)S(1)}, bf16[5,256,128]{2,1,0:T(8,128)(2,1)S(1)}, u32[]{:S(2)}, u32[]{:S(2)}) collective-permute-start(bf16[5,256,128]{2,1,0:T(8,128)(2,1)S(1)} %get-tuple-element.45.refs_8_), channel_id=1, source_target_pairs={{16,0},{32,16},{48,32},{0,48},{17,1},{33,17},{49,33},{1,49},{18,2}... | collective-permute-start | bytes 983048 | tf_op jit(solution)/shard_map/ppermute | solution.py:138
  41.0 1.9 %shard_map.60 = (bf16[1024,128]{1,0:T(8,128)(2,1)S(1)}, f32[1024,256]{1,0:T(8,128)S(1)}) custom-call(s32[3]{0:T(128)S(1)} %pad_add_fusion.place_ref, bf16[1024,128]{1,0:T(8,128)(2,1)S(1)} %get-tuple-element.27.refs_0_, bf16[1024,128]{1,0:T(8,128)(2,1)S(1)} %collective-permute-done.22.refs_1_, bf16[1024,128]{1,0:T(8,128)(2,1)S(1)} %collective-permute-done.23.refs_2_, ...), custom_call_target="tpu_custom_call" | custom-call | flops 805306368 | bytes 4194316 | tf_op jit(solution)/shard_map/pallas_call | solution.py:23
  42.9 0.7 collective-permute-start.9
  43.6 1.0 collective-permute-start.10
  44.6 2.0 %collective-permute-start.29 = (bf16[512,128]{1,0:T(8,128)(2,1)S(1)}, bf16[512,128]{1,0:T(8,128)(2,1)S(1)}, u32[]{:S(2)}, u32[]{:S(2)}) collective-permute-start(bf16[512,128]{1,0:T(8,128)(2,1)S(1)} %get-tuple-element.51), channel_id=1, source_target_pairs={{0,2},{1,3},{2,4},{3,5},{4,6},{5,7},{6,8},{7,9},{8,10},{9,11},{10,... | collective-permute-start | bytes 393224 | tf_op jit(solution)/shard_map/ppermute | solution.py:144
  46.6 4.0 %collective-permute-start.33 = (bf16[512,128]{1,0:T(8,128)(2,1)S(1)}, bf16[512,128]{1,0:T(8,128)(2,1)S(1)}, u32[]{:S(2)}, u32[]{:S(2)}) collective-permute-start(bf16[512,128]{1,0:T(8,128)(2,1)S(1)} %get-tuple-element.52), channel_id=1, source_target_pairs={{0,14},{1,15},{2,0},{3,1},{4,2},{5,3},{6,4},{7,5},{8,6},{9,7},{10,... | collective-permute-start | bytes 393224 | tf_op jit(solution)/shard_map/ppermute | solution.py:144
  50.7 1.9 %shard_map.58 = (bf16[1024,128]{1,0:T(8,128)(2,1)S(1)}, f32[1024,256]{1,0:T(8,128)S(1)}) custom-call(s32[3]{0:T(128)S(1)} %pad_add_fusion.place_ref, bf16[1024,128]{1,0:T(8,128)(2,1)S(1)} %get-tuple-element.19.refs_0_, bf16[1024,128]{1,0:T(8,128)(2,1)S(1)} %collective-permute-done.refs_1_, bf16[1024,128]{1,0:T(8,128)(2,1)S(1)} %collective-permute-done.1.refs_2_, ...), custom_call_target="tpu_custom_call" | custom-call | flops 805306368 | bytes 4194316 | tf_op jit(solution)/shard_map/pallas_call | solution.py:23
  52.6 2.5 %collective-permute-done.8.refs_9_ = bf16[5,256,128]{2,1,0:T(8,128)(2,1)S(1)} collective-permute-done((bf16[5,256,128]{2,1,0:T(8,128)(2,1)S(1)}, bf16[5,256,128]{2,1,0:T(8,128)(2,1)S(1)}, u32[]{:S(2)}, u32[]{:S(2)}) %collective-permute-start.8) | collective-permute-done | bytes 327712 | tf_op jit(solution)/shard_map/ppermute | solution.py:138
  55.1 1.9 %collective-permute-start.14 = (bf16[512,128]{1,0:T(8,128)(2,1)S(1)}, bf16[512,128]{1,0:T(8,128)(2,1)S(1)}, u32[]{:S(2)}, u32[]{:S(2)}) collective-permute-start(bf16[512,128]{1,0:T(8,128)(2,1)S(1)} %get-tuple-element.49), channel_id=1, source_target_pairs={{0,2},{1,3},{2,4},{3,5},{4,6},{5,7},{6,8},{7,9},{8,10},{9,11},{10,... | collective-permute-start | bytes 393224 | tf_op jit(solution)/shard_map/ppermute | solution.py:144
  57.1 3.9 %collective-permute-start.18 = (bf16[512,128]{1,0:T(8,128)(2,1)S(1)}, bf16[512,128]{1,0:T(8,128)(2,1)S(1)}, u32[]{:S(2)}, u32[]{:S(2)}) collective-permute-start(bf16[512,128]{1,0:T(8,128)(2,1)S(1)} %get-tuple-element.50), channel_id=1, source_target_pairs={{0,14},{1,15},{2,0},{3,1},{4,2},{5,3},{6,4},{7,5},{8,6},{9,7},{10,... | collective-permute-start | bytes 393224 | tf_op jit(solution)/shard_map/ppermute | solution.py:144
  61.0 0.4 collective-permute-done.10.refs_11_
  61.4 2.5 %shard_map.59 = (f32[1024,256]{1,0:T(8,128)S(1)}, f32[1024,256]{1,0:T(8,128)S(1)}, f32[1024,128]{1,0:T(8,128)S(1)}) custom-call(s32[3]{0:T(128)S(1)} %pad_add_fusion.place_ref, bf16[1024,128]{1,0:T(8,128)(2,1)S(1)} %get-tuple-element.27.refs_0_, bf16[1024,128]{1,0:T(8,128)(2,1)S(1)} %collective-permute-done.22.refs_1_, ...), custom_call_target="tpu_custom_call" | custom-call | flops 1342177280 | bytes 6029324 | tf_op jit(solution)/shard_map/pallas_call | solution.py:23
  64.0 2.0 %collective-permute-start.30 = (bf16[1024,128]{1,0:T(8,128)(2,1)S(1)}, bf16[1024,128]{1,0:T(8,128)(2,1)S(1)}, u32[]{:S(2)}, u32[]{:S(2)}) collective-permute-start(bf16[1024,128]{1,0:T(8,128)(2,1)S(1)} %get-tuple-element.43), channel_id=1, source_target_pairs={{0,2},{1,3},{2,4},{3,5},{4,6},{5,7},{6,8},{7,9},{8,10},{9,11},{10,... | collective-permute-start | bytes 786440 | tf_op jit(solution)/shard_map/ppermute | solution.py:144
  66.0 4.0 %collective-permute-start.34 = (bf16[1024,128]{1,0:T(8,128)(2,1)S(1)}, bf16[1024,128]{1,0:T(8,128)(2,1)S(1)}, u32[]{:S(2)}, u32[]{:S(2)}) collective-permute-start(bf16[1024,128]{1,0:T(8,128)(2,1)S(1)} %get-tuple-element.44), channel_id=1, source_target_pairs={{0,14},{1,15},{2,0},{3,1},{4,2},{5,3},{6,4},{7,5},{8,6},{9,7},{10,... | collective-permute-start | bytes 786440 | tf_op jit(solution)/shard_map/ppermute | solution.py:144
  70.1 2.5 %shard_map.57 = (f32[1024,256]{1,0:T(8,128)S(1)}, f32[1024,256]{1,0:T(8,128)S(1)}, f32[1024,128]{1,0:T(8,128)S(1)}) custom-call(s32[3]{0:T(128)S(1)} %pad_add_fusion.place_ref, bf16[1024,128]{1,0:T(8,128)(2,1)S(1)} %get-tuple-element.19.refs_0_, bf16[1024,128]{1,0:T(8,128)(2,1)S(1)} %collective-permute-done.refs_1_, ...), custom_call_target="tpu_custom_call" | custom-call | flops 1342177280 | bytes 6029324 | tf_op jit(solution)/shard_map/pallas_call | solution.py:23
  73.0 3.2 %collective-permute-start.19 = (bf16[1024,128]{1,0:T(8,128)(2,1)S(1)}, bf16[1024,128]{1,0:T(8,128)(2,1)S(1)}, u32[]{:S(2)}, u32[]{:S(2)}) collective-permute-start(bf16[1024,128]{1,0:T(8,128)(2,1)S(1)} %get-tuple-element.38), channel_id=1, source_target_pairs={{0,14},{1,15},{2,0},{3,1},{4,2},{5,3},{6,4},{7,5},{8,6},{9,7},{10,... | collective-permute-start | bytes 786440 | tf_op jit(solution)/shard_map/ppermute | solution.py:144
  76.7 3.2 %collective-permute-start.35 = (bf16[1024,128]{1,0:T(8,128)(2,1)S(1)}, bf16[1024,128]{1,0:T(8,128)(2,1)S(1)}, u32[]{:S(2)}, u32[]{:S(2)}) collective-permute-start(bf16[1024,128]{1,0:T(8,128)(2,1)S(1)} %get-tuple-element.42), channel_id=1, source_target_pairs={{0,14},{1,15},{2,0},{3,1},{4,2},{5,3},{6,4},{7,5},{8,6},{9,7},{10,... | collective-permute-start | bytes 786440 | tf_op jit(solution)/shard_map/ppermute | solution.py:144
  79.9 3.5 %collective-permute-done.15 = bf16[1024,128]{1,0:T(8,128)(2,1)S(1)} collective-permute-done((bf16[1024,128]{1,0:T(8,128)(2,1)S(1)}, bf16[1024,128]{1,0:T(8,128)(2,1)S(1)}, u32[]{:S(2)}, u32[]{:S(2)}) %collective-permute-start.15) | collective-permute-done | bytes 262176 | tf_op jit(solution)/shard_map/ppermute | solution.py:144
  83.6 3.3 %collective-permute-start.20 = (bf16[1024,128]{1,0:T(8,128)(2,1)S(1)}, bf16[1024,128]{1,0:T(8,128)(2,1)S(1)}, u32[]{:S(2)}, u32[]{:S(2)}) collective-permute-start(bf16[1024,128]{1,0:T(8,128)(2,1)S(1)} %get-tuple-element.36), channel_id=1, source_target_pairs={{0,14},{1,15},{2,0},{3,1},{4,2},{5,3},{6,4},{7,5},{8,6},{9,7},{10,... | collective-permute-start | bytes 786440 | tf_op jit(solution)/shard_map/ppermute | solution.py:144
  86.9 2.1 %collective-permute-done.31 = bf16[1024,128]{1,0:T(8,128)(2,1)S(1)} collective-permute-done((bf16[1024,128]{1,0:T(8,128)(2,1)S(1)}, bf16[1024,128]{1,0:T(8,128)(2,1)S(1)}, u32[]{:S(2)}, u32[]{:S(2)}) %collective-permute-start.31) | collective-permute-done | bytes 262176 | tf_op jit(solution)/shard_map/ppermute | solution.py:144
  89.1 3.4 %collective-permute-start.36 = (bf16[1024,128]{1,0:T(8,128)(2,1)S(1)}, bf16[1024,128]{1,0:T(8,128)(2,1)S(1)}, u32[]{:S(2)}, u32[]{:S(2)}) collective-permute-start(bf16[1024,128]{1,0:T(8,128)(2,1)S(1)} %get-tuple-element.40), channel_id=1, source_target_pairs={{0,14},{1,15},{2,0},{3,1},{4,2},{5,3},{6,4},{7,5},{8,6},{9,7},{10,... | collective-permute-start | bytes 786440 | tf_op jit(solution)/shard_map/ppermute | solution.py:144
  92.5 1.2 %collective-permute-done.16 = bf16[1024,128]{1,0:T(8,128)(2,1)S(1)} collective-permute-done((bf16[1024,128]{1,0:T(8,128)(2,1)S(1)}, bf16[1024,128]{1,0:T(8,128)(2,1)S(1)}, u32[]{:S(2)}, u32[]{:S(2)}) %collective-permute-start.16) | collective-permute-done | bytes 262176 | tf_op jit(solution)/shard_map/ppermute | solution.py:144
  93.7 0.5 collective-permute-done.20
  94.3 3.8 %collective-permute-start.21 = (bf16[1024,128]{1,0:T(8,128)(2,1)S(1)}, bf16[1024,128]{1,0:T(8,128)(2,1)S(1)}, u32[]{:S(2)}, u32[]{:S(2)}) collective-permute-start(bf16[1024,128]{1,0:T(8,128)(2,1)S(1)} %get-tuple-element.34), channel_id=1, source_target_pairs={{0,14},{1,15},{2,0},{3,1},{4,2},{5,3},{6,4},{7,5},{8,6},{9,7},{10,... | collective-permute-start | bytes 786440 | tf_op jit(solution)/shard_map/ppermute | solution.py:144
  98.1 1.7 %collective-permute-done.36 = bf16[1024,128]{1,0:T(8,128)(2,1)S(1)} collective-permute-done((bf16[1024,128]{1,0:T(8,128)(2,1)S(1)}, bf16[1024,128]{1,0:T(8,128)(2,1)S(1)}, u32[]{:S(2)}, u32[]{:S(2)}) %collective-permute-start.36) | collective-permute-done | bytes 262176 | tf_op jit(solution)/shard_map/ppermute | solution.py:144
  99.8 1.6 %collective-permute-done.32 = bf16[1024,128]{1,0:T(8,128)(2,1)S(1)} collective-permute-done((bf16[1024,128]{1,0:T(8,128)(2,1)S(1)}, bf16[1024,128]{1,0:T(8,128)(2,1)S(1)}, u32[]{:S(2)}, u32[]{:S(2)}) %collective-permute-start.32) | collective-permute-done | bytes 262176 | tf_op jit(solution)/shard_map/ppermute | solution.py:144
  101.5 2.3 %collective-permute-done.21 = bf16[1024,128]{1,0:T(8,128)(2,1)S(1)} collective-permute-done((bf16[1024,128]{1,0:T(8,128)(2,1)S(1)}, bf16[1024,128]{1,0:T(8,128)(2,1)S(1)}, u32[]{:S(2)}, u32[]{:S(2)}) %collective-permute-start.21) | collective-permute-done | bytes 262176 | tf_op jit(solution)/shard_map/ppermute | solution.py:144
  103.9 1.8 %collective-permute-done.17 = bf16[1024,128]{1,0:T(8,128)(2,1)S(1)} collective-permute-done((bf16[1024,128]{1,0:T(8,128)(2,1)S(1)}, bf16[1024,128]{1,0:T(8,128)(2,1)S(1)}, u32[]{:S(2)}, u32[]{:S(2)}) %collective-permute-start.17) | collective-permute-done | bytes 262176 | tf_op jit(solution)/shard_map/ppermute | solution.py:144
  105.8 0.8 pad_maximum_fusion
  (63 shorter events, 3.1 us)
Async XLA Ops:
  0.0 2.9 %copy-start = (bf16[2048,128]{1,0:T(8,128)(2,1)S(1)}, bf16[2048,128]{1,0:T(8,128)(2,1)}, u32[]{:S(2)}) copy-start(bf16[2048,128]{1,0:T(8,128)(2,1)} %three_ref.1) | copy-start | bytes 1572868
  0.1 1.1 %copy-start.1 = (bf16[128,2048]{1,0:T(8,128)(2,1)S(1)}, bf16[128,2048]{1,0:T(8,128)(2,1)}, u32[]{:S(2)}) copy-start(bf16[128,2048]{1,0:T(8,128)(2,1)} %dens_ref.1) | copy-start | bytes 1572868
  1.2 0.7 copy-start.2
  1.8 1.0 copy-start.4
  2.7 0.7 copy-start.3
  2.7 5.6 %collective-permute-start.7 = (bf16[8,128,128]{2,1,0:T(8,128)(2,1)S(1)}, bf16[8,128,128]{2,1,0:T(8,128)(2,1)S(1)}, u32[]{:S(2)}, u32[]{:S(2)}) collective-permute-start(bf16[8,128,128]{2,1,0:T(8,128)(2,1)S(1)} %get-tuple-element.21), channel_id=1, source_target_pairs={{0,1},{1,0},{2,3},{3,2},{4,5},{5,4},{6,7},{7,6},{8,9},{9,8},{10,11... | collective-permute-start | bytes 786440 | tf_op jit(solution)/shard_map/ppermute | solution.py:148
  4.1 6.1 %collective-permute-start.22 = (bf16[1024,128]{1,0:T(8,128)(2,1)S(1)}, bf16[1024,128]{1,0:T(8,128)(2,1)S(1)}, u32[]{:S(2)}, u32[]{:S(2)}) collective-permute-start(bf16[1024,128]{1,0:T(8,128)(2,1)S(1)} %get-tuple-element.27.refs_0_), channel_id=1, source_target_pairs={{0,1},{1,0},{2,3},{3,2},{4,5},{5,4},{6,7},{7,6},{8,9},{9,8},{10,11... | collective-permute-start | bytes 786440 | tf_op jit(solution)/shard_map/ppermute | solution.py:148
  4.2 10.8 %collective-permute-start.23 = (bf16[1024,128]{1,0:T(8,128)(2,1)S(1)}, bf16[1024,128]{1,0:T(8,128)(2,1)S(1)}, u32[]{:S(2)}, u32[]{:S(2)}) collective-permute-start(bf16[1024,128]{1,0:T(8,128)(2,1)S(1)} %get-tuple-element.27.refs_0_), channel_id=1, source_target_pairs={{64,0},{128,64},{192,128},{0,192},{65,1},{129,65},{193,129},{1,193... | collective-permute-start | bytes 786440 | tf_op jit(solution)/shard_map/ppermute | solution.py:138
  5.1 15.6 %collective-permute-start.25 = (bf16[1024,128]{1,0:T(8,128)(2,1)S(1)}, bf16[1024,128]{1,0:T(8,128)(2,1)S(1)}, u32[]{:S(2)}, u32[]{:S(2)}) collective-permute-start(bf16[1024,128]{1,0:T(8,128)(2,1)S(1)} %get-tuple-element.27.refs_0_), channel_id=1, source_target_pairs={{128,0},{192,64},{0,128},{64,192},{129,1},{193,65},{1,129},{65,193... | collective-permute-start | bytes 786440 | tf_op jit(solution)/shard_map/ppermute | solution.py:138
  7.9 15.4 %collective-permute-start.27 = (bf16[1024,128]{1,0:T(8,128)(2,1)S(1)}, bf16[1024,128]{1,0:T(8,128)(2,1)S(1)}, u32[]{:S(2)}, u32[]{:S(2)}) collective-permute-start(bf16[1024,128]{1,0:T(8,128)(2,1)S(1)} %get-tuple-element.27.refs_0_), channel_id=1, source_target_pairs={{192,0},{0,64},{64,128},{128,192},{193,1},{1,65},{65,129},{129,193... | collective-permute-start | bytes 786440 | tf_op jit(solution)/shard_map/ppermute | solution.py:138
  8.3 17.0 %collective-permute-start.1 = (bf16[1024,128]{1,0:T(8,128)(2,1)S(1)}, bf16[1024,128]{1,0:T(8,128)(2,1)S(1)}, u32[]{:S(2)}, u32[]{:S(2)}) collective-permute-start(bf16[1024,128]{1,0:T(8,128)(2,1)S(1)} %get-tuple-element.19.refs_0_), channel_id=1, source_target_pairs={{64,0},{128,64},{192,128},{0,192},{65,1},{129,65},{193,129},{1,193... | collective-permute-start | bytes 786440 | tf_op jit(solution)/shard_map/ppermute | solution.py:138
  10.2 22.3 %collective-permute-start.3 = (bf16[1024,128]{1,0:T(8,128)(2,1)S(1)}, bf16[1024,128]{1,0:T(8,128)(2,1)S(1)}, u32[]{:S(2)}, u32[]{:S(2)}) collective-permute-start(bf16[1024,128]{1,0:T(8,128)(2,1)S(1)} %get-tuple-element.19.refs_0_), channel_id=1, source_target_pairs={{128,0},{192,64},{0,128},{64,192},{129,1},{193,65},{1,129},{65,193... | collective-permute-start | bytes 786440 | tf_op jit(solution)/shard_map/ppermute | solution.py:138
  15.1 17.5 %collective-permute-start.5 = (bf16[1024,128]{1,0:T(8,128)(2,1)S(1)}, bf16[1024,128]{1,0:T(8,128)(2,1)S(1)}, u32[]{:S(2)}, u32[]{:S(2)}) collective-permute-start(bf16[1024,128]{1,0:T(8,128)(2,1)S(1)} %get-tuple-element.19.refs_0_), channel_id=1, source_target_pairs={{192,0},{0,64},{64,128},{128,192},{193,1},{1,65},{65,129},{129,193... | collective-permute-start | bytes 786440 | tf_op jit(solution)/shard_map/ppermute | solution.py:138
  20.7 12.4 %collective-permute-start.11 = (bf16[3,256,128]{2,1,0:T(8,128)(2,1)S(1)}, bf16[3,256,128]{2,1,0:T(8,128)(2,1)S(1)}, u32[]{:S(2)}, u32[]{:S(2)}) collective-permute-start(bf16[3,256,128]{2,1,0:T(8,128)(2,1)S(1)} %pad_maximum_fusion.1.refs_8_), channel_id=1, source_target_pairs={{16,0},{32,16},{48,32},{0,48},{17,1},{33,17},{49,33},{1,49},{18,2}... | collective-permute-start | bytes 589832 | tf_op jit(solution)/shard_map/ppermute | solution.py:138
  23.3 9.8 %collective-permute-start.12 = (bf16[3,256,128]{2,1,0:T(8,128)(2,1)S(1)}, bf16[3,256,128]{2,1,0:T(8,128)(2,1)S(1)}, u32[]{:S(2)}, u32[]{:S(2)}) collective-permute-start(bf16[3,256,128]{2,1,0:T(8,128)(2,1)S(1)} %pad_maximum_fusion.1.refs_8_), channel_id=1, source_target_pairs={{32,0},{48,16},{0,32},{16,48},{33,1},{49,17},{1,33},{17,49},{34,2}... | collective-permute-start | bytes 589832 | tf_op jit(solution)/shard_map/ppermute | solution.py:138
  25.4 13.3 %collective-permute-start.13 = (bf16[3,256,128]{2,1,0:T(8,128)(2,1)S(1)}, bf16[3,256,128]{2,1,0:T(8,128)(2,1)S(1)}, u32[]{:S(2)}, u32[]{:S(2)}) collective-permute-start(bf16[3,256,128]{2,1,0:T(8,128)(2,1)S(1)} %pad_maximum_fusion.1.refs_8_), channel_id=1, source_target_pairs={{48,0},{0,16},{16,32},{32,48},{49,1},{1,17},{17,33},{33,49},{50,2}... | collective-permute-start | bytes 589832 | tf_op jit(solution)/shard_map/ppermute | solution.py:138
  32.5 6.1 %collective-permute-start.24 = (bf16[1024,128]{1,0:T(8,128)(2,1)S(1)}, bf16[1024,128]{1,0:T(8,128)(2,1)S(1)}, u32[]{:S(2)}, u32[]{:S(2)}) collective-permute-start(bf16[1024,128]{1,0:T(8,128)(2,1)S(1)} %collective-permute-done.23.refs_2_), channel_id=1, source_target_pairs={{0,1},{1,0},{2,3},{3,2},{4,5},{5,4},{6,7},{7,6},{8,9},{9,8},{10,11... | collective-permute-start | bytes 786440 | tf_op jit(solution)/shard_map/ppermute | solution.py:148
  32.6 7.9 %collective-permute-start.26 = (bf16[1024,128]{1,0:T(8,128)(2,1)S(1)}, bf16[1024,128]{1,0:T(8,128)(2,1)S(1)}, u32[]{:S(2)}, u32[]{:S(2)}) collective-permute-start(bf16[1024,128]{1,0:T(8,128)(2,1)S(1)} %collective-permute-done.25.refs_4_), channel_id=1, source_target_pairs={{0,1},{1,0},{2,3},{3,2},{4,5},{5,4},{6,7},{7,6},{8,9},{9,8},{10,11... | collective-permute-start | bytes 786440 | tf_op jit(solution)/shard_map/ppermute | solution.py:148
  33.1 7.6 %collective-permute-start.28 = (bf16[1024,128]{1,0:T(8,128)(2,1)S(1)}, bf16[1024,128]{1,0:T(8,128)(2,1)S(1)}, u32[]{:S(2)}, u32[]{:S(2)}) collective-permute-start(bf16[1024,128]{1,0:T(8,128)(2,1)S(1)} %collective-permute-done.27.refs_6_), channel_id=1, source_target_pairs={{0,1},{1,0},{2,3},{3,2},{4,5},{5,4},{6,7},{7,6},{8,9},{9,8},{10,11... | collective-permute-start | bytes 786440 | tf_op jit(solution)/shard_map/ppermute | solution.py:148
  33.2 9.7 %collective-permute-start = (bf16[1024,128]{1,0:T(8,128)(2,1)S(1)}, bf16[1024,128]{1,0:T(8,128)(2,1)S(1)}, u32[]{:S(2)}, u32[]{:S(2)}) collective-permute-start(bf16[1024,128]{1,0:T(8,128)(2,1)S(1)} %get-tuple-element.19.refs_0_), channel_id=1, source_target_pairs={{0,1},{1,0},{2,3},{3,2},{4,5},{5,4},{6,7},{7,6},{8,9},{9,8},{10,11... | collective-permute-start | bytes 786440 | tf_op jit(solution)/shard_map/ppermute | solution.py:148
  38.7 4.9 %collective-permute-start.2 = (bf16[1024,128]{1,0:T(8,128)(2,1)S(1)}, bf16[1024,128]{1,0:T(8,128)(2,1)S(1)}, u32[]{:S(2)}, u32[]{:S(2)}) collective-permute-start(bf16[1024,128]{1,0:T(8,128)(2,1)S(1)} %collective-permute-done.1.refs_2_), channel_id=1, source_target_pairs={{0,1},{1,0},{2,3},{3,2},{4,5},{5,4},{6,7},{7,6},{8,9},{9,8},{10,11... | collective-permute-start | bytes 786440 | tf_op jit(solution)/shard_map/ppermute | solution.py:148
  38.7 16.4 %collective-permute-start.8 = (bf16[5,256,128]{2,1,0:T(8,128)(2,1)S(1)}, bf16[5,256,128]{2,1,0:T(8,128)(2,1)S(1)}, u32[]{:S(2)}, u32[]{:S(2)}) collective-permute-start(bf16[5,256,128]{2,1,0:T(8,128)(2,1)S(1)} %get-tuple-element.45.refs_8_), channel_id=1, source_target_pairs={{16,0},{32,16},{48,32},{0,48},{17,1},{33,17},{49,33},{1,49},{18,2}... | collective-permute-start | bytes 983048 | tf_op jit(solution)/shard_map/ppermute | solution.py:138
  40.4 4.2 %collective-permute-start.4 = (bf16[1024,128]{1,0:T(8,128)(2,1)S(1)}, bf16[1024,128]{1,0:T(8,128)(2,1)S(1)}, u32[]{:S(2)}, u32[]{:S(2)}) collective-permute-start(bf16[1024,128]{1,0:T(8,128)(2,1)S(1)} %collective-permute-done.3.refs_4_), channel_id=1, source_target_pairs={{0,1},{1,0},{2,3},{3,2},{4,5},{5,4},{6,7},{7,6},{8,9},{9,8},{10,11... | collective-permute-start | bytes 786440 | tf_op jit(solution)/shard_map/ppermute | solution.py:148
  40.7 5.9 %collective-permute-start.6 = (bf16[1024,128]{1,0:T(8,128)(2,1)S(1)}, bf16[1024,128]{1,0:T(8,128)(2,1)S(1)}, u32[]{:S(2)}, u32[]{:S(2)}) collective-permute-start(bf16[1024,128]{1,0:T(8,128)(2,1)S(1)} %collective-permute-done.5.refs_6_), channel_id=1, source_target_pairs={{0,1},{1,0},{2,3},{3,2},{4,5},{5,4},{6,7},{7,6},{8,9},{9,8},{10,11... | collective-permute-start | bytes 786440 | tf_op jit(solution)/shard_map/ppermute | solution.py:148
  42.9 14.2 %collective-permute-start.9 = (bf16[5,256,128]{2,1,0:T(8,128)(2,1)S(1)}, bf16[5,256,128]{2,1,0:T(8,128)(2,1)S(1)}, u32[]{:S(2)}, u32[]{:S(2)}) collective-permute-start(bf16[5,256,128]{2,1,0:T(8,128)(2,1)S(1)} %get-tuple-element.45.refs_8_), channel_id=1, source_target_pairs={{32,0},{48,16},{0,32},{16,48},{33,1},{49,17},{1,33},{17,49},{34,2}... | collective-permute-start | bytes 983048 | tf_op jit(solution)/shard_map/ppermute | solution.py:138
  43.6 17.8 %collective-permute-start.10 = (bf16[5,256,128]{2,1,0:T(8,128)(2,1)S(1)}, bf16[5,256,128]{2,1,0:T(8,128)(2,1)S(1)}, u32[]{:S(2)}, u32[]{:S(2)}) collective-permute-start(bf16[5,256,128]{2,1,0:T(8,128)(2,1)S(1)} %get-tuple-element.45.refs_8_), channel_id=1, source_target_pairs={{48,0},{0,16},{16,32},{32,48},{49,1},{1,17},{17,33},{33,49},{50,2}... | collective-permute-start | bytes 983048 | tf_op jit(solution)/shard_map/ppermute | solution.py:138
  44.6 19.3 %collective-permute-start.29 = (bf16[512,128]{1,0:T(8,128)(2,1)S(1)}, bf16[512,128]{1,0:T(8,128)(2,1)S(1)}, u32[]{:S(2)}, u32[]{:S(2)}) collective-permute-start(bf16[512,128]{1,0:T(8,128)(2,1)S(1)} %get-tuple-element.51), channel_id=1, source_target_pairs={{0,2},{1,3},{2,4},{3,5},{4,6},{5,7},{6,8},{7,9},{8,10},{9,11},{10,... | collective-permute-start | bytes 393224 | tf_op jit(solution)/shard_map/ppermute | solution.py:144
  46.6 17.3 %collective-permute-start.33 = (bf16[512,128]{1,0:T(8,128)(2,1)S(1)}, bf16[512,128]{1,0:T(8,128)(2,1)S(1)}, u32[]{:S(2)}, u32[]{:S(2)}) collective-permute-start(bf16[512,128]{1,0:T(8,128)(2,1)S(1)} %get-tuple-element.52), channel_id=1, source_target_pairs={{0,14},{1,15},{2,0},{3,1},{4,2},{5,3},{6,4},{7,5},{8,6},{9,7},{10,... | collective-permute-start | bytes 393224 | tf_op jit(solution)/shard_map/ppermute | solution.py:144
  55.1 17.4 %collective-permute-start.14 = (bf16[512,128]{1,0:T(8,128)(2,1)S(1)}, bf16[512,128]{1,0:T(8,128)(2,1)S(1)}, u32[]{:S(2)}, u32[]{:S(2)}) collective-permute-start(bf16[512,128]{1,0:T(8,128)(2,1)S(1)} %get-tuple-element.49), channel_id=1, source_target_pairs={{0,2},{1,3},{2,4},{3,5},{4,6},{5,7},{6,8},{7,9},{8,10},{9,11},{10,... | collective-permute-start | bytes 393224 | tf_op jit(solution)/shard_map/ppermute | solution.py:144
  57.1 15.5 %collective-permute-start.18 = (bf16[512,128]{1,0:T(8,128)(2,1)S(1)}, bf16[512,128]{1,0:T(8,128)(2,1)S(1)}, u32[]{:S(2)}, u32[]{:S(2)}) collective-permute-start(bf16[512,128]{1,0:T(8,128)(2,1)S(1)} %get-tuple-element.50), channel_id=1, source_target_pairs={{0,14},{1,15},{2,0},{3,1},{4,2},{5,3},{6,4},{7,5},{8,6},{9,7},{10,... | collective-permute-start | bytes 393224 | tf_op jit(solution)/shard_map/ppermute | solution.py:144
  64.0 12.4 %collective-permute-start.30 = (bf16[1024,128]{1,0:T(8,128)(2,1)S(1)}, bf16[1024,128]{1,0:T(8,128)(2,1)S(1)}, u32[]{:S(2)}, u32[]{:S(2)}) collective-permute-start(bf16[1024,128]{1,0:T(8,128)(2,1)S(1)} %get-tuple-element.43), channel_id=1, source_target_pairs={{0,2},{1,3},{2,4},{3,5},{4,6},{5,7},{6,8},{7,9},{8,10},{9,11},{10,... | collective-permute-start | bytes 786440 | tf_op jit(solution)/shard_map/ppermute | solution.py:144
  66.0 10.4 %collective-permute-start.34 = (bf16[1024,128]{1,0:T(8,128)(2,1)S(1)}, bf16[1024,128]{1,0:T(8,128)(2,1)S(1)}, u32[]{:S(2)}, u32[]{:S(2)}) collective-permute-start(bf16[1024,128]{1,0:T(8,128)(2,1)S(1)} %get-tuple-element.44), channel_id=1, source_target_pairs={{0,14},{1,15},{2,0},{3,1},{4,2},{5,3},{6,4},{7,5},{8,6},{9,7},{10,... | collective-permute-start | bytes 786440 | tf_op jit(solution)/shard_map/ppermute | solution.py:144
  72.7 10.7 %collective-permute-start.15 = (bf16[1024,128]{1,0:T(8,128)(2,1)S(1)}, bf16[1024,128]{1,0:T(8,128)(2,1)S(1)}, u32[]{:S(2)}, u32[]{:S(2)}) collective-permute-start(bf16[1024,128]{1,0:T(8,128)(2,1)S(1)} %get-tuple-element.37), channel_id=1, source_target_pairs={{0,2},{1,3},{2,4},{3,5},{4,6},{5,7},{6,8},{7,9},{8,10},{9,11},{10,... | collective-permute-start | bytes 786440 | tf_op jit(solution)/shard_map/ppermute | solution.py:144
  73.0 10.4 %collective-permute-start.19 = (bf16[1024,128]{1,0:T(8,128)(2,1)S(1)}, bf16[1024,128]{1,0:T(8,128)(2,1)S(1)}, u32[]{:S(2)}, u32[]{:S(2)}) collective-permute-start(bf16[1024,128]{1,0:T(8,128)(2,1)S(1)} %get-tuple-element.38), channel_id=1, source_target_pairs={{0,14},{1,15},{2,0},{3,1},{4,2},{5,3},{6,4},{7,5},{8,6},{9,7},{10,... | collective-permute-start | bytes 786440 | tf_op jit(solution)/shard_map/ppermute | solution.py:144
  76.6 12.4 %collective-permute-start.31 = (bf16[1024,128]{1,0:T(8,128)(2,1)S(1)}, bf16[1024,128]{1,0:T(8,128)(2,1)S(1)}, u32[]{:S(2)}, u32[]{:S(2)}) collective-permute-start(bf16[1024,128]{1,0:T(8,128)(2,1)S(1)} %get-tuple-element.41), channel_id=1, source_target_pairs={{0,2},{1,3},{2,4},{3,5},{4,6},{5,7},{6,8},{7,9},{8,10},{9,11},{10,... | collective-permute-start | bytes 786440 | tf_op jit(solution)/shard_map/ppermute | solution.py:144
  76.7 12.4 %collective-permute-start.35 = (bf16[1024,128]{1,0:T(8,128)(2,1)S(1)}, bf16[1024,128]{1,0:T(8,128)(2,1)S(1)}, u32[]{:S(2)}, u32[]{:S(2)}) collective-permute-start(bf16[1024,128]{1,0:T(8,128)(2,1)S(1)} %get-tuple-element.42), channel_id=1, source_target_pairs={{0,14},{1,15},{2,0},{3,1},{4,2},{5,3},{6,4},{7,5},{8,6},{9,7},{10,... | collective-permute-start | bytes 786440 | tf_op jit(solution)/shard_map/ppermute | solution.py:144
  83.5 10.2 %collective-permute-start.16 = (bf16[1024,128]{1,0:T(8,128)(2,1)S(1)}, bf16[1024,128]{1,0:T(8,128)(2,1)S(1)}, u32[]{:S(2)}, u32[]{:S(2)}) collective-permute-start(bf16[1024,128]{1,0:T(8,128)(2,1)S(1)} %get-tuple-element.35), channel_id=1, source_target_pairs={{0,2},{1,3},{2,4},{3,5},{4,6},{5,7},{6,8},{7,9},{8,10},{9,11},{10,... | collective-permute-start | bytes 786440 | tf_op jit(solution)/shard_map/ppermute | solution.py:144
  83.6 10.6 %collective-permute-start.20 = (bf16[1024,128]{1,0:T(8,128)(2,1)S(1)}, bf16[1024,128]{1,0:T(8,128)(2,1)S(1)}, u32[]{:S(2)}, u32[]{:S(2)}) collective-permute-start(bf16[1024,128]{1,0:T(8,128)(2,1)S(1)} %get-tuple-element.36), channel_id=1, source_target_pairs={{0,14},{1,15},{2,0},{3,1},{4,2},{5,3},{6,4},{7,5},{8,6},{9,7},{10,... | collective-permute-start | bytes 786440 | tf_op jit(solution)/shard_map/ppermute | solution.py:144
  89.1 10.7 %collective-permute-start.36 = (bf16[1024,128]{1,0:T(8,128)(2,1)S(1)}, bf16[1024,128]{1,0:T(8,128)(2,1)S(1)}, u32[]{:S(2)}, u32[]{:S(2)}) collective-permute-start(bf16[1024,128]{1,0:T(8,128)(2,1)S(1)} %get-tuple-element.40), channel_id=1, source_target_pairs={{0,14},{1,15},{2,0},{3,1},{4,2},{5,3},{6,4},{7,5},{8,6},{9,7},{10,... | collective-permute-start | bytes 786440 | tf_op jit(solution)/shard_map/ppermute | solution.py:144
  92.5 9.0 %collective-permute-start.32 = (bf16[1024,128]{1,0:T(8,128)(2,1)S(1)}, bf16[1024,128]{1,0:T(8,128)(2,1)S(1)}, u32[]{:S(2)}, u32[]{:S(2)}) collective-permute-start(bf16[1024,128]{1,0:T(8,128)(2,1)S(1)} %get-tuple-element.39), channel_id=1, source_target_pairs={{0,2},{1,3},{2,4},{3,5},{4,6},{5,7},{6,8},{7,9},{8,10},{9,11},{10,... | collective-permute-start | bytes 786440 | tf_op jit(solution)/shard_map/ppermute | solution.py:144
  94.3 9.6 %collective-permute-start.21 = (bf16[1024,128]{1,0:T(8,128)(2,1)S(1)}, bf16[1024,128]{1,0:T(8,128)(2,1)S(1)}, u32[]{:S(2)}, u32[]{:S(2)}) collective-permute-start(bf16[1024,128]{1,0:T(8,128)(2,1)S(1)} %get-tuple-element.34), channel_id=1, source_target_pairs={{0,14},{1,15},{2,0},{3,1},{4,2},{5,3},{6,4},{7,5},{8,6},{9,7},{10,... | collective-permute-start | bytes 786440 | tf_op jit(solution)/shard_map/ppermute | solution.py:144
  98.1 7.6 %collective-permute-start.17 = (bf16[1024,128]{1,0:T(8,128)(2,1)S(1)}, bf16[1024,128]{1,0:T(8,128)(2,1)S(1)}, u32[]{:S(2)}, u32[]{:S(2)}) collective-permute-start(bf16[1024,128]{1,0:T(8,128)(2,1)S(1)} %get-tuple-element.33), channel_id=1, source_target_pairs={{0,2},{1,3},{2,4},{3,5},{4,6},{5,7},{6,8},{7,9},{8,10},{9,11},{10,... | collective-permute-start | bytes 786440 | tf_op jit(solution)/shard_map/ppermute | solution.py:144

commit v2 on v0

v2 whole, which is shorter than its diff:
```python
import functools

import jax
import jax.numpy as jnp
from jax import lax
from jax.experimental import pallas as pl
from jax.experimental.pallas import tpu as pltpu
from jax.sharding import PartitionSpec as P

BS = 32
VMEM_BYTES = 8 * 1024 * 1024

vmem = functools.partial(pl.BlockSpec, memory_space=pltpu.VMEM)
smem = functools.partial(pl.BlockSpec, memory_space=pltpu.SMEM)


def call(kernel, outs, operands, in_specs, scratch=(), flops=0, limit=VMEM_BYTES):
    moved = sum(a.size * a.dtype.itemsize for a in operands)
    moved += sum(o.size * o.dtype.itemsize for o in outs)
    return pl.pallas_call(
        kernel,
        out_shape=outs,
        in_specs=in_specs,
        out_specs=[vmem()] * len(outs),
        scratch_shapes=list(scratch),
        compiler_params=pltpu.CompilerParams(vmem_limit_bytes=limit),
        cost_estimate=pl.CostEstimate(flops=flops, bytes_accessed=moved, transcendentals=0),
    )(*operands)


def masked(three_center, three_mask, density, density_mask, nu_sizes):
    rows, cols = three_center.shape
    deep, wide = density.shape
    share = 128
    count = wide // (2 * share)
    tiles = cols // BS

    def kernel(three_hbm, mask3_hbm, dens_hbm, maskd_hbm, sizes_hbm, live_ref, own_ref, other_ref, *scratch):
        three_ref, mask3_ref, dens_ref, maskd_ref, sizes_ref, held, sems = scratch
        depth = lax.axis_index("depth")
        z, c = depth // 2, depth % 2
        copies = [
            pltpu.make_async_copy(src, dst, sems.at[i])
            for i, (src, dst) in enumerate(
                (
                    (dens_hbm, dens_ref),
                    (maskd_hbm, maskd_ref),
                    (sizes_hbm, sizes_ref),
                    (mask3_hbm, mask3_ref),
                    (three_hbm, three_ref),
                )
            )
        ]
        for copy in copies:
            copy.start()
        for copy in copies[:2]:
            copy.wait()
        lane = lax.broadcasted_iota(jnp.int32, (wide // BS, wide), 1)
        spread = (lane // BS == lax.broadcasted_iota(jnp.int32, lane.shape, 0)).astype(jnp.bfloat16)
        keep = jnp.dot(
            maskd_ref[...].astype(jnp.float32).astype(jnp.bfloat16), spread, preferred_element_type=jnp.float32
        )
        for i in range(deep // BS):
            kept = jnp.broadcast_to(keep[i : i + 1, :], (BS, wide)).astype(jnp.bfloat16)
            held[i * BS : (i + 1) * BS, :] = dens_ref[i * BS : (i + 1) * BS, :] * kept
        for j in range(count):
            first = lax.rem(z + j, count) * 2
            own_at = pl.multiple_of((first + c) * share, share)
            other_at = pl.multiple_of((first + 1 - c) * share, share)
            own_ref[j] = held[:, pl.ds(own_at, share)]
            other_ref[j] = held[:, pl.ds(other_at, share)]
        for copy in copies[2:]:
            copy.wait()
        lane = lax.broadcasted_iota(jnp.int32, (tiles, cols), 1)
        tile = lax.broadcasted_iota(jnp.int32, lane.shape, 0)
        size = jnp.zeros_like(lane)
        for j in range(tiles):
            size = jnp.where(tile == j, sizes_ref[j], size)
        spread = ((lane // BS == tile) & (lane % BS < size)).astype(jnp.bfloat16)
        keep = lax.dot_general(
            mask3_ref[...].astype(jnp.float32).astype(jnp.bfloat16),
            spread,
            (((0,), (0,)), ((), ())),
            preferred_element_type=jnp.float32,
        )
        for g in range(rows // BS):
            kept = jnp.broadcast_to(keep[g : g + 1, :], (BS, cols)).astype(jnp.bfloat16)
            live_ref[g * BS : (g + 1) * BS, :] = three_ref[g * BS : (g + 1) * BS, :] * kept

    return call(
        kernel,
        [jax.ShapeDtypeStruct((rows, cols), jnp.bfloat16)]
        + [jax.ShapeDtypeStruct((count, deep, share), jnp.bfloat16)] * 2,
        (three_center, three_mask.T, density, density_mask, nu_sizes),
        [pl.BlockSpec(memory_space=pltpu.HBM)] * 5,
        [
            pltpu.VMEM((rows, cols), jnp.bfloat16),
            pltpu.VMEM((tiles, rows // BS), jnp.int32),
            pltpu.VMEM((deep, wide), jnp.bfloat16),
            pltpu.VMEM((deep // BS, wide // BS), jnp.int32),
            pltpu.SMEM((tiles,), jnp.int32),
            pltpu.VMEM((deep, wide), jnp.bfloat16),
            pltpu.SemaphoreType.DMA((5,)),
        ],
        limit=56 * 1024 * 1024,
    )


def dots(three, dens, jobs):
    pieces = len(dens)
    k_piece, share = dens[0].shape[1:]
    tile = 256
    arrays = []
    for array, _ in three:
        if not any(array is other for other in arrays):
            arrays.append(array)
    where = [[array is other for other in arrays].index(True) for array, _ in three]
    shares = [j for _, _, picked, _ in jobs for j in picked]
    shares = sorted(set(shares), key=shares.index)

    def kernel(*refs):
        a_refs, b_refs = refs[: len(arrays)], refs[len(arrays) : len(arrays) + pieces]
        outs, held = list(refs[len(arrays) + pieces : -1]), refs[-1]
        across = lax.axis_index("col") - lax.axis_index("row")
        turn = jnp.where(lax.axis_index("depth") % 2 == 0, across, -across) + pieces
        for s in range(pieces):
            at = pl.multiple_of(lax.rem(s + turn, pieces) * k_piece, k_piece)
            for n, j in enumerate(shares):
                held[pl.ds(at, k_piece), n * share : (n + 1) * share] = b_refs[s][j]
        for first, rows, picked, wanted in jobs:
            lo = shares.index(picked[0]) * share
            right = held[:, lo : lo + len(picked) * share]
            for m in range(0, rows, tile):
                left = jnp.concatenate(
                    [a_refs[w][base + first + m : base + first + m + tile, :] for w, (_, base) in zip(where, three)],
                    axis=1,
                )
                total = jnp.dot(left, right, preferred_element_type=jnp.float32)
                for out, (kind, r0, height, c0, width) in zip(outs, wanted):
                    if r0 <= m < r0 + height:
                        out[m - r0 : m - r0 + tile, :] = total[:, c0 : c0 + width].astype(kind)
            outs = outs[len(wanted) :]

    deep = pieces * k_piece
    return call(
        kernel,
        [jax.ShapeDtypeStruct((o[2], o[4]), o[0]) for job in jobs for o in job[3]],
        (*arrays, *dens),
        [vmem()] * (len(arrays) + pieces),
        [pltpu.VMEM((deep, len(shares) * share), jnp.bfloat16)],
        flops=2 * deep * share * sum(rows * len(picked) for _, rows, picked, _ in jobs),
    )


def along_z(block, distance):
    count = lax.axis_size("depth") // 2
    route = [(z * 2 + c, (z + distance) % count * 2 + c) for z in range(count) for c in range(2)]
    return lax.ppermute(block, "depth", route)


def other_core(block):
    return lax.ppermute(block, "depth", [(i, i ^ 1) for i in range(lax.axis_size("depth"))])


def opposed(block, axis, step):
    count, depth = lax.axis_size(axis), lax.axis_size("depth")
    route = [
        (i * depth + d, (i + (step if d % 2 == 0 else -step)) % count * depth + d)
        for i in range(count)
        for d in range(depth)
    ]
    return lax.ppermute(block, (axis, "depth"), route)


def after(block, *earlier):
    return lax.optimization_barrier((block, *earlier))[0]


def on_device(three_center, three_mask, density, density_mask, nu_sizes):
    live, own, other = masked(three_center, three_mask, density, density_mask, nu_sizes)
    dens = jnp.concatenate([own, other_core(other)], axis=1)
    a_back, b_back = opposed(live, "row", 1), opposed(dens, "col", 1)
    a_front, b_front = opposed(live, "row", -1), opposed(dens, "col", -1)
    a_back, a_front, b_back, b_front = lax.optimization_barrier((a_back, a_front, b_back, b_front))
    a_far, b_far = opposed(a_back, "row", 1), opposed(b_back, "col", 1)
    live_other, front_other, back_other = other_core(live), other_core(a_front), other_core(a_back)
    far_other = other_core(a_far)
    n = live.shape[0]
    three = [(x, 0) for x in (live, live_other, a_front, back_other, a_far, far_other, a_back, front_other)]
    dens = [dens, b_front, b_far, b_back]

    share = dens[0].shape[2]
    half = n // 2
    bf16, f32 = jnp.bfloat16, jnp.float32

    def later(done):
        return [(after(live, done), 0)] + three[1:]

    def plus(near, arrived):
        return (near + arrived.astype(f32)).astype(bf16)

    def job(first, kinds, picked):
        return [(first, half, picked, [(kind, 0, half, i * share, share) for i, kind in enumerate(kinds)])]

    (ra4,) = dots(three, dens, job(0, (bf16,), (4,)))
    ra = along_z(ra4, 1)
    (lb4,) = dots(later(ra4), dens, job(half, (bf16,), (4,)))
    lb = along_z(lb4, -1)
    rb3, lb3 = dots(later(lb4), dens, job(half, (bf16, f32), (3, 5)))
    rb = along_z(rb3, 1)
    ra3, la3 = dots(later(rb3), dens, job(0, (f32, bf16), (3, 5)))
    la = along_z(la3, -1)
    ra2, la2, rb2, lb2 = dots(later(la3), dens, job(0, (f32, f32), (2, 6)) + job(half, (f32, f32), (2, 6)))
    ra, lb = along_z(plus(ra3, ra), 1), along_z(plus(lb3, lb), -1)
    ra1, la1, rb1, lb1 = dots(later(ra2), dens, job(0, (f32, f32), (1, 7)) + job(half, (f32, f32), (1, 7)))
    la, rb = along_z(plus(la2, la), -1), along_z(plus(rb2, rb), 1)
    ra, lb = along_z(plus(ra2, ra), 1), along_z(plus(lb2, lb), -1)
    (end,) = dots(later(ra1), dens, [(0, n, (0,), [(f32, 0, n, 0, share)])])
    la, rb = along_z(plus(la1, la), -1), along_z(plus(rb1, rb), 1)
    ra, lb = along_z(plus(ra1, ra), 1), along_z(plus(lb1, lb), -1)
    top = end[:half] + la.astype(f32) + ra.astype(f32)
    bottom = end[half:] + rb.astype(f32) + lb.astype(f32)
    return jnp.concatenate([top.astype(bf16), bottom.astype(bf16)])


def solution(mesh):
    in_specs = (
        P("col", ("row", "depth")),
        P("col", ("row", "depth")),
        P(("col", "depth"), "row"),
        P(("col", "depth"), "row"),
        P(("row", "depth")),
    )
    out_specs = P("col", ("row", "depth"))
    return jax.shard_map(
        on_device, mesh=mesh, in_specs=in_specs, out_specs=out_specs, check_vma=False
    )
```

time: 193 us -> 85.9 us (0.45)
  waiting for transfers between devices: 103 us -> 41.2 us
  matrix products: 33.9 us -> 0 us
  local copies, waits for them, and re-layouts: 21.9 us -> 1.07 us
  starting transfers between devices: 15.7 us -> 32.2 us
  between operations: 13.5 us -> 0.22 us
  Pallas kernels: 0 us -> 9.5 us
  other arithmetic: 4.73 us -> 1.55 us
    unnamed x2 -> x0, waiting for transfers between devices: 71 us -> none
    dot_general x4 -> x0, matrix products: 33.9 us -> none  [on_device(): jnp.dot(live_tile, dens_tile, preferred_element_type=jnp.float32)]
    ppermute x10 -> x25, starting transfers between devices: 15.7 us -> 32.2 us  [the longest x14 23 us: along_z(): return lax.ppermute(block, 'depth', route)]
    unnamed x3, local copies, waits for them, and re-layouts: 15.6 us -> 1.03 us
    ppermute x10 -> x25, waiting for transfers between devices: 31.6 us -> 41.2 us  [the longest x14 20.2 us: along_z(): return lax.ppermute(block, 'depth', route)]
    pallas_call x0 -> x8, Pallas kernels: none -> 9.5 us  [call(): pl.pallas_call(kernel, out_shape=outs, in_specs=in_specs, out_specs=[vmem...]
    mul x4 -> x0, local copies, waits for them, and re-layouts: 6.36 us -> none  [the longest x2 3.51 us: mask_three(): shaped = three_center.reshape(row_blocks, BS, col_blocks, BS) * keep_mask]
  transfers between devices with their start and end apart: 11 -> 25, of which waited for: 9 -> 12; matrix products, arithmetic and copies ran while one was open for 13% -> 2% of each run, Pallas kernels for 0% -> 6%
where the time goes in v2:
time: 85.9 us; the launch traced here: 85.8 us
  waiting for transfers between devices  41.2 us (48%)
  starting transfers between devices  32.2 us (37%)
  Pallas kernels  9.5 us (11%)
  other arithmetic  1.55 us (2%)
  local copies, waits for them, and re-layouts  1.07 us (1%)
    ppermute x14, starting transfers between devices, along_z(): return lax.ppermute(block, 'depth', route)  23 us
    ppermute x14, waiting for transfers between devices, along_z(): return lax.ppermute(block, 'depth', route)  20.2 us
    ppermute x6, waiting for transfers between devices, opposed(): return lax.ppermute(block, (axis, 'depth'), route)  19.6 us
    pallas_call x8, Pallas kernels, call(): pl.pallas_call(kernel, out_shape=outs, in_specs=in_specs, out_specs=[vmem...  9.5 us
    ppermute x6, starting transfers between devices, opposed(): return lax.ppermute(block, (axis, 'depth'), route)  8.62 us
  transfers between devices with their start and end apart: 25, of which 12 were waited for; matrix products, arithmetic and copies ran while one was open for 2% of the time, Pallas kernels for 6%

profile of v2, /device:TPU:24, one launch (start us, length us, event | category | flops | bytes accessed | tf_op | source)
XLA Modules:
  0.0 85.8 jit_solution(5067295864996700691)
XLA Ops:
  0.0 2.5 %shard_map.55 = (bf16[2048,128]{1,0:T(8,128)(2,1)}, bf16[8,128,128]{2,1,0:T(8,128)(2,1)}, bf16[8,128,128]{2,1,0:T(8,128)(2,1)}) custom-call(bf16[2048,128]{1,0:T(8,128)(2,1)} %three_hbm.1, s32[4,64]{1,0:T(4,128)} %bitcast.1, bf16[128,2048]{1,0:T(8,128)(2,1)} %dens_hbm.1, s32[4,64]{1,0:T(4,128)} %maskd_hbm.1, s32[4]{0:T(128)} %sizes_hbm.1), custom_call_target="tpu_custom_call" | custom-call | bytes 2099216 | tf_op jit(solution)/shard_map/pallas_call | solution.py:20
  2.5 0.1 collective-permute-start.3
  2.6 2.8 %collective-permute-start.2 = (bf16[2048,128]{1,0:T(8,128)(2,1)}, bf16[2048,128]{1,0:T(8,128)(2,1)S(1)}, u32[]{:S(2)}, u32[]{:S(2)}) collective-permute-start(bf16[2048,128]{1,0:T(8,128)(2,1)} %get-tuple-element.46.refs_0_), channel_id=1, source_target_pairs={{0,192},{1,65},{2,194},{3,67},{4,196},{5,69},{6,198},{7,71},{8,200... | collective-permute-start | bytes 1572872 | tf_op jit(solution)/shard_map/ppermute | solution.py:172
  5.4 1.0 %constant_dynamic-update-slice_fusion.1 = bf16[8,256,128]{2,1,0:T(8,128)(2,1)S(1)} fusion(bf16[8,128,128]{2,1,0:T(8,128)(2,1)} %get-tuple-element.31), kind=kLoop, calls=%fused_computation.18 | loop fusion | bytes 524288
  6.5 0.8 collective-permute-start.5
  7.3 2.5 %collective-permute-start.4 = (bf16[8,256,128]{2,1,0:T(8,128)(2,1)S(1)}, bf16[8,256,128]{2,1,0:T(8,128)(2,1)S(1)}, u32[]{:S(2)}, u32[]{:S(2)}) collective-permute-start(bf16[8,256,128]{2,1,0:T(8,128)(2,1)S(1)} %constant_dynamic-update-slice_fusion.refs_8_), channel_id=1, source_target_pairs={{0,16},{1,49},{2,18},{3,51},{4,20},{5,53},{6,22},{7,55},{8,24},{9,... | collective-permute-start | bytes 1572872 | tf_op jit(solution)/shard_map/ppermute | solution.py:172
  9.8 7.9 %collective-permute-done.2.refs_2_ = bf16[2048,128]{1,0:T(8,128)(2,1)S(1)} collective-permute-done((bf16[2048,128]{1,0:T(8,128)(2,1)}, bf16[2048,128]{1,0:T(8,128)(2,1)S(1)}, u32[]{:S(2)}, u32[]{:S(2)}) %collective-permute-start.2) | collective-permute-done | bytes 524320 | tf_op jit(solution)/shard_map/ppermute | solution.py:172
  17.7 0.6 collective-permute-done.1.refs_6_
  18.3 3.2 %collective-permute-done.5.refs_9_ = bf16[8,256,128]{2,1,0:T(8,128)(2,1)S(1)} collective-permute-done((bf16[8,256,128]{2,1,0:T(8,128)(2,1)S(1)}, bf16[8,256,128]{2,1,0:T(8,128)(2,1)S(1)}, u32[]{:S(2)}, u32[]{:S(2)}) %collective-permute-start.5) | collective-permute-done | bytes 524320 | tf_op jit(solution)/shard_map/ppermute | solution.py:172
  21.5 1.2 %collective-permute-start.7 = (bf16[2048,128]{1,0:T(8,128)(2,1)S(1)}, bf16[2048,128]{1,0:T(8,128)(2,1)S(1)}, u32[]{:S(2)}, u32[]{:S(2)}) collective-permute-start(bf16[2048,128]{1,0:T(8,128)(2,1)S(1)} %collective-permute-done.1.refs_6_), channel_id=1, source_target_pairs={{0,64},{1,193},{2,66},{3,195},{4,68},{5,197},{6,70},{7,199},{8,72}... | collective-permute-start | bytes 1572872 | tf_op jit(solution)/shard_map/ppermute | solution.py:172
  22.7 0.5 collective-permute-start.6
  23.2 1.3 %collective-permute-start.10 = (bf16[8,256,128]{2,1,0:T(8,128)(2,1)S(1)}, bf16[8,256,128]{2,1,0:T(8,128)(2,1)S(1)}, u32[]{:S(2)}, u32[]{:S(2)}) collective-permute-start(bf16[8,256,128]{2,1,0:T(8,128)(2,1)S(1)} %collective-permute-done.4.refs_11_), channel_id=1, source_target_pairs={{0,16},{1,49},{2,18},{3,51},{4,20},{5,53},{6,22},{7,55},{8,24},{9,... | collective-permute-start | bytes 1572872 | tf_op jit(solution)/shard_map/ppermute | solution.py:172
  24.5 7.4 %collective-permute-done.7.refs_4_ = bf16[2048,128]{1,0:T(8,128)(2,1)S(1)} collective-permute-done((bf16[2048,128]{1,0:T(8,128)(2,1)S(1)}, bf16[2048,128]{1,0:T(8,128)(2,1)S(1)}, u32[]{:S(2)}, u32[]{:S(2)}) %collective-permute-start.7) | collective-permute-done | bytes 524320 | tf_op jit(solution)/shard_map/ppermute | solution.py:172
  31.9 0.5 collective-permute-done.10.refs_10_
  32.4 1.4 %collective-permute-done.8.refs_5_ = bf16[2048,128]{1,0:T(8,128)(2,1)S(1)} collective-permute-done((bf16[2048,128]{1,0:T(8,128)(2,1)S(1)}, bf16[2048,128]{1,0:T(8,128)(2,1)S(1)}, u32[]{:S(2)}, u32[]{:S(2)}) %collective-permute-start.8) | collective-permute-done | bytes 524320 | tf_op jit(solution)/shard_map/ppermute | solution.py:162
  33.8 0.7 shard_map.56
  34.6 0.7 shard_map.57
  35.3 6.5 %collective-permute-start.21 = (bf16[1024,128]{1,0:T(8,128)(2,1)S(1)}, bf16[1024,128]{1,0:T(8,128)(2,1)S(1)}, u32[]{:S(2)}, u32[]{:S(2)}) collective-permute-start(bf16[1024,128]{1,0:T(8,128)(2,1)S(1)} %shard_map.57), channel_id=1, source_target_pairs={{0,14},{1,15},{2,0},{3,1},{4,2},{5,3},{6,4},{7,5},{8,6},{9,7},{10,... | collective-permute-start | bytes 786440 | tf_op jit(solution)/shard_map/ppermute | solution.py:158
  41.8 0.8 shard_map.58
  42.6 0.3 collective-permute-start.18
  42.9 0.8 shard_map.59
  43.7 3.3 %collective-permute-start.11 = (bf16[1024,128]{1,0:T(8,128)(2,1)S(1)}, bf16[1024,128]{1,0:T(8,128)(2,1)S(1)}, u32[]{:S(2)}, u32[]{:S(2)}) collective-permute-start(bf16[1024,128]{1,0:T(8,128)(2,1)S(1)} %get-tuple-element.41), channel_id=1, source_target_pairs={{0,14},{1,15},{2,0},{3,1},{4,2},{5,3},{6,4},{7,5},{8,6},{9,7},{10,... | collective-permute-start | bytes 786440 | tf_op jit(solution)/shard_map/ppermute | solution.py:158
  47.0 1.3 %shard_map.60 = (f32[1024,128]{1,0:T(8,128)S(1)}, f32[1024,128]{1,0:T(8,128)S(1)}, f32[1024,128]{1,0:T(8,128)S(1)}, f32[1024,128]{1,0:T(8,128)S(1)}) custom-call(bf16[2048,128]{1,0:T(8,128)(2,1)S(1)} %copy-done, bf16[2048,128]{1,0:T(8,128)(2,1)S(1)} %collective-permute-done.refs_1_, bf16[2048,128]{1,0:T(8,128)(2,1)S(1)} %collective-permute-done.2.refs_2_, ...), custom_call_target="tpu_custom_call" | custom-call | flops 1073741824 | bytes 8388608 | tf_op jit(solution)/shard_map/pallas_call | solution.py:20
  48.3 1.3 %shard_map.61 = (f32[1024,128]{1,0:T(8,128)S(1)}, f32[1024,128]{1,0:T(8,128)S(1)}, f32[1024,128]{1,0:T(8,128)S(1)}, f32[1024,128]{1,0:T(8,128)S(1)}) custom-call(bf16[2048,128]{1,0:T(8,128)(2,1)S(1)} %copy-done, bf16[2048,128]{1,0:T(8,128)(2,1)S(1)} %collective-permute-done.refs_1_, bf16[2048,128]{1,0:T(8,128)(2,1)S(1)} %collective-permute-done.2.refs_2_, ...), custom_call_target="tpu_custom_call" | custom-call | flops 1073741824 | bytes 8388608 | tf_op jit(solution)/shard_map/pallas_call | solution.py:20
  49.7 0.1 add_convert_fusion.2
  49.8 2.5 %collective-permute-start.22 = (bf16[1024,128]{1,0:T(8,128)(2,1)S(1)}, bf16[1024,128]{1,0:T(8,128)(2,1)S(1)}, u32[]{:S(2)}, u32[]{:S(2)}) collective-permute-start(bf16[1024,128]{1,0:T(8,128)(2,1)S(1)} %add_convert_fusion.2), channel_id=1, source_target_pairs={{0,14},{1,15},{2,0},{3,1},{4,2},{5,3},{6,4},{7,5},{8,6},{9,7},{10,... | collective-permute-start | bytes 786440 | tf_op jit(solution)/shard_map/ppermute | solution.py:158
  52.3 0.1 collective-permute-start.15
  52.4 5.4 %collective-permute-done.18 = bf16[1024,128]{1,0:T(8,128)(2,1)S(1)} collective-permute-done((bf16[1024,128]{1,0:T(8,128)(2,1)S(1)}, bf16[1024,128]{1,0:T(8,128)(2,1)S(1)}, u32[]{:S(2)}, u32[]{:S(2)}) %collective-permute-start.18) | collective-permute-done | bytes 262176 | tf_op jit(solution)/shard_map/ppermute | solution.py:158
  57.9 0.1 collective-permute-start.19
  58.0 0.1 add_convert_fusion.9
  58.0 3.3 %collective-permute-start.12 = (bf16[1024,128]{1,0:T(8,128)(2,1)S(1)}, bf16[1024,128]{1,0:T(8,128)(2,1)S(1)}, u32[]{:S(2)}, u32[]{:S(2)}) collective-permute-start(bf16[1024,128]{1,0:T(8,128)(2,1)S(1)} %add_convert_fusion.9), channel_id=1, source_target_pairs={{0,14},{1,15},{2,0},{3,1},{4,2},{5,3},{6,4},{7,5},{8,6},{9,7},{10,... | collective-permute-start | bytes 786440 | tf_op jit(solution)/shard_map/ppermute | solution.py:158
  61.3 0.1 add_convert_fusion.1
  61.4 1.3 %collective-permute-start.23 = (bf16[1024,128]{1,0:T(8,128)(2,1)S(1)}, bf16[1024,128]{1,0:T(8,128)(2,1)S(1)}, u32[]{:S(2)}, u32[]{:S(2)}) collective-permute-start(bf16[1024,128]{1,0:T(8,128)(2,1)S(1)} %add_convert_fusion.1), channel_id=1, source_target_pairs={{0,14},{1,15},{2,0},{3,1},{4,2},{5,3},{6,4},{7,5},{8,6},{9,7},{10,... | collective-permute-start | bytes 786440 | tf_op jit(solution)/shard_map/ppermute | solution.py:158
  62.7 0.7 collective-permute-done.15
  63.5 0.1 collective-permute-start.16
  63.6 5.4 %collective-permute-done.19 = bf16[1024,128]{1,0:T(8,128)(2,1)S(1)} collective-permute-done((bf16[1024,128]{1,0:T(8,128)(2,1)S(1)}, bf16[1024,128]{1,0:T(8,128)(2,1)S(1)}, u32[]{:S(2)}, u32[]{:S(2)}) %collective-permute-start.19) | collective-permute-done | bytes 262176 | tf_op jit(solution)/shard_map/ppermute | solution.py:158
  69.0 0.1 add_convert_fusion.3
  69.1 0.1 collective-permute-start.20
  69.2 0.1 add_convert_fusion.8
  69.3 3.3 %collective-permute-start.13 = (bf16[1024,128]{1,0:T(8,128)(2,1)S(1)}, bf16[1024,128]{1,0:T(8,128)(2,1)S(1)}, u32[]{:S(2)}, u32[]{:S(2)}) collective-permute-start(bf16[1024,128]{1,0:T(8,128)(2,1)S(1)} %add_convert_fusion.8), channel_id=1, source_target_pairs={{0,14},{1,15},{2,0},{3,1},{4,2},{5,3},{6,4},{7,5},{8,6},{9,7},{10,... | collective-permute-start | bytes 786440 | tf_op jit(solution)/shard_map/ppermute | solution.py:158
  72.6 2.0 %collective-permute-start.24 = (bf16[1024,128]{1,0:T(8,128)(2,1)S(1)}, bf16[1024,128]{1,0:T(8,128)(2,1)S(1)}, u32[]{:S(2)}, u32[]{:S(2)}) collective-permute-start(bf16[1024,128]{1,0:T(8,128)(2,1)S(1)} %add_convert_fusion), channel_id=1, source_target_pairs={{0,14},{1,15},{2,0},{3,1},{4,2},{5,3},{6,4},{7,5},{8,6},{9,7},{10,... | collective-permute-start | bytes 786440 | tf_op jit(solution)/shard_map/ppermute | solution.py:158
  74.7 0.1 collective-permute-start.17
  74.8 1.3 %shard_map.62 = f32[2048,128]{1,0:T(8,128)S(1)} custom-call(bf16[2048,128]{1,0:T(8,128)(2,1)S(1)} %copy-done, bf16[2048,128]{1,0:T(8,128)(2,1)S(1)} %collective-permute-done.refs_1_, bf16[2048,128]{1,0:T(8,128)(2,1)S(1)} %collective-permute-done.2.refs_2_, bf16[2048,128]{1,0:T(8,128)(2,1)S(1)} %collective-permute-done.6.refs_3_, ...), custom_call_target="tpu_custom_call" | custom-call | flops 536870912 | bytes 7340032 | tf_op jit(solution)/shard_map/pallas_call | solution.py:20
  76.1 4.1 %collective-permute-done.20 = bf16[1024,128]{1,0:T(8,128)(2,1)S(1)} collective-permute-done((bf16[1024,128]{1,0:T(8,128)(2,1)S(1)}, bf16[1024,128]{1,0:T(8,128)(2,1)S(1)}, u32[]{:S(2)}, u32[]{:S(2)}) %collective-permute-start.20) | collective-permute-done | bytes 262176 | tf_op jit(solution)/shard_map/ppermute | solution.py:158
  80.3 1.5 %collective-permute-done.24 = bf16[1024,128]{1,0:T(8,128)(2,1)S(1)} collective-permute-done((bf16[1024,128]{1,0:T(8,128)(2,1)S(1)}, bf16[1024,128]{1,0:T(8,128)(2,1)S(1)}, u32[]{:S(2)}, u32[]{:S(2)}) %collective-permute-start.24) | collective-permute-done | bytes 262176 | tf_op jit(solution)/shard_map/ppermute | solution.py:158
  81.8 3.0 %collective-permute-done.17 = bf16[1024,128]{1,0:T(8,128)(2,1)S(1)} collective-permute-done((bf16[1024,128]{1,0:T(8,128)(2,1)S(1)}, bf16[1024,128]{1,0:T(8,128)(2,1)S(1)}, u32[]{:S(2)}, u32[]{:S(2)}) %collective-permute-start.17) | collective-permute-done | bytes 262176 | tf_op jit(solution)/shard_map/ppermute | solution.py:158
  84.8 0.2 fusion.3
  84.9 0.8 pad_maximum_fusion
  (26 shorter events, 0.4 us)
Async XLA Ops:
  2.5 4.0 %collective-permute-start.3 = (bf16[8,128,128]{2,1,0:T(8,128)(2,1)}, bf16[8,128,128]{2,1,0:T(8,128)(2,1)S(1)}, u32[]{:S(2)}, u32[]{:S(2)}) collective-permute-start(bf16[8,128,128]{2,1,0:T(8,128)(2,1)} %get-tuple-element.32), channel_id=1, source_target_pairs={{0,1},{1,0},{2,3},{3,2},{4,5},{5,4},{6,7},{7,6},{8,9},{9,8},{10,11... | collective-permute-start | bytes 786440 | tf_op jit(solution)/shard_map/ppermute | solution.py:162
  2.6 15.1 %collective-permute-start.2 = (bf16[2048,128]{1,0:T(8,128)(2,1)}, bf16[2048,128]{1,0:T(8,128)(2,1)S(1)}, u32[]{:S(2)}, u32[]{:S(2)}) collective-permute-start(bf16[2048,128]{1,0:T(8,128)(2,1)} %get-tuple-element.46.refs_0_), channel_id=1, source_target_pairs={{0,192},{1,65},{2,194},{3,67},{4,196},{5,69},{6,198},{7,71},{8,200... | collective-permute-start | bytes 1572872 | tf_op jit(solution)/shard_map/ppermute | solution.py:172
  5.4 12.9 %collective-permute-start.1 = (bf16[2048,128]{1,0:T(8,128)(2,1)}, bf16[2048,128]{1,0:T(8,128)(2,1)S(1)}, u32[]{:S(2)}, u32[]{:S(2)}) collective-permute-start(bf16[2048,128]{1,0:T(8,128)(2,1)} %get-tuple-element.46.refs_0_), channel_id=1, source_target_pairs={{0,64},{1,193},{2,66},{3,195},{4,68},{5,197},{6,70},{7,199},{8,72}... | collective-permute-start | bytes 1572872 | tf_op jit(solution)/shard_map/ppermute | solution.py:172
  5.4 17.3 %copy-start = (bf16[2048,128]{1,0:T(8,128)(2,1)S(1)}, bf16[2048,128]{1,0:T(8,128)(2,1)}, u32[]{:S(2)}) copy-start(bf16[2048,128]{1,0:T(8,128)(2,1)} %get-tuple-element.46.refs_0_) | copy-start | bytes 1572868
  6.5 15.0 %collective-permute-start.5 = (bf16[8,256,128]{2,1,0:T(8,128)(2,1)S(1)}, bf16[8,256,128]{2,1,0:T(8,128)(2,1)S(1)}, u32[]{:S(2)}, u32[]{:S(2)}) collective-permute-start(bf16[8,256,128]{2,1,0:T(8,128)(2,1)S(1)} %constant_dynamic-update-slice_fusion.refs_8_), channel_id=1, source_target_pairs={{0,48},{1,17},{2,50},{3,19},{4,52},{5,21},{6,54},{7,23},{8,56},{9,... | collective-permute-start | bytes 1572872 | tf_op jit(solution)/shard_map/ppermute | solution.py:172
  7.3 14.2 %collective-permute-start.4 = (bf16[8,256,128]{2,1,0:T(8,128)(2,1)S(1)}, bf16[8,256,128]{2,1,0:T(8,128)(2,1)S(1)}, u32[]{:S(2)}, u32[]{:S(2)}) collective-permute-start(bf16[8,256,128]{2,1,0:T(8,128)(2,1)S(1)} %constant_dynamic-update-slice_fusion.refs_8_), channel_id=1, source_target_pairs={{0,16},{1,49},{2,18},{3,51},{4,20},{5,53},{6,22},{7,55},{8,24},{9,... | collective-permute-start | bytes 1572872 | tf_op jit(solution)/shard_map/ppermute | solution.py:172
  21.5 10.4 %collective-permute-start.7 = (bf16[2048,128]{1,0:T(8,128)(2,1)S(1)}, bf16[2048,128]{1,0:T(8,128)(2,1)S(1)}, u32[]{:S(2)}, u32[]{:S(2)}) collective-permute-start(bf16[2048,128]{1,0:T(8,128)(2,1)S(1)} %collective-permute-done.1.refs_6_), channel_id=1, source_target_pairs={{0,64},{1,193},{2,66},{3,195},{4,68},{5,197},{6,70},{7,199},{8,72}... | collective-permute-start | bytes 1572872 | tf_op jit(solution)/shard_map/ppermute | solution.py:172
  22.7 9.2 %collective-permute-start = (bf16[2048,128]{1,0:T(8,128)(2,1)S(1)}, bf16[2048,128]{1,0:T(8,128)(2,1)S(1)}, u32[]{:S(2)}, u32[]{:S(2)}) collective-permute-start(bf16[2048,128]{1,0:T(8,128)(2,1)S(1)} %copy-done), channel_id=1, source_target_pairs={{0,1},{1,0},{2,3},{3,2},{4,5},{5,4},{6,7},{7,6},{8,9},{9,8},{10,11... | collective-permute-start | bytes 1572872 | tf_op jit(solution)/shard_map/ppermute | solution.py:162
  22.7 9.7 %collective-permute-start.6 = (bf16[2048,128]{1,0:T(8,128)(2,1)S(1)}, bf16[2048,128]{1,0:T(8,128)(2,1)S(1)}, u32[]{:S(2)}, u32[]{:S(2)}) collective-permute-start(bf16[2048,128]{1,0:T(8,128)(2,1)S(1)} %collective-permute-done.1.refs_6_), channel_id=1, source_target_pairs={{0,1},{1,0},{2,3},{3,2},{4,5},{5,4},{6,7},{7,6},{8,9},{9,8},{10,11... | collective-permute-start | bytes 1572872 | tf_op jit(solution)/shard_map/ppermute | solution.py:162
  23.2 8.7 %collective-permute-start.9 = (bf16[2048,128]{1,0:T(8,128)(2,1)S(1)}, bf16[2048,128]{1,0:T(8,128)(2,1)S(1)}, u32[]{:S(2)}, u32[]{:S(2)}) collective-permute-start(bf16[2048,128]{1,0:T(8,128)(2,1)S(1)} %collective-permute-done.2.refs_2_), channel_id=1, source_target_pairs={{0,1},{1,0},{2,3},{3,2},{4,5},{5,4},{6,7},{7,6},{8,9},{9,8},{10,11... | collective-permute-start | bytes 1572872 | tf_op jit(solution)/shard_map/ppermute | solution.py:162
  23.2 9.2 %collective-permute-start.10 = (bf16[8,256,128]{2,1,0:T(8,128)(2,1)S(1)}, bf16[8,256,128]{2,1,0:T(8,128)(2,1)S(1)}, u32[]{:S(2)}, u32[]{:S(2)}) collective-permute-start(bf16[8,256,128]{2,1,0:T(8,128)(2,1)S(1)} %collective-permute-done.4.refs_11_), channel_id=1, source_target_pairs={{0,16},{1,49},{2,18},{3,51},{4,20},{5,53},{6,22},{7,55},{8,24},{9,... | collective-permute-start | bytes 1572872 | tf_op jit(solution)/shard_map/ppermute | solution.py:172
  31.9 1.9 %collective-permute-start.8 = (bf16[2048,128]{1,0:T(8,128)(2,1)S(1)}, bf16[2048,128]{1,0:T(8,128)(2,1)S(1)}, u32[]{:S(2)}, u32[]{:S(2)}) collective-permute-start(bf16[2048,128]{1,0:T(8,128)(2,1)S(1)} %collective-permute-done.7.refs_4_), channel_id=1, source_target_pairs={{0,1},{1,0},{2,3},{3,2},{4,5},{5,4},{6,7},{7,6},{8,9},{9,8},{10,11... | collective-permute-start | bytes 1572872 | tf_op jit(solution)/shard_map/ppermute | solution.py:162
  35.3 14.4 %collective-permute-start.21 = (bf16[1024,128]{1,0:T(8,128)(2,1)S(1)}, bf16[1024,128]{1,0:T(8,128)(2,1)S(1)}, u32[]{:S(2)}, u32[]{:S(2)}) collective-permute-start(bf16[1024,128]{1,0:T(8,128)(2,1)S(1)} %shard_map.57), channel_id=1, source_target_pairs={{0,14},{1,15},{2,0},{3,1},{4,2},{5,3},{6,4},{7,5},{8,6},{9,7},{10,... | collective-permute-start | bytes 786440 | tf_op jit(solution)/shard_map/ppermute | solution.py:158
  41.8 10.5 %collective-permute-start.14 = (bf16[1024,128]{1,0:T(8,128)(2,1)S(1)}, bf16[1024,128]{1,0:T(8,128)(2,1)S(1)}, u32[]{:S(2)}, u32[]{:S(2)}) collective-permute-start(bf16[1024,128]{1,0:T(8,128)(2,1)S(1)} %shard_map.56), channel_id=1, source_target_pairs={{0,2},{1,3},{2,4},{3,5},{4,6},{5,7},{6,8},{7,9},{8,10},{9,11},{10,... | collective-permute-start | bytes 786440 | tf_op jit(solution)/shard_map/ppermute | solution.py:158
  42.6 15.2 %collective-permute-start.18 = (bf16[1024,128]{1,0:T(8,128)(2,1)S(1)}, bf16[1024,128]{1,0:T(8,128)(2,1)S(1)}, u32[]{:S(2)}, u32[]{:S(2)}) collective-permute-start(bf16[1024,128]{1,0:T(8,128)(2,1)S(1)} %get-tuple-element.39), channel_id=1, source_target_pairs={{0,2},{1,3},{2,4},{3,5},{4,6},{5,7},{6,8},{7,9},{8,10},{9,11},{10,... | collective-permute-start | bytes 786440 | tf_op jit(solution)/shard_map/ppermute | solution.py:158
  43.7 14.3 %collective-permute-start.11 = (bf16[1024,128]{1,0:T(8,128)(2,1)S(1)}, bf16[1024,128]{1,0:T(8,128)(2,1)S(1)}, u32[]{:S(2)}, u32[]{:S(2)}) collective-permute-start(bf16[1024,128]{1,0:T(8,128)(2,1)S(1)} %get-tuple-element.41), channel_id=1, source_target_pairs={{0,14},{1,15},{2,0},{3,1},{4,2},{5,3},{6,4},{7,5},{8,6},{9,7},{10,... | collective-permute-start | bytes 786440 | tf_op jit(solution)/shard_map/ppermute | solution.py:158
  49.8 11.6 %collective-permute-start.22 = (bf16[1024,128]{1,0:T(8,128)(2,1)S(1)}, bf16[1024,128]{1,0:T(8,128)(2,1)S(1)}, u32[]{:S(2)}, u32[]{:S(2)}) collective-permute-start(bf16[1024,128]{1,0:T(8,128)(2,1)S(1)} %add_convert_fusion.2), channel_id=1, source_target_pairs={{0,14},{1,15},{2,0},{3,1},{4,2},{5,3},{6,4},{7,5},{8,6},{9,7},{10,... | collective-permute-start | bytes 786440 | tf_op jit(solution)/shard_map/ppermute | solution.py:158
  52.3 11.1 %collective-permute-start.15 = (bf16[1024,128]{1,0:T(8,128)(2,1)S(1)}, bf16[1024,128]{1,0:T(8,128)(2,1)S(1)}, u32[]{:S(2)}, u32[]{:S(2)}) collective-permute-start(bf16[1024,128]{1,0:T(8,128)(2,1)S(1)} %add_convert_fusion.7), channel_id=1, source_target_pairs={{0,2},{1,3},{2,4},{3,5},{4,6},{5,7},{6,8},{7,9},{8,10},{9,11},{10,... | collective-permute-start | bytes 786440 | tf_op jit(solution)/shard_map/ppermute | solution.py:158
  57.9 11.2 %collective-permute-start.19 = (bf16[1024,128]{1,0:T(8,128)(2,1)S(1)}, bf16[1024,128]{1,0:T(8,128)(2,1)S(1)}, u32[]{:S(2)}, u32[]{:S(2)}) collective-permute-start(bf16[1024,128]{1,0:T(8,128)(2,1)S(1)} %add_convert_fusion.4), channel_id=1, source_target_pairs={{0,2},{1,3},{2,4},{3,5},{4,6},{5,7},{6,8},{7,9},{8,10},{9,11},{10,... | collective-permute-start | bytes 786440 | tf_op jit(solution)/shard_map/ppermute | solution.py:158
  58.0 11.2 %collective-permute-start.12 = (bf16[1024,128]{1,0:T(8,128)(2,1)S(1)}, bf16[1024,128]{1,0:T(8,128)(2,1)S(1)}, u32[]{:S(2)}, u32[]{:S(2)}) collective-permute-start(bf16[1024,128]{1,0:T(8,128)(2,1)S(1)} %add_convert_fusion.9), channel_id=1, source_target_pairs={{0,14},{1,15},{2,0},{3,1},{4,2},{5,3},{6,4},{7,5},{8,6},{9,7},{10,... | collective-permute-start | bytes 786440 | tf_op jit(solution)/shard_map/ppermute | solution.py:158
  61.4 11.2 %collective-permute-start.23 = (bf16[1024,128]{1,0:T(8,128)(2,1)S(1)}, bf16[1024,128]{1,0:T(8,128)(2,1)S(1)}, u32[]{:S(2)}, u32[]{:S(2)}) collective-permute-start(bf16[1024,128]{1,0:T(8,128)(2,1)S(1)} %add_convert_fusion.1), channel_id=1, source_target_pairs={{0,14},{1,15},{2,0},{3,1},{4,2},{5,3},{6,4},{7,5},{8,6},{9,7},{10,... | collective-permute-start | bytes 786440 | tf_op jit(solution)/shard_map/ppermute | solution.py:158
  63.5 11.2 %collective-permute-start.16 = (bf16[1024,128]{1,0:T(8,128)(2,1)S(1)}, bf16[1024,128]{1,0:T(8,128)(2,1)S(1)}, u32[]{:S(2)}, u32[]{:S(2)}) collective-permute-start(bf16[1024,128]{1,0:T(8,128)(2,1)S(1)} %add_convert_fusion.6), channel_id=1, source_target_pairs={{0,2},{1,3},{2,4},{3,5},{4,6},{5,7},{6,8},{7,9},{8,10},{9,11},{10,... | collective-permute-start | bytes 786440 | tf_op jit(solution)/shard_map/ppermute | solution.py:158
  69.1 11.2 %collective-permute-start.20 = (bf16[1024,128]{1,0:T(8,128)(2,1)S(1)}, bf16[1024,128]{1,0:T(8,128)(2,1)S(1)}, u32[]{:S(2)}, u32[]{:S(2)}) collective-permute-start(bf16[1024,128]{1,0:T(8,128)(2,1)S(1)} %add_convert_fusion.3), channel_id=1, source_target_pairs={{0,2},{1,3},{2,4},{3,5},{4,6},{5,7},{6,8},{7,9},{8,10},{9,11},{10,... | collective-permute-start | bytes 786440 | tf_op jit(solution)/shard_map/ppermute | solution.py:158
  69.3 11.0 %collective-permute-start.13 = (bf16[1024,128]{1,0:T(8,128)(2,1)S(1)}, bf16[1024,128]{1,0:T(8,128)(2,1)S(1)}, u32[]{:S(2)}, u32[]{:S(2)}) collective-permute-start(bf16[1024,128]{1,0:T(8,128)(2,1)S(1)} %add_convert_fusion.8), channel_id=1, source_target_pairs={{0,14},{1,15},{2,0},{3,1},{4,2},{5,3},{6,4},{7,5},{8,6},{9,7},{10,... | collective-permute-start | bytes 786440 | tf_op jit(solution)/shard_map/ppermute | solution.py:158
  72.6 9.2 %collective-permute-start.24 = (bf16[1024,128]{1,0:T(8,128)(2,1)S(1)}, bf16[1024,128]{1,0:T(8,128)(2,1)S(1)}, u32[]{:S(2)}, u32[]{:S(2)}) collective-permute-start(bf16[1024,128]{1,0:T(8,128)(2,1)S(1)} %add_convert_fusion), channel_id=1, source_target_pairs={{0,14},{1,15},{2,0},{3,1},{4,2},{5,3},{6,4},{7,5},{8,6},{9,7},{10,... | collective-permute-start | bytes 786440 | tf_op jit(solution)/shard_map/ppermute | solution.py:158
  74.7 10.1 %collective-permute-start.17 = (bf16[1024,128]{1,0:T(8,128)(2,1)S(1)}, bf16[1024,128]{1,0:T(8,128)(2,1)S(1)}, u32[]{:S(2)}, u32[]{:S(2)}) collective-permute-start(bf16[1024,128]{1,0:T(8,128)(2,1)S(1)} %add_convert_fusion.5), channel_id=1, source_target_pairs={{0,2},{1,3},{2,4},{3,5},{4,6},{5,7},{6,8},{7,9},{8,10},{9,11},{10,... | collective-permute-start | bytes 786440 | tf_op jit(solution)/shard_map/ppermute | solution.py:158

commit v3 on v2

v3 whole, which is shorter than its diff:
```python
import functools

import jax
import jax.numpy as jnp
from jax import lax
from jax.experimental import pallas as pl
from jax.experimental.pallas import tpu as pltpu
from jax.sharding import PartitionSpec as P

BS = 32
EARLY = (4, 3, 5)
LATE = (2, 6, 1, 7, 0)
COST = 1
VMEM_BYTES = 8 * 1024 * 1024

vmem = functools.partial(pl.BlockSpec, memory_space=pltpu.VMEM)
smem = functools.partial(pl.BlockSpec, memory_space=pltpu.SMEM)


def call(kernel, outs, operands, in_specs, scratch=(), flops=0, moved=0, limit=VMEM_BYTES):
    return pl.pallas_call(
        kernel,
        out_shape=outs,
        in_specs=in_specs,
        out_specs=[vmem()] * len(outs),
        scratch_shapes=list(scratch),
        compiler_params=pltpu.CompilerParams(vmem_limit_bytes=limit),
        cost_estimate=pl.CostEstimate(flops=flops, bytes_accessed=moved, transcendentals=0),
    )(*operands)


def masked(three_center, three_mask, density, density_mask, nu_sizes):
    rows, cols = three_center.shape
    deep, wide = density.shape
    share = 128
    count = wide // (2 * share)
    tiles = cols // BS

    def kernel(three_hbm, mask3_hbm, dens_hbm, maskd_hbm, sizes_hbm, live_ref, cut_ref, swap_ref, *scratch):
        three_ref, mask3_ref, dens_ref, maskd_ref, sizes_ref, held, sems = scratch
        depth = lax.axis_index("depth")
        z, c = depth // 2, depth % 2
        copies = [
            pltpu.make_async_copy(src, dst, sems.at[i])
            for i, (src, dst) in enumerate(
                (
                    (dens_hbm, dens_ref),
                    (maskd_hbm, maskd_ref),
                    (sizes_hbm, sizes_ref),
                    (mask3_hbm, mask3_ref),
                    (three_hbm, three_ref),
                )
            )
        ]
        for copy in copies:
            copy.start()
        for copy in copies[:2]:
            copy.wait()
        lane = lax.broadcasted_iota(jnp.int32, (wide // BS, wide), 1)
        spread = (lane // BS == lax.broadcasted_iota(jnp.int32, lane.shape, 0)).astype(jnp.bfloat16)
        keep = jnp.dot(
            maskd_ref[...].astype(jnp.float32).astype(jnp.bfloat16), spread, preferred_element_type=jnp.float32
        )
        for i in range(deep // BS):
            kept = jnp.broadcast_to(keep[i : i + 1, :], (BS, wide)).astype(jnp.bfloat16)
            held[i * BS : (i + 1) * BS, :] = dens_ref[i * BS : (i + 1) * BS, :] * kept
        at, swap_at = 0, rows
        for shares in (EARLY, LATE):
            for side in (0, 1):
                for j in shares:
                    here = lax.rem(z + j, count) * 2 + (c if side == 0 else 1 - c)
                    piece = held[:, pl.ds(pl.multiple_of(here * share, share), share)]
                    cut_ref[at : at + deep, :] = piece
                    at += deep
                    if side:
                        swap_ref[swap_at : swap_at + deep, :] = piece
                        swap_at += deep
        for copy in copies[2:]:
            copy.wait()
        lane = lax.broadcasted_iota(jnp.int32, (tiles, cols), 1)
        tile = lax.broadcasted_iota(jnp.int32, lane.shape, 0)
        size = jnp.zeros_like(lane)
        for j in range(tiles):
            size = jnp.where(tile == j, sizes_ref[j], size)
        spread = ((lane // BS == tile) & (lane % BS < size)).astype(jnp.bfloat16)
        keep = lax.dot_general(
            mask3_ref[...].astype(jnp.float32).astype(jnp.bfloat16),
            spread,
            (((0,), (0,)), ((), ())),
            preferred_element_type=jnp.float32,
        )
        for g in range(rows // BS):
            kept = jnp.broadcast_to(keep[g : g + 1, :], (BS, cols)).astype(jnp.bfloat16)
            tile_rows = three_ref[g * BS : (g + 1) * BS, :] * kept
            live_ref[g * BS : (g + 1) * BS, :] = tile_rows
            swap_ref[g * BS : (g + 1) * BS, :] = tile_rows

    return call(
        kernel,
        [jax.ShapeDtypeStruct((rows, cols), jnp.bfloat16)]
        + [jax.ShapeDtypeStruct((r, share), jnp.bfloat16) for r in (2 * count * deep, rows + count * deep)],
        (three_center, three_mask.T, density, density_mask, nu_sizes),
        [pl.BlockSpec(memory_space=pltpu.HBM)] * 5,
        [
            pltpu.VMEM((rows, cols), jnp.bfloat16),
            pltpu.VMEM((tiles, rows // BS), jnp.int32),
            pltpu.VMEM((deep, wide), jnp.bfloat16),
            pltpu.VMEM((deep // BS, wide // BS), jnp.int32),
            pltpu.SMEM((tiles,), jnp.int32),
            pltpu.VMEM((deep, wide), jnp.bfloat16),
            pltpu.SemaphoreType.DMA((5,)),
        ],
        limit=56 * 1024 * 1024,
    )


def dots(three, dens, jobs, cost=0):
    deep, share = 128, dens[0][0].shape[1]
    tile = 256
    arrays = []
    for array, _ in (*three, *dens):
        if not any(array is other for other in arrays):
            arrays.append(array)

    def place(array):
        return [array is other for other in arrays].index(True)

    three_at = [(place(array), base) for array, base in three]
    dens_at = [(place(array), rows) for array, rows in dens]
    shares = [j for _, picked, _ in jobs for j in picked]

    def kernel(*refs):
        ins, outs, held = refs[: len(arrays)], list(refs[len(arrays) : -1]), refs[-1]
        across = lax.axis_index("col") - lax.axis_index("row")
        turn = jnp.where(lax.axis_index("depth") % 2 == 0, across, -across) + 4
        for s, (w, rows) in enumerate(dens_at):
            at = pl.multiple_of(lax.rem(s // 2 + turn, 4) * (2 * deep) + s % 2 * deep, deep)
            for n, j in enumerate(shares):
                held[pl.ds(at, deep), n * share : (n + 1) * share] = ins[w][rows[j] : rows[j] + deep, :]
        lo = 0
        for rows, picked, kinds in jobs:
            right = held[:, lo : lo + len(picked) * share]
            lo += len(picked) * share
            for m in range(0, rows, tile):
                left = jnp.concatenate([ins[w][base + m : base + m + tile, :] for w, base in three_at], axis=1)
                total = jnp.dot(left, right, preferred_element_type=jnp.float32)
                for i, kind in enumerate(kinds):
                    outs[i][m : m + tile, :] = total[:, i * share : (i + 1) * share].astype(kind)
            outs = outs[len(kinds) :]

    return call(
        kernel,
        [jax.ShapeDtypeStruct((rows, share), kind) for rows, _, kinds in jobs for kind in kinds],
        arrays,
        [vmem()] * len(arrays),
        [pltpu.VMEM((len(dens) * deep, len(shares) * share), jnp.bfloat16)],
        flops=cost * 2 * len(dens) * deep * share * sum(rows * len(picked) for rows, picked, _ in jobs),
    )


def along_z(block, distance):
    count = lax.axis_size("depth") // 2
    route = [(z * 2 + c, (z + distance) % count * 2 + c) for z in range(count) for c in range(2)]
    return lax.ppermute(block, "depth", route)


def other_core(block):
    return lax.ppermute(block, "depth", [(i, i ^ 1) for i in range(lax.axis_size("depth"))])


def opposed(block, axis, step):
    count, depth = lax.axis_size(axis), lax.axis_size("depth")
    route = [
        (i * depth + d, (i + (step if d % 2 == 0 else -step)) % count * depth + d)
        for i in range(count)
        for d in range(depth)
    ]
    return lax.ppermute(block, (axis, "depth"), route)


def after(block, *earlier):
    return lax.optimization_barrier((block, *earlier))[0]


def on_device(three_center, three_mask, density, density_mask, nu_sizes):
    live, dens, here = masked(three_center, three_mask, density, density_mask, nu_sizes)
    bf16, f32 = jnp.bfloat16, jnp.float32
    n, deep = live.shape[0], 128
    half = n // 2
    e, l = len(EARLY) * deep, len(LATE) * deep

    def for_other(block):
        return [block[e : 2 * e], block[2 * e + l :]]

    a_back, b_back = opposed(live, "row", 1), opposed(dens, "col", 1)
    a_front, b_front = opposed(live, "row", -1), opposed(dens, "col", -1)
    here_other = other_core(here)
    a_far, b_far = opposed(a_back, "row", 1), opposed(b_back, "col", 1)
    back_other = other_core(jnp.concatenate([a_back, *for_other(b_back)]))
    a_front, b_front, here_other = lax.optimization_barrier((a_front, b_front, here_other))
    front_other = other_core(jnp.concatenate([a_front, *for_other(b_front)]))
    far_other = other_core(jnp.concatenate([a_far, *for_other(b_far)]))

    def three(at):
        return [
            (x, at) for x in (live, here_other, a_front, back_other, a_far, far_other, a_back, front_other)
        ]

    def rows(shares, at):
        return {j: at + i * deep for i, j in enumerate(shares)}

    def shares_of(shares, at, other_at):
        return [
            (x, rows(shares, at) if i % 2 == 0 else rows(shares, n + other_at))
            for i, x in enumerate((dens, here_other, b_front, back_other, b_far, far_other, b_back, front_other))
        ]

    three_a, three_b = three(0), three(half)
    dens_e, dens_l = shares_of(EARLY, 0, 0), shares_of(LATE, 2 * e, e)

    def later(pieces, done):
        held = after(pieces[0][0], done)
        return [(held, pieces[0][1])] + pieces[1:]

    def plus(near, arrived):
        return (near + arrived.astype(f32)).astype(bf16)

    (lb4,) = dots(three_b, dens_e, [(half, (4,), (bf16,))], COST)
    lb = along_z(lb4, -1)
    (ra4,) = dots(later(three_a, lb4), dens_e, [(half, (4,), (bf16,))], COST)
    ra = along_z(ra4, 1)
    la3, ra3 = dots(later(three_a, ra4), dens_e, [(half, (5, 3), (bf16, f32))], COST)
    la = along_z(la3, -1)
    rb3, lb3 = dots(later(three_b, la3), dens_e, [(half, (3, 5), (bf16, f32))], COST)
    rb = along_z(rb3, 1)
    sa = plus(ra3, ra)
    sb = plus(lb3, lb)
    ra, lb = along_z(sa, 1), along_z(sb, -1)
    ra2, la2 = dots(later(three_a, sa), dens_l, [(half, (2, 6), (f32, f32))])
    rb2, lb2 = dots(later(three_b, sb), dens_l, [(half, (2, 6), (f32, f32))])
    la, rb = along_z(plus(la2, la), -1), along_z(plus(rb2, rb), 1)
    sa = plus(ra2, ra)
    sb = plus(lb2, lb)
    ra, lb = along_z(sa, 1), along_z(sb, -1)
    ra1, la1 = dots(later(three_a, sa), dens_l, [(half, (1, 7), (f32, f32))])
    rb1, lb1 = dots(later(three_b, sb), dens_l, [(half, (1, 7), (f32, f32))])
    la, rb = along_z(plus(la1, la), -1), along_z(plus(rb1, rb), 1)
    sa = plus(ra1, ra)
    sb = plus(lb1, lb)
    ra, lb = along_z(sa, 1), along_z(sb, -1)
    (enda,) = dots(later(three_a, sa), dens_l, [(half, (0,), (f32,))])
    (endb,) = dots(later(three_b, sb), dens_l, [(half, (0,), (f32,))])
    top = enda + la.astype(f32) + ra.astype(f32)
    bottom = endb + rb.astype(f32) + lb.astype(f32)
    return jnp.concatenate([top.astype(bf16), bottom.astype(bf16)])


def solution(mesh):
    in_specs = (
        P("col", ("row", "depth")),
        P("col", ("row", "depth")),
        P(("col", "depth"), "row"),
        P(("col", "depth"), "row"),
        P(("row", "depth")),
    )
    out_specs = P("col", ("row", "depth"))
    return jax.shard_map(
        on_device, mesh=mesh, in_specs=in_specs, out_specs=out_specs, check_vma=False
    )
```

time: 85.9 us -> 83.9 us (0.977)
  the two profiles are of different devices: /device:TPU:24 before, /device:TPU:8 now
where the time goes in v3:
time: 83.9 us; the launch traced here: 83.8 us
  waiting for transfers between devices  38.1 us (45%)
  starting transfers between devices  33 us (39%)
  Pallas kernels  10.5 us (13%)
  other arithmetic  1.82 us (2%)
    ppermute x14, starting transfers between devices, along_z(): return lax.ppermute(block, 'depth', route)  23.9 us
    ppermute x6, waiting for transfers between devices, opposed(): return lax.ppermute(block, (axis, 'depth'), route)  18 us
    ppermute x14, waiting for transfers between devices, along_z(): return lax.ppermute(block, 'depth', route)  17.9 us
    pallas_call x11, Pallas kernels, call(): pl.pallas_call(kernel, out_shape=outs, in_specs=in_specs, out_specs=[vmem...  10.5 us
    ppermute x6, starting transfers between devices, opposed(): return lax.ppermute(block, (axis, 'depth'), route)  8.3 us
    ppermute x4, waiting for transfers between devices, other_core(): lax.ppermute(block, 'depth', [(i, i ^ 1) for i in range(lax.axis_size('de...  2.26 us
  transfers between devices with their start and end apart: 24, of which 15 were waited for; matrix products, arithmetic and copies ran while one was open for 1% of the time, Pallas kernels for 8%

profile of v3, /device:TPU:8, one launch (start us, length us, event | category | flops | bytes accessed | tf_op | source)
XLA Modules:
  0.0 83.8 jit_solution(13321161757857619463)
XLA Ops:
  0.0 2.7 %shard_map.55 = (bf16[2048,128]{1,0:T(8,128)(2,1)}, bf16[2048,128]{1,0:T(8,128)(2,1)}, bf16[3072,128]{1,0:T(8,128)(2,1)}) custom-call(bf16[2048,128]{1,0:T(8,128)(2,1)} %three_hbm.1, s32[4,64]{1,0:T(4,128)} %bitcast.1, bf16[128,2048]{1,0:T(8,128)(2,1)} %dens_hbm.1, s32[4,64]{1,0:T(4,128)} %maskd_hbm.1, s32[4]{0:T(128)} %sizes_hbm.1), custom_call_target="tpu_custom_call" | custom-call | tf_op jit(solution)/shard_map/pallas_call | solution.py:21
  2.8 1.7 %collective-permute-start.4 = (bf16[2048,128]{1,0:T(8,128)(2,1)}, bf16[2048,128]{1,0:T(8,128)(2,1)S(1)}, u32[]{:S(2)}, u32[]{:S(2)}) collective-permute-start(bf16[2048,128]{1,0:T(8,128)(2,1)} %get-tuple-element.33.refs_8_), channel_id=1, source_target_pairs={{0,16},{1,49},{2,18},{3,51},{4,20},{5,53},{6,22},{7,55},{8,24},{9,... | collective-permute-start | bytes 1572872 | tf_op jit(solution)/shard_map/ppermute | solution.py:178
  4.4 1.5 %collective-permute-start.3 = (bf16[2048,128]{1,0:T(8,128)(2,1)}, bf16[2048,128]{1,0:T(8,128)(2,1)S(1)}, u32[]{:S(2)}, u32[]{:S(2)}) collective-permute-start(bf16[2048,128]{1,0:T(8,128)(2,1)} %get-tuple-element.45.refs_0_), channel_id=1, source_target_pairs={{0,64},{1,193},{2,66},{3,195},{4,68},{5,197},{6,70},{7,199},{8,72}... | collective-permute-start | bytes 1572872 | tf_op jit(solution)/shard_map/ppermute | solution.py:178
  5.9 1.7 %collective-permute-start = (bf16[2048,128]{1,0:T(8,128)(2,1)}, bf16[2048,128]{1,0:T(8,128)(2,1)S(1)}, u32[]{:S(2)}, u32[]{:S(2)}) collective-permute-start(bf16[2048,128]{1,0:T(8,128)(2,1)} %get-tuple-element.45.refs_0_), channel_id=1, source_target_pairs={{0,192},{1,65},{2,194},{3,67},{4,196},{5,69},{6,198},{7,71},{8,200... | collective-permute-start | bytes 1572872 | tf_op jit(solution)/shard_map/ppermute | solution.py:178
  7.6 1.5 %collective-permute-start.1 = (bf16[2048,128]{1,0:T(8,128)(2,1)}, bf16[2048,128]{1,0:T(8,128)(2,1)S(1)}, u32[]{:S(2)}, u32[]{:S(2)}) collective-permute-start(bf16[2048,128]{1,0:T(8,128)(2,1)} %get-tuple-element.33.refs_8_), channel_id=1, source_target_pairs={{0,48},{1,17},{2,50},{3,19},{4,52},{5,21},{6,54},{7,23},{8,56},{9,... | collective-permute-start | bytes 1572872 | tf_op jit(solution)/shard_map/ppermute | solution.py:178
  9.2 5.1 %collective-permute-done.4.refs_11_ = bf16[2048,128]{1,0:T(8,128)(2,1)S(1)} collective-permute-done((bf16[2048,128]{1,0:T(8,128)(2,1)}, bf16[2048,128]{1,0:T(8,128)(2,1)S(1)}, u32[]{:S(2)}, u32[]{:S(2)}) %collective-permute-start.4) | collective-permute-done | bytes 524320 | tf_op jit(solution)/shard_map/ppermute | solution.py:178
  14.3 1.6 %collective-permute-start.7 = (bf16[2048,128]{1,0:T(8,128)(2,1)S(1)}, bf16[2048,128]{1,0:T(8,128)(2,1)S(1)}, u32[]{:S(2)}, u32[]{:S(2)}) collective-permute-start(bf16[2048,128]{1,0:T(8,128)(2,1)S(1)} %collective-permute-done.4.refs_11_), channel_id=1, source_target_pairs={{0,16},{1,49},{2,18},{3,51},{4,20},{5,53},{6,22},{7,55},{8,24},{9,... | collective-permute-start | bytes 1572872 | tf_op jit(solution)/shard_map/ppermute | solution.py:178
  15.9 3.7 %collective-permute-done.3.refs_6_ = bf16[2048,128]{1,0:T(8,128)(2,1)S(1)} collective-permute-done((bf16[2048,128]{1,0:T(8,128)(2,1)}, bf16[2048,128]{1,0:T(8,128)(2,1)S(1)}, u32[]{:S(2)}, u32[]{:S(2)}) %collective-permute-start.3) | collective-permute-done | bytes 524320 | tf_op jit(solution)/shard_map/ppermute | solution.py:178
  19.6 0.3 collective-permute-start.6
  19.9 0.5 collective-permute-start.5
  20.5 0.2 collective-permute-start.9
  20.7 5.4 %collective-permute-done.7.refs_10_ = bf16[2048,128]{1,0:T(8,128)(2,1)S(1)} collective-permute-done((bf16[2048,128]{1,0:T(8,128)(2,1)S(1)}, bf16[2048,128]{1,0:T(8,128)(2,1)S(1)}, u32[]{:S(2)}, u32[]{:S(2)}) %collective-permute-start.7) | collective-permute-done | bytes 524320 | tf_op jit(solution)/shard_map/ppermute | solution.py:178
  26.1 3.8 %collective-permute-done.6.refs_4_ = bf16[2048,128]{1,0:T(8,128)(2,1)S(1)} collective-permute-done((bf16[2048,128]{1,0:T(8,128)(2,1)S(1)}, bf16[2048,128]{1,0:T(8,128)(2,1)S(1)}, u32[]{:S(2)}, u32[]{:S(2)}) %collective-permute-start.6) | collective-permute-done | bytes 524320 | tf_op jit(solution)/shard_map/ppermute | solution.py:178
  30.0 0.1 collective-permute-start.8
  30.2 2.3 %collective-permute-done.8.refs_5_ = bf16[3072,128]{1,0:T(8,128)(2,1)S(1)} collective-permute-done((bf16[3072,128]{1,0:T(8,128)(2,1)S(1)}, bf16[3072,128]{1,0:T(8,128)(2,1)S(1)}, u32[]{:S(2)}, u32[]{:S(2)}) %collective-permute-start.8) | collective-permute-done | bytes 786464 | tf_op jit(solution)/shard_map/ppermute | solution.py:168
  32.4 0.7 shard_map.56
  33.2 5.9 %collective-permute-start.17 = (bf16[1024,128]{1,0:T(8,128)(2,1)S(1)}, bf16[1024,128]{1,0:T(8,128)(2,1)S(1)}, u32[]{:S(2)}, u32[]{:S(2)}) collective-permute-start(bf16[1024,128]{1,0:T(8,128)(2,1)S(1)} %shard_map.56), channel_id=1, source_target_pairs={{0,14},{1,15},{2,0},{3,1},{4,2},{5,3},{6,4},{7,5},{8,6},{9,7},{10,... | collective-permute-start | bytes 786440 | tf_op jit(solution)/shard_map/ppermute | solution.py:164
  39.1 0.7 shard_map.57
  39.8 0.1 collective-permute-start.10
  39.9 0.8 shard_map.58
  40.8 3.5 %collective-permute-start.13 = (bf16[1024,128]{1,0:T(8,128)(2,1)S(1)}, bf16[1024,128]{1,0:T(8,128)(2,1)S(1)}, u32[]{:S(2)}, u32[]{:S(2)}) collective-permute-start(bf16[1024,128]{1,0:T(8,128)(2,1)S(1)} %get-tuple-element.48), channel_id=1, source_target_pairs={{0,14},{1,15},{2,0},{3,1},{4,2},{5,3},{6,4},{7,5},{8,6},{9,7},{10,... | collective-permute-start | bytes 786440 | tf_op jit(solution)/shard_map/ppermute | solution.py:164
  44.2 0.8 shard_map.62
  45.1 0.6 collective-permute-done.17
  45.8 3.8 %collective-permute-start.18 = (bf16[1024,128]{1,0:T(8,128)(2,1)S(1)}, bf16[1024,128]{1,0:T(8,128)(2,1)S(1)}, u32[]{:S(2)}, u32[]{:S(2)}) collective-permute-start(bf16[1024,128]{1,0:T(8,128)(2,1)S(1)} %add_convert_fusion.5), channel_id=1, source_target_pairs={{0,14},{1,15},{2,0},{3,1},{4,2},{5,3},{6,4},{7,5},{8,6},{9,7},{10,... | collective-permute-start | bytes 786440 | tf_op jit(solution)/shard_map/ppermute | solution.py:164
  49.6 0.5 collective-permute-done.10
  50.3 0.8 shard_map.63
  51.1 4.6 %collective-permute-done.20 = bf16[1024,128]{1,0:T(8,128)(2,1)S(1)} collective-permute-done((bf16[1024,128]{1,0:T(8,128)(2,1)S(1)}, bf16[1024,128]{1,0:T(8,128)(2,1)S(1)}, u32[]{:S(2)}, u32[]{:S(2)}) %collective-permute-start.20) | collective-permute-done | bytes 262176 | tf_op jit(solution)/shard_map/ppermute | solution.py:164
  55.9 0.8 shard_map.59
  56.8 3.3 %collective-permute-start.14 = (bf16[1024,128]{1,0:T(8,128)(2,1)S(1)}, bf16[1024,128]{1,0:T(8,128)(2,1)S(1)}, u32[]{:S(2)}, u32[]{:S(2)}) collective-permute-start(bf16[1024,128]{1,0:T(8,128)(2,1)S(1)} %add_convert_fusion.8), channel_id=1, source_target_pairs={{0,14},{1,15},{2,0},{3,1},{4,2},{5,3},{6,4},{7,5},{8,6},{9,7},{10,... | collective-permute-start | bytes 786440 | tf_op jit(solution)/shard_map/ppermute | solution.py:164
  60.1 0.1 collective-permute-start.19
  60.2 1.1 %collective-permute-done.11 = bf16[1024,128]{1,0:T(8,128)(2,1)S(1)} collective-permute-done((bf16[1024,128]{1,0:T(8,128)(2,1)S(1)}, bf16[1024,128]{1,0:T(8,128)(2,1)S(1)}, u32[]{:S(2)}, u32[]{:S(2)}) %collective-permute-start.11) | collective-permute-done | bytes 262176 | tf_op jit(solution)/shard_map/ppermute | solution.py:164
  61.4 1.0 %collective-permute-start.12 = (bf16[1024,128]{1,0:T(8,128)(2,1)S(1)}, bf16[1024,128]{1,0:T(8,128)(2,1)S(1)}, u32[]{:S(2)}, u32[]{:S(2)}) collective-permute-start(bf16[1024,128]{1,0:T(8,128)(2,1)S(1)} %add_convert_fusion.10), channel_id=1, source_target_pairs={{0,2},{1,3},{2,4},{3,5},{4,6},{5,7},{6,8},{7,9},{8,10},{9,11},{10,... | collective-permute-start | bytes 786440 | tf_op jit(solution)/shard_map/ppermute | solution.py:164
  62.4 0.8 shard_map.64
  63.2 3.8 %collective-permute-done.21 = bf16[1024,128]{1,0:T(8,128)(2,1)S(1)} collective-permute-done((bf16[1024,128]{1,0:T(8,128)(2,1)S(1)}, bf16[1024,128]{1,0:T(8,128)(2,1)S(1)}, u32[]{:S(2)}, u32[]{:S(2)}) %collective-permute-start.21) | collective-permute-done | bytes 262176 | tf_op jit(solution)/shard_map/ppermute | solution.py:164
  67.1 0.8 shard_map.60
  67.9 1.5 %collective-permute-done.19 = bf16[1024,128]{1,0:T(8,128)(2,1)S(1)} collective-permute-done((bf16[1024,128]{1,0:T(8,128)(2,1)S(1)}, bf16[1024,128]{1,0:T(8,128)(2,1)S(1)}, u32[]{:S(2)}, u32[]{:S(2)}) %collective-permute-start.19) | collective-permute-done | bytes 262176 | tf_op jit(solution)/shard_map/ppermute | solution.py:164
  69.5 3.8 %collective-permute-start.23 = (bf16[1024,128]{1,0:T(8,128)(2,1)S(1)}, bf16[1024,128]{1,0:T(8,128)(2,1)S(1)}, u32[]{:S(2)}, u32[]{:S(2)}) collective-permute-start(bf16[1024,128]{1,0:T(8,128)(2,1)S(1)} %add_convert_fusion.3), channel_id=1, source_target_pairs={{0,14},{1,15},{2,0},{3,1},{4,2},{5,3},{6,4},{7,5},{8,6},{9,7},{10,... | collective-permute-start | bytes 786440 | tf_op jit(solution)/shard_map/ppermute | solution.py:164
  73.3 0.1 collective-permute-start.15
  73.5 2.1 %collective-permute-start.16 = (bf16[1024,128]{1,0:T(8,128)(2,1)S(1)}, bf16[1024,128]{1,0:T(8,128)(2,1)S(1)}, u32[]{:S(2)}, u32[]{:S(2)}) collective-permute-start(bf16[1024,128]{1,0:T(8,128)(2,1)S(1)} %add_convert_fusion.9), channel_id=1, source_target_pairs={{0,2},{1,3},{2,4},{3,5},{4,6},{5,7},{6,8},{7,9},{8,10},{9,11},{10,... | collective-permute-start | bytes 786440 | tf_op jit(solution)/shard_map/ppermute | solution.py:164
  75.6 0.7 shard_map.65
  76.3 0.7 shard_map.61
  77.1 1.1 %collective-permute-done.22 = bf16[1024,128]{1,0:T(8,128)(2,1)S(1)} collective-permute-done((bf16[1024,128]{1,0:T(8,128)(2,1)S(1)}, bf16[1024,128]{1,0:T(8,128)(2,1)S(1)}, u32[]{:S(2)}, u32[]{:S(2)}) %collective-permute-start.22) | collective-permute-done | bytes 262176 | tf_op jit(solution)/shard_map/ppermute | solution.py:164
  78.2 0.6 collective-permute-done.23
  78.8 0.1 add_convert_fusion
  78.9 2.7 %collective-permute-done.15 = bf16[1024,128]{1,0:T(8,128)(2,1)S(1)} collective-permute-done((bf16[1024,128]{1,0:T(8,128)(2,1)S(1)}, bf16[1024,128]{1,0:T(8,128)(2,1)S(1)}, u32[]{:S(2)}, u32[]{:S(2)}) %collective-permute-start.15) | collective-permute-done | bytes 262176 | tf_op jit(solution)/shard_map/ppermute | solution.py:164
  81.6 1.3 %collective-permute-done.16 = bf16[1024,128]{1,0:T(8,128)(2,1)S(1)} collective-permute-done((bf16[1024,128]{1,0:T(8,128)(2,1)S(1)}, bf16[1024,128]{1,0:T(8,128)(2,1)S(1)}, u32[]{:S(2)}, u32[]{:S(2)}) %collective-permute-start.16) | collective-permute-done | bytes 262176 | tf_op jit(solution)/shard_map/ppermute | solution.py:164
  82.9 0.1 add_convert_fusion.6
  83.0 0.8 pad_maximum_fusion.3
  (37 shorter events, 1.2 us)
Async XLA Ops:
  2.8 11.5 %collective-permute-start.4 = (bf16[2048,128]{1,0:T(8,128)(2,1)}, bf16[2048,128]{1,0:T(8,128)(2,1)S(1)}, u32[]{:S(2)}, u32[]{:S(2)}) collective-permute-start(bf16[2048,128]{1,0:T(8,128)(2,1)} %get-tuple-element.33.refs_8_), channel_id=1, source_target_pairs={{0,16},{1,49},{2,18},{3,51},{4,20},{5,53},{6,22},{7,55},{8,24},{9,... | collective-permute-start | bytes 1572872 | tf_op jit(solution)/shard_map/ppermute | solution.py:178
  4.4 15.2 %collective-permute-start.3 = (bf16[2048,128]{1,0:T(8,128)(2,1)}, bf16[2048,128]{1,0:T(8,128)(2,1)S(1)}, u32[]{:S(2)}, u32[]{:S(2)}) collective-permute-start(bf16[2048,128]{1,0:T(8,128)(2,1)} %get-tuple-element.45.refs_0_), channel_id=1, source_target_pairs={{0,64},{1,193},{2,66},{3,195},{4,68},{5,197},{6,70},{7,199},{8,72}... | collective-permute-start | bytes 1572872 | tf_op jit(solution)/shard_map/ppermute | solution.py:178
  5.9 14.6 %collective-permute-start.2 = (bf16[3072,128]{1,0:T(8,128)(2,1)}, bf16[3072,128]{1,0:T(8,128)(2,1)S(1)}, u32[]{:S(2)}, u32[]{:S(2)}) collective-permute-start(bf16[3072,128]{1,0:T(8,128)(2,1)} %get-tuple-element.34), channel_id=1, source_target_pairs={{0,1},{1,0},{2,3},{3,2},{4,5},{5,4},{6,7},{7,6},{8,9},{9,8},{10,11... | collective-permute-start | bytes 2359304 | tf_op jit(solution)/shard_map/ppermute | solution.py:168
  5.9 14.0 %collective-permute-start = (bf16[2048,128]{1,0:T(8,128)(2,1)}, bf16[2048,128]{1,0:T(8,128)(2,1)S(1)}, u32[]{:S(2)}, u32[]{:S(2)}) collective-permute-start(bf16[2048,128]{1,0:T(8,128)(2,1)} %get-tuple-element.45.refs_0_), channel_id=1, source_target_pairs={{0,192},{1,65},{2,194},{3,67},{4,196},{5,69},{6,198},{7,71},{8,200... | collective-permute-start | bytes 1572872 | tf_op jit(solution)/shard_map/ppermute | solution.py:178
  7.6 12.8 %collective-permute-start.1 = (bf16[2048,128]{1,0:T(8,128)(2,1)}, bf16[2048,128]{1,0:T(8,128)(2,1)S(1)}, u32[]{:S(2)}, u32[]{:S(2)}) collective-permute-start(bf16[2048,128]{1,0:T(8,128)(2,1)} %get-tuple-element.33.refs_8_), channel_id=1, source_target_pairs={{0,48},{1,17},{2,50},{3,19},{4,52},{5,21},{6,54},{7,23},{8,56},{9,... | collective-permute-start | bytes 1572872 | tf_op jit(solution)/shard_map/ppermute | solution.py:178
  14.3 11.8 %collective-permute-start.7 = (bf16[2048,128]{1,0:T(8,128)(2,1)S(1)}, bf16[2048,128]{1,0:T(8,128)(2,1)S(1)}, u32[]{:S(2)}, u32[]{:S(2)}) collective-permute-start(bf16[2048,128]{1,0:T(8,128)(2,1)S(1)} %collective-permute-done.4.refs_11_), channel_id=1, source_target_pairs={{0,16},{1,49},{2,18},{3,51},{4,20},{5,53},{6,22},{7,55},{8,24},{9,... | collective-permute-start | bytes 1572872 | tf_op jit(solution)/shard_map/ppermute | solution.py:178
  19.6 10.4 %collective-permute-start.6 = (bf16[2048,128]{1,0:T(8,128)(2,1)S(1)}, bf16[2048,128]{1,0:T(8,128)(2,1)S(1)}, u32[]{:S(2)}, u32[]{:S(2)}) collective-permute-start(bf16[2048,128]{1,0:T(8,128)(2,1)S(1)} %collective-permute-done.3.refs_6_), channel_id=1, source_target_pairs={{0,64},{1,193},{2,66},{3,195},{4,68},{5,197},{6,70},{7,199},{8,72}... | collective-permute-start | bytes 1572872 | tf_op jit(solution)/shard_map/ppermute | solution.py:178
  19.9 10.2 %collective-permute-start.5 = (bf16[3072,128]{1,0:T(8,128)(2,1)S(1)}, bf16[3072,128]{1,0:T(8,128)(2,1)S(1)}, u32[]{:S(2)}, u32[]{:S(2)}) collective-permute-start(bf16[3072,128]{1,0:T(8,128)(2,1)S(1)} %pad_maximum_fusion), channel_id=1, source_target_pairs={{0,1},{1,0},{2,3},{3,2},{4,5},{5,4},{6,7},{7,6},{8,9},{9,8},{10,11... | collective-permute-start | bytes 2359304 | tf_op jit(solution)/shard_map/ppermute | solution.py:168
  20.5 9.6 %collective-permute-start.9 = (bf16[3072,128]{1,0:T(8,128)(2,1)S(1)}, bf16[3072,128]{1,0:T(8,128)(2,1)S(1)}, u32[]{:S(2)}, u32[]{:S(2)}) collective-permute-start(bf16[3072,128]{1,0:T(8,128)(2,1)S(1)} %pad_maximum_fusion.2), channel_id=1, source_target_pairs={{0,1},{1,0},{2,3},{3,2},{4,5},{5,4},{6,7},{7,6},{8,9},{9,8},{10,11... | collective-permute-start | bytes 2359304 | tf_op jit(solution)/shard_map/ppermute | solution.py:168
  26.1 6.3 %copy-start = (bf16[2048,128]{1,0:T(8,128)(2,1)S(1)}, bf16[2048,128]{1,0:T(8,128)(2,1)}, u32[]{:S(2)}) copy-start(bf16[2048,128]{1,0:T(8,128)(2,1)} %get-tuple-element.45.refs_0_) | copy-start | bytes 1572868
  26.1 6.3 %copy-start.1 = (bf16[2048,128]{1,0:T(8,128)(2,1)S(1)}, bf16[2048,128]{1,0:T(8,128)(2,1)}, u32[]{:S(2)}) copy-start(bf16[2048,128]{1,0:T(8,128)(2,1)} %get-tuple-element.33.refs_8_) | copy-start | bytes 1572868
  30.0 2.4 %collective-permute-start.8 = (bf16[3072,128]{1,0:T(8,128)(2,1)S(1)}, bf16[3072,128]{1,0:T(8,128)(2,1)S(1)}, u32[]{:S(2)}, u32[]{:S(2)}) collective-permute-start(bf16[3072,128]{1,0:T(8,128)(2,1)S(1)} %pad_maximum_fusion.1), channel_id=1, source_target_pairs={{0,1},{1,0},{2,3},{3,2},{4,5},{5,4},{6,7},{7,6},{8,9},{9,8},{10,11... | collective-permute-start | bytes 2359304 | tf_op jit(solution)/shard_map/ppermute | solution.py:168
  33.2 12.6 %collective-permute-start.17 = (bf16[1024,128]{1,0:T(8,128)(2,1)S(1)}, bf16[1024,128]{1,0:T(8,128)(2,1)S(1)}, u32[]{:S(2)}, u32[]{:S(2)}) collective-permute-start(bf16[1024,128]{1,0:T(8,128)(2,1)S(1)} %shard_map.56), channel_id=1, source_target_pairs={{0,14},{1,15},{2,0},{3,1},{4,2},{5,3},{6,4},{7,5},{8,6},{9,7},{10,... | collective-permute-start | bytes 786440 | tf_op jit(solution)/shard_map/ppermute | solution.py:164
  39.8 10.3 %collective-permute-start.10 = (bf16[1024,128]{1,0:T(8,128)(2,1)S(1)}, bf16[1024,128]{1,0:T(8,128)(2,1)S(1)}, u32[]{:S(2)}, u32[]{:S(2)}) collective-permute-start(bf16[1024,128]{1,0:T(8,128)(2,1)S(1)} %shard_map.57), channel_id=1, source_target_pairs={{0,2},{1,3},{2,4},{3,5},{4,6},{5,7},{6,8},{7,9},{8,10},{9,11},{10,... | collective-permute-start | bytes 786440 | tf_op jit(solution)/shard_map/ppermute | solution.py:164
  40.8 15.9 %collective-permute-start.13 = (bf16[1024,128]{1,0:T(8,128)(2,1)S(1)}, bf16[1024,128]{1,0:T(8,128)(2,1)S(1)}, u32[]{:S(2)}, u32[]{:S(2)}) collective-permute-start(bf16[1024,128]{1,0:T(8,128)(2,1)S(1)} %get-tuple-element.48), channel_id=1, source_target_pairs={{0,14},{1,15},{2,0},{3,1},{4,2},{5,3},{6,4},{7,5},{8,6},{9,7},{10,... | collective-permute-start | bytes 786440 | tf_op jit(solution)/shard_map/ppermute | solution.py:164
  45.0 10.7 %collective-permute-start.20 = (bf16[1024,128]{1,0:T(8,128)(2,1)S(1)}, bf16[1024,128]{1,0:T(8,128)(2,1)S(1)}, u32[]{:S(2)}, u32[]{:S(2)}) collective-permute-start(bf16[1024,128]{1,0:T(8,128)(2,1)S(1)} %get-tuple-element.58), channel_id=1, source_target_pairs={{0,2},{1,3},{2,4},{3,5},{4,6},{5,7},{6,8},{7,9},{8,10},{9,11},{10,... | collective-permute-start | bytes 786440 | tf_op jit(solution)/shard_map/ppermute | solution.py:164
  45.8 14.2 %collective-permute-start.18 = (bf16[1024,128]{1,0:T(8,128)(2,1)S(1)}, bf16[1024,128]{1,0:T(8,128)(2,1)S(1)}, u32[]{:S(2)}, u32[]{:S(2)}) collective-permute-start(bf16[1024,128]{1,0:T(8,128)(2,1)S(1)} %add_convert_fusion.5), channel_id=1, source_target_pairs={{0,14},{1,15},{2,0},{3,1},{4,2},{5,3},{6,4},{7,5},{8,6},{9,7},{10,... | collective-permute-start | bytes 786440 | tf_op jit(solution)/shard_map/ppermute | solution.py:164
  50.2 11.2 %collective-permute-start.11 = (bf16[1024,128]{1,0:T(8,128)(2,1)S(1)}, bf16[1024,128]{1,0:T(8,128)(2,1)S(1)}, u32[]{:S(2)}, u32[]{:S(2)}) collective-permute-start(bf16[1024,128]{1,0:T(8,128)(2,1)S(1)} %add_convert_fusion.11), channel_id=1, source_target_pairs={{0,2},{1,3},{2,4},{3,5},{4,6},{5,7},{6,8},{7,9},{8,10},{9,11},{10,... | collective-permute-start | bytes 786440 | tf_op jit(solution)/shard_map/ppermute | solution.py:164
  55.8 11.2 %collective-permute-start.21 = (bf16[1024,128]{1,0:T(8,128)(2,1)S(1)}, bf16[1024,128]{1,0:T(8,128)(2,1)S(1)}, u32[]{:S(2)}, u32[]{:S(2)}) collective-permute-start(bf16[1024,128]{1,0:T(8,128)(2,1)S(1)} %add_convert_fusion.2), channel_id=1, source_target_pairs={{0,2},{1,3},{2,4},{3,5},{4,6},{5,7},{6,8},{7,9},{8,10},{9,11},{10,... | collective-permute-start | bytes 786440 | tf_op jit(solution)/shard_map/ppermute | solution.py:164
  56.8 16.5 %collective-permute-start.14 = (bf16[1024,128]{1,0:T(8,128)(2,1)S(1)}, bf16[1024,128]{1,0:T(8,128)(2,1)S(1)}, u32[]{:S(2)}, u32[]{:S(2)}) collective-permute-start(bf16[1024,128]{1,0:T(8,128)(2,1)S(1)} %add_convert_fusion.8), channel_id=1, source_target_pairs={{0,14},{1,15},{2,0},{3,1},{4,2},{5,3},{6,4},{7,5},{8,6},{9,7},{10,... | collective-permute-start | bytes 786440 | tf_op jit(solution)/shard_map/ppermute | solution.py:164
  60.1 9.3 %collective-permute-start.19 = (bf16[1024,128]{1,0:T(8,128)(2,1)S(1)}, bf16[1024,128]{1,0:T(8,128)(2,1)S(1)}, u32[]{:S(2)}, u32[]{:S(2)}) collective-permute-start(bf16[1024,128]{1,0:T(8,128)(2,1)S(1)} %add_convert_fusion.4), channel_id=1, source_target_pairs={{0,14},{1,15},{2,0},{3,1},{4,2},{5,3},{6,4},{7,5},{8,6},{9,7},{10,... | collective-permute-start | bytes 786440 | tf_op jit(solution)/shard_map/ppermute | solution.py:164
  61.4 12.0 %collective-permute-start.12 = (bf16[1024,128]{1,0:T(8,128)(2,1)S(1)}, bf16[1024,128]{1,0:T(8,128)(2,1)S(1)}, u32[]{:S(2)}, u32[]{:S(2)}) collective-permute-start(bf16[1024,128]{1,0:T(8,128)(2,1)S(1)} %add_convert_fusion.10), channel_id=1, source_target_pairs={{0,2},{1,3},{2,4},{3,5},{4,6},{5,7},{6,8},{7,9},{8,10},{9,11},{10,... | collective-permute-start | bytes 786440 | tf_op jit(solution)/shard_map/ppermute | solution.py:164
  67.0 11.2 %collective-permute-start.22 = (bf16[1024,128]{1,0:T(8,128)(2,1)S(1)}, bf16[1024,128]{1,0:T(8,128)(2,1)S(1)}, u32[]{:S(2)}, u32[]{:S(2)}) collective-permute-start(bf16[1024,128]{1,0:T(8,128)(2,1)S(1)} %add_convert_fusion.1), channel_id=1, source_target_pairs={{0,2},{1,3},{2,4},{3,5},{4,6},{5,7},{6,8},{7,9},{8,10},{9,11},{10,... | collective-permute-start | bytes 786440 | tf_op jit(solution)/shard_map/ppermute | solution.py:164
  69.5 9.4 %collective-permute-start.23 = (bf16[1024,128]{1,0:T(8,128)(2,1)S(1)}, bf16[1024,128]{1,0:T(8,128)(2,1)S(1)}, u32[]{:S(2)}, u32[]{:S(2)}) collective-permute-start(bf16[1024,128]{1,0:T(8,128)(2,1)S(1)} %add_convert_fusion.3), channel_id=1, source_target_pairs={{0,14},{1,15},{2,0},{3,1},{4,2},{5,3},{6,4},{7,5},{8,6},{9,7},{10,... | collective-permute-start | bytes 786440 | tf_op jit(solution)/shard_map/ppermute | solution.py:164
  73.3 8.3 %collective-permute-start.15 = (bf16[1024,128]{1,0:T(8,128)(2,1)S(1)}, bf16[1024,128]{1,0:T(8,128)(2,1)S(1)}, u32[]{:S(2)}, u32[]{:S(2)}) collective-permute-start(bf16[1024,128]{1,0:T(8,128)(2,1)S(1)} %add_convert_fusion.7), channel_id=1, source_target_pairs={{0,14},{1,15},{2,0},{3,1},{4,2},{5,3},{6,4},{7,5},{8,6},{9,7},{10,... | collective-permute-start | bytes 786440 | tf_op jit(solution)/shard_map/ppermute | solution.py:164
  73.5 9.4 %collective-permute-start.16 = (bf16[1024,128]{1,0:T(8,128)(2,1)S(1)}, bf16[1024,128]{1,0:T(8,128)(2,1)S(1)}, u32[]{:S(2)}, u32[]{:S(2)}) collective-permute-start(bf16[1024,128]{1,0:T(8,128)(2,1)S(1)} %add_convert_fusion.9), channel_id=1, source_target_pairs={{0,2},{1,3},{2,4},{3,5},{4,6},{5,7},{6,8},{7,9},{8,10},{9,11},{10,... | collective-permute-start | bytes 786440 | tf_op jit(solution)/shard_map/ppermute | solution.py:164

commit v4 on v3

v4 whole, which is shorter than its diff:
```python
import functools

import jax
import jax.numpy as jnp
from jax import lax
from jax.experimental import pallas as pl
from jax.experimental.pallas import tpu as pltpu
from jax.sharding import PartitionSpec as P

BS = 32
COST = 1
AHEAD = 2 * 10**9
VMEM_BYTES = 8 * 1024 * 1024

vmem = functools.partial(pl.BlockSpec, memory_space=pltpu.VMEM)
smem = functools.partial(pl.BlockSpec, memory_space=pltpu.SMEM)


def call(kernel, outs, operands, in_specs, scratch=(), flops=0, limit=VMEM_BYTES):
    return pl.pallas_call(
        kernel,
        out_shape=outs,
        in_specs=in_specs,
        out_specs=[vmem()] * len(outs),
        scratch_shapes=list(scratch),
        compiler_params=pltpu.CompilerParams(vmem_limit_bytes=limit),
        cost_estimate=pl.CostEstimate(flops=flops, bytes_accessed=0, transcendentals=0),
    )(*operands)


def masked(three_center, three_mask, density, density_mask, nu_sizes):
    rows, cols = three_center.shape
    deep, wide = density.shape
    share = 128
    count = wide // (2 * share)
    tiles = cols // BS

    def kernel(three_hbm, mask3_hbm, dens_hbm, maskd_hbm, sizes_hbm, live_ref, own_ref, other_ref, *scratch):
        three_ref, mask3_ref, dens_ref, maskd_ref, sizes_ref, held, sems = scratch
        depth = lax.axis_index("depth")
        z, c = depth // 2, depth % 2
        copies = [
            pltpu.make_async_copy(src, dst, sems.at[i])
            for i, (src, dst) in enumerate(
                (
                    (dens_hbm, dens_ref),
                    (maskd_hbm, maskd_ref),
                    (sizes_hbm, sizes_ref),
                    (mask3_hbm, mask3_ref),
                    (three_hbm, three_ref),
                )
            )
        ]
        for copy in copies:
            copy.start()
        for copy in copies[:2]:
            copy.wait()
        lane = lax.broadcasted_iota(jnp.int32, (wide // BS, wide), 1)
        spread = (lane // BS == lax.broadcasted_iota(jnp.int32, lane.shape, 0)).astype(jnp.bfloat16)
        keep = jnp.dot(
            maskd_ref[...].astype(jnp.float32).astype(jnp.bfloat16), spread, preferred_element_type=jnp.float32
        )
        for i in range(deep // BS):
            kept = jnp.broadcast_to(keep[i : i + 1, :], (BS, wide)).astype(jnp.bfloat16)
            held[i * BS : (i + 1) * BS, :] = dens_ref[i * BS : (i + 1) * BS, :] * kept
        for j in range(count):
            first = lax.rem(z + j, count) * 2
            for side, out_ref in ((c, own_ref), (1 - c, other_ref)):
                place = pl.multiple_of((first + side) * share, share)
                out_ref[j * deep : (j + 1) * deep, :] = held[:, pl.ds(place, share)]
        for copy in copies[2:]:
            copy.wait()
        lane = lax.broadcasted_iota(jnp.int32, (tiles, cols), 1)
        tile = lax.broadcasted_iota(jnp.int32, lane.shape, 0)
        size = jnp.zeros_like(lane)
        for j in range(tiles):
            size = jnp.where(tile == j, sizes_ref[j], size)
        spread = ((lane // BS == tile) & (lane % BS < size)).astype(jnp.bfloat16)
        keep = lax.dot_general(
            mask3_ref[...].astype(jnp.float32).astype(jnp.bfloat16),
            spread,
            (((0,), (0,)), ((), ())),
            preferred_element_type=jnp.float32,
        )
        for g in range(rows // BS):
            kept = jnp.broadcast_to(keep[g : g + 1, :], (BS, cols)).astype(jnp.bfloat16)
            live_ref[g * BS : (g + 1) * BS, :] = three_ref[g * BS : (g + 1) * BS, :] * kept

    return call(
        kernel,
        [jax.ShapeDtypeStruct((rows, cols), jnp.bfloat16)]
        + [jax.ShapeDtypeStruct((r, share), jnp.bfloat16) for r in (count * deep, count * deep)],
        (three_center, three_mask.T, density, density_mask, nu_sizes),
        [pl.BlockSpec(memory_space=pltpu.HBM)] * 5,
        [
            pltpu.VMEM((rows, cols), jnp.bfloat16),
            pltpu.VMEM((tiles, rows // BS), jnp.int32),
            pltpu.VMEM((deep, wide), jnp.bfloat16),
            pltpu.VMEM((deep // BS, wide // BS), jnp.int32),
            pltpu.SMEM((tiles,), jnp.int32),
            pltpu.VMEM((deep, wide), jnp.bfloat16),
            pltpu.SemaphoreType.DMA((5,)),
        ],
        limit=56 * 1024 * 1024,
    )


def in_order(blocks):
    deep, share = 128, blocks[0].shape[1]
    both = blocks[0].shape[0] // 2
    whole = 2 * len(blocks) * deep

    def kernel(*refs):
        out = refs[-1]
        across = lax.axis_index("col") - lax.axis_index("row")
        turn = jnp.where(lax.axis_index("depth") % 2 == 0, across, -across) + 4
        for s, block in enumerate(refs[:-1]):
            at = pl.multiple_of(lax.rem(s + turn, 4) * (2 * deep), 2 * deep)
            for j in range(both // deep):
                for side in range(2):
                    piece = block[side * both + j * deep : side * both + (j + 1) * deep, :]
                    out[pl.ds(j * whole + side * deep + at, deep), :] = piece

    return call(
        kernel,
        [jax.ShapeDtypeStruct((both // deep * whole, share), blocks[0].dtype)],
        blocks,
        [vmem()] * len(blocks),
        flops=AHEAD,
    )[0]


def dots(three, dens, jobs, cost=0):
    deep, share = 8 * 128, dens.shape[1]
    tile = 256
    arrays = []
    for array, _ in three:
        if not any(array is other for other in arrays):
            arrays.append(array)
    three_at = [([array is other for other in arrays].index(True), base) for array, base in three]

    def kernel(*refs):
        ins, dens_ref, outs = refs[: len(arrays)], refs[len(arrays)], list(refs[len(arrays) + 1 :])
        for rows, picked, kinds in jobs:
            right = jnp.concatenate([dens_ref[j * deep : (j + 1) * deep, :] for j in picked], axis=1)
            for m in range(0, rows, tile):
                left = jnp.concatenate([ins[w][base + m : base + m + tile, :] for w, base in three_at], axis=1)
                total = jnp.dot(left, right, preferred_element_type=jnp.float32)
                for i, kind in enumerate(kinds):
                    outs[i][m : m + tile, :] = total[:, i * share : (i + 1) * share].astype(kind)
            outs = outs[len(kinds) :]

    return call(
        kernel,
        [jax.ShapeDtypeStruct((rows, share), kind) for rows, _, kinds in jobs for kind in kinds],
        (*arrays, dens),
        [vmem()] * (len(arrays) + 1),
        flops=cost * 2 * deep * share * sum(rows * len(picked) for rows, picked, _ in jobs),
    )


def along_z(block, distance):
    count = lax.axis_size("depth") // 2
    route = [(z * 2 + c, (z + distance) % count * 2 + c) for z in range(count) for c in range(2)]
    return lax.ppermute(block, "depth", route)


def other_core(block):
    return lax.ppermute(block, "depth", [(i, i ^ 1) for i in range(lax.axis_size("depth"))])


def opposed(block, axis, step):
    count, depth = lax.axis_size(axis), lax.axis_size("depth")
    route = [
        (i * depth + d, (i + (step if d % 2 == 0 else -step)) % count * depth + d)
        for i in range(count)
        for d in range(depth)
    ]
    return lax.ppermute(block, (axis, "depth"), route)


def after(block, *earlier):
    return lax.optimization_barrier((block, *earlier))[0]


def on_device(three_center, three_mask, density, density_mask, nu_sizes):
    live, own, other = masked(three_center, three_mask, density, density_mask, nu_sizes)
    bf16, f32 = jnp.bfloat16, jnp.float32
    n, deep = live.shape[0], 128
    half, both = n // 2, own.shape[0]

    a_back = opposed(live, "row", 1)
    dens = jnp.concatenate([own, other_core(other)])
    b_back = opposed(dens, "col", 1)
    a_front, b_front = opposed(live, "row", -1), opposed(dens, "col", -1)
    live_other = other_core(live)
    a_far, b_far = opposed(a_back, "row", 1), opposed(b_back, "col", 1)
    back_other = other_core(a_back)
    a_front, b_front, live_other = lax.optimization_barrier((a_front, b_front, live_other))
    front_other = other_core(a_front)
    far_other = other_core(a_far)

    def three(at):
        return [
            (x, at) for x in (live, live_other, a_front, back_other, a_far, far_other, a_back, front_other)
        ]

    three_a, three_b = three(0), three(half)
    dens = in_order((dens, b_front, b_far, b_back))

    def later(pieces, done):
        held = after(pieces[0][0], done)
        return [(held, pieces[0][1])] + pieces[1:]

    def plus(near, arrived):
        return (near + arrived.astype(f32)).astype(bf16)

    (lb4,) = dots(three_b, dens, [(half, (4,), (bf16,))], COST)
    lb = along_z(lb4, -1)
    (ra4,) = dots(later(three_a, lb4), dens, [(half, (4,), (bf16,))], COST)
    ra = along_z(ra4, 1)
    la3, ra3 = dots(later(three_a, ra4), dens, [(half, (5, 3), (bf16, f32))], COST)
    la = along_z(la3, -1)
    rb3, lb3 = dots(later(three_b, la3), dens, [(half, (3, 5), (bf16, f32))], COST)
    rb = along_z(rb3, 1)
    sa = plus(ra3, ra)
    sb = plus(lb3, lb)
    ra, lb = along_z(sa, 1), along_z(sb, -1)
    ra2, la2 = dots(later(three_a, sa), dens, [(half, (2, 6), (f32, f32))])
    rb2, lb2 = dots(later(three_b, sb), dens, [(half, (2, 6), (f32, f32))])
    la, rb = along_z(plus(la2, la), -1), along_z(plus(rb2, rb), 1)
    sa = plus(ra2, ra)
    sb = plus(lb2, lb)
    ra, lb = along_z(sa, 1), along_z(sb, -1)
    ra1, la1 = dots(later(three_a, sa), dens, [(half, (1, 7), (f32, f32))])
    rb1, lb1 = dots(later(three_b, sb), dens, [(half, (1, 7), (f32, f32))])
    la, rb = along_z(plus(la1, la), -1), along_z(plus(rb1, rb), 1)
    sa = plus(ra1, ra)
    sb = plus(lb1, lb)
    ra, lb = along_z(sa, 1), along_z(sb, -1)
    (enda,) = dots(later(three_a, sa), dens, [(half, (0,), (f32,))])
    (endb,) = dots(later(three_b, sb), dens, [(half, (0,), (f32,))])
    top = enda + la.astype(f32) + ra.astype(f32)
    bottom = endb + rb.astype(f32) + lb.astype(f32)
    return jnp.concatenate([top.astype(bf16), bottom.astype(bf16)])


def solution(mesh):
    in_specs = (
        P("col", ("row", "depth")),
        P("col", ("row", "depth")),
        P(("col", "depth"), "row"),
        P(("col", "depth"), "row"),
        P(("row", "depth")),
    )
    out_specs = P("col", ("row", "depth"))
    return jax.shard_map(
        on_device, mesh=mesh, in_specs=in_specs, out_specs=out_specs, check_vma=False
    )
```

time: 83.9 us -> 80.5 us (0.959)
  the two profiles are of different devices: /device:TPU:8 before, /device:TPU:24 now
where the time goes in v4:
time: 80.5 us; the launch traced here: 80.1 us
  waiting for transfers between devices  35.4 us (44%)
  starting transfers between devices  32.2 us (40%)
  Pallas kernels  9.61 us (12%)
  other arithmetic  1.64 us (2%)
  local copies, waits for them, and re-layouts  1.01 us (1%)
    ppermute x14, starting transfers between devices, along_z(): return lax.ppermute(block, 'depth', route)  24 us
    ppermute x14, waiting for transfers between devices, along_z(): return lax.ppermute(block, 'depth', route)  18.9 us
    ppermute x6, waiting for transfers between devices, opposed(): return lax.ppermute(block, (axis, 'depth'), route)  16.5 us
    pallas_call x12, Pallas kernels, call(): pl.pallas_call(kernel, out_shape=outs, in_specs=in_specs, out_specs=[vmem...  9.61 us
    ppermute x6, starting transfers between devices, opposed(): return lax.ppermute(block, (axis, 'depth'), route)  7.35 us
  transfers between devices with their start and end apart: 25, of which 15 were waited for; matrix products, arithmetic and copies ran while one was open for 2% of the time, Pallas kernels for 8%

profile of v4, /device:TPU:24, one launch (start us, length us, event | category | flops | bytes accessed | tf_op | source)
XLA Modules:
  0.0 80.1 jit_solution(3328438495319331897)
XLA Ops:
  0.0 2.5 %shard_map.55 = (bf16[2048,128]{1,0:T(8,128)(2,1)}, bf16[1024,128]{1,0:T(8,128)(2,1)}, bf16[1024,128]{1,0:T(8,128)(2,1)}) custom-call(bf16[2048,128]{1,0:T(8,128)(2,1)} %three_hbm.1, s32[4,64]{1,0:T(4,128)} %bitcast.1, bf16[128,2048]{1,0:T(8,128)(2,1)} %dens_hbm.1, s32[4,64]{1,0:T(4,128)} %maskd_hbm.1, s32[4]{0:T(128)} %sizes_hbm.1), custom_call_target="tpu_custom_call" | custom-call | tf_op jit(solution)/shard_map/pallas_call | solution.py:20
  2.5 0.1 collective-permute-start.1
  2.6 1.6 %collective-permute-start.4 = (bf16[2048,128]{1,0:T(8,128)(2,1)}, bf16[2048,128]{1,0:T(8,128)(2,1)S(1)}, u32[]{:S(2)}, u32[]{:S(2)}) collective-permute-start(bf16[2048,128]{1,0:T(8,128)(2,1)} %get-tuple-element.45.refs_0_), channel_id=1, source_target_pairs={{0,64},{1,193},{2,66},{3,195},{4,68},{5,197},{6,70},{7,199},{8,72}... | collective-permute-start | bytes 1572872 | tf_op jit(solution)/shard_map/ppermute | solution.py:179
  4.1 1.0 %constant_dynamic-update-slice_fusion.1 = bf16[2048,128]{1,0:T(8,128)(2,1)S(1)} fusion(bf16[1024,128]{1,0:T(8,128)(2,1)} %get-tuple-element.33), kind=kLoop, calls=%fused_computation.14 | loop fusion | bytes 524288
  5.2 1.2 %collective-permute-start.9 = (bf16[2048,128]{1,0:T(8,128)(2,1)S(1)}, bf16[2048,128]{1,0:T(8,128)(2,1)S(1)}, u32[]{:S(2)}, u32[]{:S(2)}) collective-permute-start(bf16[2048,128]{1,0:T(8,128)(2,1)S(1)} %constant_dynamic-update-slice_fusion.refs_0_), channel_id=1, source_target_pairs={{0,16},{1,49},{2,18},{3,51},{4,20},{5,53},{6,22},{7,55},{8,24},{9,... | collective-permute-start | bytes 1572872 | tf_op jit(solution)/shard_map/ppermute | solution.py:179
  6.4 0.7 collective-permute-start.3
  7.1 1.8 %collective-permute-start = (bf16[2048,128]{1,0:T(8,128)(2,1)}, bf16[2048,128]{1,0:T(8,128)(2,1)S(1)}, u32[]{:S(2)}, u32[]{:S(2)}) collective-permute-start(bf16[2048,128]{1,0:T(8,128)(2,1)} %get-tuple-element.45.refs_0_), channel_id=1, source_target_pairs={{0,192},{1,65},{2,194},{3,67},{4,196},{5,69},{6,198},{7,71},{8,200... | collective-permute-start | bytes 1572872 | tf_op jit(solution)/shard_map/ppermute | solution.py:179
  9.0 0.3 collective-permute-start.2
  9.2 6.1 %collective-permute-done.4.refs_6_ = bf16[2048,128]{1,0:T(8,128)(2,1)S(1)} collective-permute-done((bf16[2048,128]{1,0:T(8,128)(2,1)}, bf16[2048,128]{1,0:T(8,128)(2,1)S(1)}, u32[]{:S(2)}, u32[]{:S(2)}) %collective-permute-start.4) | collective-permute-done | bytes 524320 | tf_op jit(solution)/shard_map/ppermute | solution.py:179
  15.3 1.4 %collective-permute-start.6 = (bf16[2048,128]{1,0:T(8,128)(2,1)S(1)}, bf16[2048,128]{1,0:T(8,128)(2,1)S(1)}, u32[]{:S(2)}, u32[]{:S(2)}) collective-permute-start(bf16[2048,128]{1,0:T(8,128)(2,1)S(1)} %collective-permute-done.4.refs_6_), channel_id=1, source_target_pairs={{0,64},{1,193},{2,66},{3,195},{4,68},{5,197},{6,70},{7,199},{8,72}... | collective-permute-start | bytes 1572872 | tf_op jit(solution)/shard_map/ppermute | solution.py:179
  16.7 2.3 %collective-permute-done.9.refs_3_ = bf16[2048,128]{1,0:T(8,128)(2,1)S(1)} collective-permute-done((bf16[2048,128]{1,0:T(8,128)(2,1)S(1)}, bf16[2048,128]{1,0:T(8,128)(2,1)S(1)}, u32[]{:S(2)}, u32[]{:S(2)}) %collective-permute-start.9) | collective-permute-done | bytes 524320 | tf_op jit(solution)/shard_map/ppermute | solution.py:179
  19.0 1.1 %collective-permute-start.10 = (bf16[2048,128]{1,0:T(8,128)(2,1)S(1)}, bf16[2048,128]{1,0:T(8,128)(2,1)S(1)}, u32[]{:S(2)}, u32[]{:S(2)}) collective-permute-start(bf16[2048,128]{1,0:T(8,128)(2,1)S(1)} %collective-permute-done.9.refs_3_), channel_id=1, source_target_pairs={{0,16},{1,49},{2,18},{3,51},{4,20},{5,53},{6,22},{7,55},{8,24},{9,... | collective-permute-start | bytes 1572872 | tf_op jit(solution)/shard_map/ppermute | solution.py:179
  20.1 1.6 %collective-permute-done.2.refs_1_ = bf16[2048,128]{1,0:T(8,128)(2,1)S(1)} collective-permute-done((bf16[2048,128]{1,0:T(8,128)(2,1)S(1)}, bf16[2048,128]{1,0:T(8,128)(2,1)S(1)}, u32[]{:S(2)}, u32[]{:S(2)}) %collective-permute-start.2) | collective-permute-done | bytes 524320 | tf_op jit(solution)/shard_map/ppermute | solution.py:179
  21.7 4.0 %collective-permute-done.6.refs_4_ = bf16[2048,128]{1,0:T(8,128)(2,1)S(1)} collective-permute-done((bf16[2048,128]{1,0:T(8,128)(2,1)S(1)}, bf16[2048,128]{1,0:T(8,128)(2,1)S(1)}, u32[]{:S(2)}, u32[]{:S(2)}) %collective-permute-start.6) | collective-permute-done | bytes 524320 | tf_op jit(solution)/shard_map/ppermute | solution.py:179
  25.7 2.5 %collective-permute-done.10.refs_2_ = bf16[2048,128]{1,0:T(8,128)(2,1)S(1)} collective-permute-done((bf16[2048,128]{1,0:T(8,128)(2,1)S(1)}, bf16[2048,128]{1,0:T(8,128)(2,1)S(1)}, u32[]{:S(2)}, u32[]{:S(2)}) %collective-permute-start.10) | collective-permute-done | bytes 524320 | tf_op jit(solution)/shard_map/ppermute | solution.py:179
  28.2 0.2 shard_map.56.refs_8_
  28.4 0.7 shard_map.57
  29.1 5.9 %collective-permute-start.18 = (bf16[1024,128]{1,0:T(8,128)(2,1)S(1)}, bf16[1024,128]{1,0:T(8,128)(2,1)S(1)}, u32[]{:S(2)}, u32[]{:S(2)}) collective-permute-start(bf16[1024,128]{1,0:T(8,128)(2,1)S(1)} %shard_map.57), channel_id=1, source_target_pairs={{0,14},{1,15},{2,0},{3,1},{4,2},{5,3},{6,4},{7,5},{8,6},{9,7},{10,... | collective-permute-start | bytes 786440 | tf_op jit(solution)/shard_map/ppermute | solution.py:165
  35.0 0.7 shard_map.58
  35.8 0.7 shard_map.59
  36.5 3.5 %collective-permute-start.14 = (bf16[1024,128]{1,0:T(8,128)(2,1)S(1)}, bf16[1024,128]{1,0:T(8,128)(2,1)S(1)}, u32[]{:S(2)}, u32[]{:S(2)}) collective-permute-start(bf16[1024,128]{1,0:T(8,128)(2,1)S(1)} %get-tuple-element.48), channel_id=1, source_target_pairs={{0,14},{1,15},{2,0},{3,1},{4,2},{5,3},{6,4},{7,5},{8,6},{9,7},{10,... | collective-permute-start | bytes 786440 | tf_op jit(solution)/shard_map/ppermute | solution.py:165
  40.0 0.7 shard_map.63
  40.8 0.8 %collective-permute-done.18 = bf16[1024,128]{1,0:T(8,128)(2,1)S(1)} collective-permute-done((bf16[1024,128]{1,0:T(8,128)(2,1)S(1)}, bf16[1024,128]{1,0:T(8,128)(2,1)S(1)}, u32[]{:S(2)}, u32[]{:S(2)}) %collective-permute-start.18) | collective-permute-done | bytes 262176 | tf_op jit(solution)/shard_map/ppermute | solution.py:165
  41.7 3.8 %collective-permute-start.19 = (bf16[1024,128]{1,0:T(8,128)(2,1)S(1)}, bf16[1024,128]{1,0:T(8,128)(2,1)S(1)}, u32[]{:S(2)}, u32[]{:S(2)}) collective-permute-start(bf16[1024,128]{1,0:T(8,128)(2,1)S(1)} %add_convert_fusion.5), channel_id=1, source_target_pairs={{0,14},{1,15},{2,0},{3,1},{4,2},{5,3},{6,4},{7,5},{8,6},{9,7},{10,... | collective-permute-start | bytes 786440 | tf_op jit(solution)/shard_map/ppermute | solution.py:165
  45.5 0.7 collective-permute-done.11
  46.3 0.7 shard_map.64
  47.0 4.7 %collective-permute-done.21 = bf16[1024,128]{1,0:T(8,128)(2,1)S(1)} collective-permute-done((bf16[1024,128]{1,0:T(8,128)(2,1)S(1)}, bf16[1024,128]{1,0:T(8,128)(2,1)S(1)}, u32[]{:S(2)}, u32[]{:S(2)}) %collective-permute-start.21) | collective-permute-done | bytes 262176 | tf_op jit(solution)/shard_map/ppermute | solution.py:165
  51.9 0.7 shard_map.60
  52.7 3.3 %collective-permute-start.15 = (bf16[1024,128]{1,0:T(8,128)(2,1)S(1)}, bf16[1024,128]{1,0:T(8,128)(2,1)S(1)}, u32[]{:S(2)}, u32[]{:S(2)}) collective-permute-start(bf16[1024,128]{1,0:T(8,128)(2,1)S(1)} %add_convert_fusion.8), channel_id=1, source_target_pairs={{0,14},{1,15},{2,0},{3,1},{4,2},{5,3},{6,4},{7,5},{8,6},{9,7},{10,... | collective-permute-start | bytes 786440 | tf_op jit(solution)/shard_map/ppermute | solution.py:165
  56.1 0.3 collective-permute-start.20
  56.4 1.0 %collective-permute-done.12 = bf16[1024,128]{1,0:T(8,128)(2,1)S(1)} collective-permute-done((bf16[1024,128]{1,0:T(8,128)(2,1)S(1)}, bf16[1024,128]{1,0:T(8,128)(2,1)S(1)}, u32[]{:S(2)}, u32[]{:S(2)}) %collective-permute-start.12) | collective-permute-done | bytes 262176 | tf_op jit(solution)/shard_map/ppermute | solution.py:165
  57.5 0.9 %collective-permute-start.13 = (bf16[1024,128]{1,0:T(8,128)(2,1)S(1)}, bf16[1024,128]{1,0:T(8,128)(2,1)S(1)}, u32[]{:S(2)}, u32[]{:S(2)}) collective-permute-start(bf16[1024,128]{1,0:T(8,128)(2,1)S(1)} %add_convert_fusion.10), channel_id=1, source_target_pairs={{0,2},{1,3},{2,4},{3,5},{4,6},{5,7},{6,8},{7,9},{8,10},{9,11},{10,... | collective-permute-start | bytes 786440 | tf_op jit(solution)/shard_map/ppermute | solution.py:165
  58.3 0.7 shard_map.65
  59.0 4.0 %collective-permute-done.22 = bf16[1024,128]{1,0:T(8,128)(2,1)S(1)} collective-permute-done((bf16[1024,128]{1,0:T(8,128)(2,1)S(1)}, bf16[1024,128]{1,0:T(8,128)(2,1)S(1)}, u32[]{:S(2)}, u32[]{:S(2)}) %collective-permute-start.22) | collective-permute-done | bytes 262176 | tf_op jit(solution)/shard_map/ppermute | solution.py:165
  63.2 0.7 shard_map.61
  63.9 2.0 %collective-permute-done.20 = bf16[1024,128]{1,0:T(8,128)(2,1)S(1)} collective-permute-done((bf16[1024,128]{1,0:T(8,128)(2,1)S(1)}, bf16[1024,128]{1,0:T(8,128)(2,1)S(1)}, u32[]{:S(2)}, u32[]{:S(2)}) %collective-permute-start.20) | collective-permute-done | bytes 262176 | tf_op jit(solution)/shard_map/ppermute | solution.py:165
  65.9 3.8 %collective-permute-start.24 = (bf16[1024,128]{1,0:T(8,128)(2,1)S(1)}, bf16[1024,128]{1,0:T(8,128)(2,1)S(1)}, u32[]{:S(2)}, u32[]{:S(2)}) collective-permute-start(bf16[1024,128]{1,0:T(8,128)(2,1)S(1)} %add_convert_fusion.3), channel_id=1, source_target_pairs={{0,14},{1,15},{2,0},{3,1},{4,2},{5,3},{6,4},{7,5},{8,6},{9,7},{10,... | collective-permute-start | bytes 786440 | tf_op jit(solution)/shard_map/ppermute | solution.py:165
  69.7 0.1 collective-permute-start.16
  69.9 2.1 %collective-permute-start.17 = (bf16[1024,128]{1,0:T(8,128)(2,1)S(1)}, bf16[1024,128]{1,0:T(8,128)(2,1)S(1)}, u32[]{:S(2)}, u32[]{:S(2)}) collective-permute-start(bf16[1024,128]{1,0:T(8,128)(2,1)S(1)} %add_convert_fusion.9), channel_id=1, source_target_pairs={{0,2},{1,3},{2,4},{3,5},{4,6},{5,7},{6,8},{7,9},{8,10},{9,11},{10,... | collective-permute-start | bytes 786440 | tf_op jit(solution)/shard_map/ppermute | solution.py:165
  72.0 0.7 shard_map.66
  72.7 0.7 shard_map.62
  73.4 0.9 %collective-permute-done.23 = bf16[1024,128]{1,0:T(8,128)(2,1)S(1)} collective-permute-done((bf16[1024,128]{1,0:T(8,128)(2,1)S(1)}, bf16[1024,128]{1,0:T(8,128)(2,1)S(1)}, u32[]{:S(2)}, u32[]{:S(2)}) %collective-permute-start.23) | collective-permute-done | bytes 262176 | tf_op jit(solution)/shard_map/ppermute | solution.py:165
  74.3 1.5 %collective-permute-done.24 = bf16[1024,128]{1,0:T(8,128)(2,1)S(1)} collective-permute-done((bf16[1024,128]{1,0:T(8,128)(2,1)S(1)}, bf16[1024,128]{1,0:T(8,128)(2,1)S(1)}, u32[]{:S(2)}, u32[]{:S(2)}) %collective-permute-start.24) | collective-permute-done | bytes 262176 | tf_op jit(solution)/shard_map/ppermute | solution.py:165
  75.8 0.1 add_convert_fusion
  75.9 2.7 %collective-permute-done.16 = bf16[1024,128]{1,0:T(8,128)(2,1)S(1)} collective-permute-done((bf16[1024,128]{1,0:T(8,128)(2,1)S(1)}, bf16[1024,128]{1,0:T(8,128)(2,1)S(1)}, u32[]{:S(2)}, u32[]{:S(2)}) %collective-permute-start.16) | collective-permute-done | bytes 262176 | tf_op jit(solution)/shard_map/ppermute | solution.py:165
  78.6 0.6 collective-permute-done.17
  79.2 0.1 add_convert_fusion.6
  79.3 0.8 %pad_maximum_fusion = bf16[2048,128]{1,0:T(8,128)(2,1)} fusion(bf16[1024,128]{1,0:T(8,128)(2,1)S(1)} %add_convert_fusion, bf16[1024,128]{1,0:T(8,128)(2,1)S(1)} %add_convert_fusion.6), kind=kLoop, calls=%fused_computation | loop fusion | flops 1048576 | bytes 1048576 | tf_op jit(solution)/shard_map/concatenate | solution.py:245
  (31 shorter events, 1.1 us)
Async XLA Ops:
  2.5 2.6 %collective-permute-start.1 = (bf16[1024,128]{1,0:T(8,128)(2,1)}, bf16[1024,128]{1,0:T(8,128)(2,1)S(1)}, u32[]{:S(2)}, u32[]{:S(2)}) collective-permute-start(bf16[1024,128]{1,0:T(8,128)(2,1)} %get-tuple-element.34), channel_id=1, source_target_pairs={{0,1},{1,0},{2,3},{3,2},{4,5},{5,4},{6,7},{7,6},{8,9},{9,8},{10,11... | collective-permute-start | bytes 786440 | tf_op jit(solution)/shard_map/ppermute | solution.py:169
  2.6 12.7 %collective-permute-start.4 = (bf16[2048,128]{1,0:T(8,128)(2,1)}, bf16[2048,128]{1,0:T(8,128)(2,1)S(1)}, u32[]{:S(2)}, u32[]{:S(2)}) collective-permute-start(bf16[2048,128]{1,0:T(8,128)(2,1)} %get-tuple-element.45.refs_0_), channel_id=1, source_target_pairs={{0,64},{1,193},{2,66},{3,195},{4,68},{5,197},{6,70},{7,199},{8,72}... | collective-permute-start | bytes 1572872 | tf_op jit(solution)/shard_map/ppermute | solution.py:179
  5.2 23.2 %copy-start = (bf16[2048,128]{1,0:T(8,128)(2,1)S(1)}, bf16[2048,128]{1,0:T(8,128)(2,1)}, u32[]{:S(2)}) copy-start(bf16[2048,128]{1,0:T(8,128)(2,1)} %get-tuple-element.45.refs_0_) | copy-start | bytes 1572868
  5.2 13.8 %collective-permute-start.9 = (bf16[2048,128]{1,0:T(8,128)(2,1)S(1)}, bf16[2048,128]{1,0:T(8,128)(2,1)S(1)}, u32[]{:S(2)}, u32[]{:S(2)}) collective-permute-start(bf16[2048,128]{1,0:T(8,128)(2,1)S(1)} %constant_dynamic-update-slice_fusion.refs_0_), channel_id=1, source_target_pairs={{0,16},{1,49},{2,18},{3,51},{4,20},{5,53},{6,22},{7,55},{8,24},{9,... | collective-permute-start | bytes 1572872 | tf_op jit(solution)/shard_map/ppermute | solution.py:179
  6.4 13.7 %collective-permute-start.3 = (bf16[2048,128]{1,0:T(8,128)(2,1)}, bf16[2048,128]{1,0:T(8,128)(2,1)S(1)}, u32[]{:S(2)}, u32[]{:S(2)}) collective-permute-start(bf16[2048,128]{1,0:T(8,128)(2,1)} %get-tuple-element.45.refs_0_), channel_id=1, source_target_pairs={{0,1},{1,0},{2,3},{3,2},{4,5},{5,4},{6,7},{7,6},{8,9},{9,8},{10,11... | collective-permute-start | bytes 1572872 | tf_op jit(solution)/shard_map/ppermute | solution.py:169
  7.1 13.0 %collective-permute-start = (bf16[2048,128]{1,0:T(8,128)(2,1)}, bf16[2048,128]{1,0:T(8,128)(2,1)S(1)}, u32[]{:S(2)}, u32[]{:S(2)}) collective-permute-start(bf16[2048,128]{1,0:T(8,128)(2,1)} %get-tuple-element.45.refs_0_), channel_id=1, source_target_pairs={{0,192},{1,65},{2,194},{3,67},{4,196},{5,69},{6,198},{7,71},{8,200... | collective-permute-start | bytes 1572872 | tf_op jit(solution)/shard_map/ppermute | solution.py:179
  9.0 12.7 %collective-permute-start.2 = (bf16[2048,128]{1,0:T(8,128)(2,1)S(1)}, bf16[2048,128]{1,0:T(8,128)(2,1)S(1)}, u32[]{:S(2)}, u32[]{:S(2)}) collective-permute-start(bf16[2048,128]{1,0:T(8,128)(2,1)S(1)} %constant_dynamic-update-slice_fusion.refs_0_), channel_id=1, source_target_pairs={{0,48},{1,17},{2,50},{3,19},{4,52},{5,21},{6,54},{7,23},{8,56},{9,... | collective-permute-start | bytes 1572872 | tf_op jit(solution)/shard_map/ppermute | solution.py:179
  15.3 10.4 %collective-permute-start.6 = (bf16[2048,128]{1,0:T(8,128)(2,1)S(1)}, bf16[2048,128]{1,0:T(8,128)(2,1)S(1)}, u32[]{:S(2)}, u32[]{:S(2)}) collective-permute-start(bf16[2048,128]{1,0:T(8,128)(2,1)S(1)} %collective-permute-done.4.refs_6_), channel_id=1, source_target_pairs={{0,64},{1,193},{2,66},{3,195},{4,68},{5,197},{6,70},{7,199},{8,72}... | collective-permute-start | bytes 1572872 | tf_op jit(solution)/shard_map/ppermute | solution.py:179
  19.0 9.2 %collective-permute-start.10 = (bf16[2048,128]{1,0:T(8,128)(2,1)S(1)}, bf16[2048,128]{1,0:T(8,128)(2,1)S(1)}, u32[]{:S(2)}, u32[]{:S(2)}) collective-permute-start(bf16[2048,128]{1,0:T(8,128)(2,1)S(1)} %collective-permute-done.9.refs_3_), channel_id=1, source_target_pairs={{0,16},{1,49},{2,18},{3,51},{4,20},{5,53},{6,22},{7,55},{8,24},{9,... | collective-permute-start | bytes 1572872 | tf_op jit(solution)/shard_map/ppermute | solution.py:179
  20.1 8.3 %collective-permute-start.5 = (bf16[2048,128]{1,0:T(8,128)(2,1)S(1)}, bf16[2048,128]{1,0:T(8,128)(2,1)S(1)}, u32[]{:S(2)}, u32[]{:S(2)}) collective-permute-start(bf16[2048,128]{1,0:T(8,128)(2,1)S(1)} %collective-permute-done.4.refs_6_), channel_id=1, source_target_pairs={{0,1},{1,0},{2,3},{3,2},{4,5},{5,4},{6,7},{7,6},{8,9},{9,8},{10,11... | collective-permute-start | bytes 1572872 | tf_op jit(solution)/shard_map/ppermute | solution.py:169
  21.7 6.7 %collective-permute-start.8 = (bf16[2048,128]{1,0:T(8,128)(2,1)S(1)}, bf16[2048,128]{1,0:T(8,128)(2,1)S(1)}, u32[]{:S(2)}, u32[]{:S(2)}) collective-permute-start(bf16[2048,128]{1,0:T(8,128)(2,1)S(1)} %collective-permute-done.refs_2_), channel_id=1, source_target_pairs={{0,1},{1,0},{2,3},{3,2},{4,5},{5,4},{6,7},{7,6},{8,9},{9,8},{10,11... | collective-permute-start | bytes 1572872 | tf_op jit(solution)/shard_map/ppermute | solution.py:169
  25.7 2.7 %collective-permute-start.7 = (bf16[2048,128]{1,0:T(8,128)(2,1)S(1)}, bf16[2048,128]{1,0:T(8,128)(2,1)S(1)}, u32[]{:S(2)}, u32[]{:S(2)}) collective-permute-start(bf16[2048,128]{1,0:T(8,128)(2,1)S(1)} %collective-permute-done.6.refs_4_), channel_id=1, source_target_pairs={{0,1},{1,0},{2,3},{3,2},{4,5},{5,4},{6,7},{7,6},{8,9},{9,8},{10,11... | collective-permute-start | bytes 1572872 | tf_op jit(solution)/shard_map/ppermute | solution.py:169
  29.1 12.6 %collective-permute-start.18 = (bf16[1024,128]{1,0:T(8,128)(2,1)S(1)}, bf16[1024,128]{1,0:T(8,128)(2,1)S(1)}, u32[]{:S(2)}, u32[]{:S(2)}) collective-permute-start(bf16[1024,128]{1,0:T(8,128)(2,1)S(1)} %shard_map.57), channel_id=1, source_target_pairs={{0,14},{1,15},{2,0},{3,1},{4,2},{5,3},{6,4},{7,5},{8,6},{9,7},{10,... | collective-permute-start | bytes 786440 | tf_op jit(solution)/shard_map/ppermute | solution.py:165
  35.7 10.4 %collective-permute-start.11 = (bf16[1024,128]{1,0:T(8,128)(2,1)S(1)}, bf16[1024,128]{1,0:T(8,128)(2,1)S(1)}, u32[]{:S(2)}, u32[]{:S(2)}) collective-permute-start(bf16[1024,128]{1,0:T(8,128)(2,1)S(1)} %shard_map.58), channel_id=1, source_target_pairs={{0,2},{1,3},{2,4},{3,5},{4,6},{5,7},{6,8},{7,9},{8,10},{9,11},{10,... | collective-permute-start | bytes 786440 | tf_op jit(solution)/shard_map/ppermute | solution.py:165
  36.5 16.1 %collective-permute-start.14 = (bf16[1024,128]{1,0:T(8,128)(2,1)S(1)}, bf16[1024,128]{1,0:T(8,128)(2,1)S(1)}, u32[]{:S(2)}, u32[]{:S(2)}) collective-permute-start(bf16[1024,128]{1,0:T(8,128)(2,1)S(1)} %get-tuple-element.48), channel_id=1, source_target_pairs={{0,14},{1,15},{2,0},{3,1},{4,2},{5,3},{6,4},{7,5},{8,6},{9,7},{10,... | collective-permute-start | bytes 786440 | tf_op jit(solution)/shard_map/ppermute | solution.py:165
  40.7 11.1 %collective-permute-start.21 = (bf16[1024,128]{1,0:T(8,128)(2,1)S(1)}, bf16[1024,128]{1,0:T(8,128)(2,1)S(1)}, u32[]{:S(2)}, u32[]{:S(2)}) collective-permute-start(bf16[1024,128]{1,0:T(8,128)(2,1)S(1)} %get-tuple-element.58), channel_id=1, source_target_pairs={{0,2},{1,3},{2,4},{3,5},{4,6},{5,7},{6,8},{7,9},{8,10},{9,11},{10,... | collective-permute-start | bytes 786440 | tf_op jit(solution)/shard_map/ppermute | solution.py:165
  41.7 14.3 %collective-permute-start.19 = (bf16[1024,128]{1,0:T(8,128)(2,1)S(1)}, bf16[1024,128]{1,0:T(8,128)(2,1)S(1)}, u32[]{:S(2)}, u32[]{:S(2)}) collective-permute-start(bf16[1024,128]{1,0:T(8,128)(2,1)S(1)} %add_convert_fusion.5), channel_id=1, source_target_pairs={{0,14},{1,15},{2,0},{3,1},{4,2},{5,3},{6,4},{7,5},{8,6},{9,7},{10,... | collective-permute-start | bytes 786440 | tf_op jit(solution)/shard_map/ppermute | solution.py:165
  46.2 11.2 %collective-permute-start.12 = (bf16[1024,128]{1,0:T(8,128)(2,1)S(1)}, bf16[1024,128]{1,0:T(8,128)(2,1)S(1)}, u32[]{:S(2)}, u32[]{:S(2)}) collective-permute-start(bf16[1024,128]{1,0:T(8,128)(2,1)S(1)} %add_convert_fusion.11), channel_id=1, source_target_pairs={{0,2},{1,3},{2,4},{3,5},{4,6},{5,7},{6,8},{7,9},{8,10},{9,11},{10,... | collective-permute-start | bytes 786440 | tf_op jit(solution)/shard_map/ppermute | solution.py:165
  51.8 11.2 %collective-permute-start.22 = (bf16[1024,128]{1,0:T(8,128)(2,1)S(1)}, bf16[1024,128]{1,0:T(8,128)(2,1)S(1)}, u32[]{:S(2)}, u32[]{:S(2)}) collective-permute-start(bf16[1024,128]{1,0:T(8,128)(2,1)S(1)} %add_convert_fusion.2), channel_id=1, source_target_pairs={{0,2},{1,3},{2,4},{3,5},{4,6},{5,7},{6,8},{7,9},{8,10},{9,11},{10,... | collective-permute-start | bytes 786440 | tf_op jit(solution)/shard_map/ppermute | solution.py:165
  52.7 17.0 %collective-permute-start.15 = (bf16[1024,128]{1,0:T(8,128)(2,1)S(1)}, bf16[1024,128]{1,0:T(8,128)(2,1)S(1)}, u32[]{:S(2)}, u32[]{:S(2)}) collective-permute-start(bf16[1024,128]{1,0:T(8,128)(2,1)S(1)} %add_convert_fusion.8), channel_id=1, source_target_pairs={{0,14},{1,15},{2,0},{3,1},{4,2},{5,3},{6,4},{7,5},{8,6},{9,7},{10,... | collective-permute-start | bytes 786440 | tf_op jit(solution)/shard_map/ppermute | solution.py:165
  56.1 9.7 %collective-permute-start.20 = (bf16[1024,128]{1,0:T(8,128)(2,1)S(1)}, bf16[1024,128]{1,0:T(8,128)(2,1)S(1)}, u32[]{:S(2)}, u32[]{:S(2)}) collective-permute-start(bf16[1024,128]{1,0:T(8,128)(2,1)S(1)} %add_convert_fusion.4), channel_id=1, source_target_pairs={{0,14},{1,15},{2,0},{3,1},{4,2},{5,3},{6,4},{7,5},{8,6},{9,7},{10,... | collective-permute-start | bytes 786440 | tf_op jit(solution)/shard_map/ppermute | solution.py:165
  57.5 12.4 %collective-permute-start.13 = (bf16[1024,128]{1,0:T(8,128)(2,1)S(1)}, bf16[1024,128]{1,0:T(8,128)(2,1)S(1)}, u32[]{:S(2)}, u32[]{:S(2)}) collective-permute-start(bf16[1024,128]{1,0:T(8,128)(2,1)S(1)} %add_convert_fusion.10), channel_id=1, source_target_pairs={{0,2},{1,3},{2,4},{3,5},{4,6},{5,7},{6,8},{7,9},{8,10},{9,11},{10,... | collective-permute-start | bytes 786440 | tf_op jit(solution)/shard_map/ppermute | solution.py:165
  63.1 11.2 %collective-permute-start.23 = (bf16[1024,128]{1,0:T(8,128)(2,1)S(1)}, bf16[1024,128]{1,0:T(8,128)(2,1)S(1)}, u32[]{:S(2)}, u32[]{:S(2)}) collective-permute-start(bf16[1024,128]{1,0:T(8,128)(2,1)S(1)} %add_convert_fusion.1), channel_id=1, source_target_pairs={{0,2},{1,3},{2,4},{3,5},{4,6},{5,7},{6,8},{7,9},{8,10},{9,11},{10,... | collective-permute-start | bytes 786440 | tf_op jit(solution)/shard_map/ppermute | solution.py:165
  65.9 9.9 %collective-permute-start.24 = (bf16[1024,128]{1,0:T(8,128)(2,1)S(1)}, bf16[1024,128]{1,0:T(8,128)(2,1)S(1)}, u32[]{:S(2)}, u32[]{:S(2)}) collective-permute-start(bf16[1024,128]{1,0:T(8,128)(2,1)S(1)} %add_convert_fusion.3), channel_id=1, source_target_pairs={{0,14},{1,15},{2,0},{3,1},{4,2},{5,3},{6,4},{7,5},{8,6},{9,7},{10,... | collective-permute-start | bytes 786440 | tf_op jit(solution)/shard_map/ppermute | solution.py:165
  69.7 8.8 %collective-permute-start.16 = (bf16[1024,128]{1,0:T(8,128)(2,1)S(1)}, bf16[1024,128]{1,0:T(8,128)(2,1)S(1)}, u32[]{:S(2)}, u32[]{:S(2)}) collective-permute-start(bf16[1024,128]{1,0:T(8,128)(2,1)S(1)} %add_convert_fusion.7), channel_id=1, source_target_pairs={{0,14},{1,15},{2,0},{3,1},{4,2},{5,3},{6,4},{7,5},{8,6},{9,7},{10,... | collective-permute-start | bytes 786440 | tf_op jit(solution)/shard_map/ppermute | solution.py:165
  69.9 9.3 %collective-permute-start.17 = (bf16[1024,128]{1,0:T(8,128)(2,1)S(1)}, bf16[1024,128]{1,0:T(8,128)(2,1)S(1)}, u32[]{:S(2)}, u32[]{:S(2)}) collective-permute-start(bf16[1024,128]{1,0:T(8,128)(2,1)S(1)} %add_convert_fusion.9), channel_id=1, source_target_pairs={{0,2},{1,3},{2,4},{3,5},{4,6},{5,7},{6,8},{7,9},{8,10},{9,11},{10,... | collective-permute-start | bytes 786440 | tf_op jit(solution)/shard_map/ppermute | solution.py:165

commit v5 on v4

--- a/solution.py
+++ b/solution.py
@@ -13,15 +13,14 @@
 VMEM_BYTES = 8 * 1024 * 1024
 
 vmem = functools.partial(pl.BlockSpec, memory_space=pltpu.VMEM)
-smem = functools.partial(pl.BlockSpec, memory_space=pltpu.SMEM)
-
-
-def call(kernel, outs, operands, in_specs, scratch=(), flops=0, limit=VMEM_BYTES):
+
+
+def call(kernel, outs, operands, in_specs, scratch=(), flops=0, limit=VMEM_BYTES, out_space=pltpu.VMEM):
     return pl.pallas_call(
         kernel,
         out_shape=outs,
         in_specs=in_specs,
-        out_specs=[vmem()] * len(outs),
+        out_specs=[pl.BlockSpec(memory_space=out_space)] * len(outs),
         scratch_shapes=list(scratch),
         compiler_params=pltpu.CompilerParams(vmem_limit_bytes=limit),
         cost_estimate=pl.CostEstimate(flops=flops, bytes_accessed=0, transcendentals=0),
@@ -35,56 +34,69 @@
     count = wide // (2 * share)
     tiles = cols // BS
 
-    def kernel(three_hbm, mask3_hbm, dens_hbm, maskd_hbm, sizes_hbm, live_ref, own_ref, other_ref, *scratch):
-        three_ref, mask3_ref, dens_ref, maskd_ref, sizes_ref, held, sems = scratch
+    def kernel(three_hbm, mask3_hbm, dens_hbm, maskd_hbm, sizes_hbm, live_hbm, own_hbm, other_hbm, *scratch):
+        three_ref, mask3_ref, dens_ref, maskd_ref, sizes_ref, held, live_ref, own_ref, other_ref, sems = scratch
         depth = lax.axis_index("depth")
         z, c = depth // 2, depth % 2
         copies = [
             pltpu.make_async_copy(src, dst, sems.at[i])
             for i, (src, dst) in enumerate(
                 (
-                    (dens_hbm, dens_ref),
                     (maskd_hbm, maskd_ref),
                     (sizes_hbm, sizes_ref),
                     (mask3_hbm, mask3_ref),
+                    (dens_hbm, dens_ref),
                     (three_hbm, three_ref),
                 )
             )
         ]
         for copy in copies:
             copy.start()
-        for copy in copies[:2]:
-            copy.wait()
         lane = lax.broadcasted_iota(jnp.int32, (wide // BS, wide), 1)
         spread = (lane // BS == lax.broadcasted_iota(jnp.int32, lane.shape, 0)).astype(jnp.bfloat16)
-        keep = jnp.dot(
+        copies[0].wait()
+        held[...] = jnp.dot(
             maskd_ref[...].astype(jnp.float32).astype(jnp.bfloat16), spread, preferred_element_type=jnp.float32
         )
-        for i in range(deep // BS):
-            kept = jnp.broadcast_to(keep[i : i + 1, :], (BS, wide)).astype(jnp.bfloat16)
-            held[i * BS : (i + 1) * BS, :] = dens_ref[i * BS : (i + 1) * BS, :] * kept
-        for j in range(count):
-            first = lax.rem(z + j, count) * 2
-            for side, out_ref in ((c, own_ref), (1 - c, other_ref)):
-                place = pl.multiple_of((first + side) * share, share)
-                out_ref[j * deep : (j + 1) * deep, :] = held[:, pl.ds(place, share)]
-        for copy in copies[2:]:
-            copy.wait()
+        copies[1].wait()
         lane = lax.broadcasted_iota(jnp.int32, (tiles, cols), 1)
         tile = lax.broadcasted_iota(jnp.int32, lane.shape, 0)
         size = jnp.zeros_like(lane)
         for j in range(tiles):
             size = jnp.where(tile == j, sizes_ref[j], size)
         spread = ((lane // BS == tile) & (lane % BS < size)).astype(jnp.bfloat16)
+        copies[2].wait()
         keep = lax.dot_general(
             mask3_ref[...].astype(jnp.float32).astype(jnp.bfloat16),
             spread,
             (((0,), (0,)), ((), ())),
             preferred_element_type=jnp.float32,
         )
+        copies[3].wait()
+        for j in range(count):
+            first = lax.rem(z + j, count) * 2
+            for side, out_ref in ((c, own_ref), (1 - c, other_ref)):
+                place = pl.multiple_of((first + side) * share, share)
+                for i in range(deep // BS):
+                    kept = jnp.broadcast_to(held[i : i + 1, pl.ds(place, share)], (BS, share)).astype(jnp.bfloat16)
+                    piece = dens_ref[i * BS : (i + 1) * BS, pl.ds(place, share)]
+                    out_ref[j * deep + i * BS : j * deep + (i + 1) * BS, :] = piece * kept
+        leaving = [(other_ref, other_hbm), (own_ref, own_hbm)]
+        leaving = [pltpu.make_async_copy(src, dst, sems.at[5 + i]) for i, (src, dst) in enumerate(leaving)]
+        for copy in leaving:
+            copy.start()
+        copies[4].wait()
+        part = rows // 2
         for g in range(rows // BS):
             kept = jnp.broadcast_to(keep[g : g + 1, :], (BS, cols)).astype(jnp.bfloat16)
             live_ref[g * BS : (g + 1) * BS, :] = three_ref[g * BS : (g + 1) * BS, :] * kept
+            if (g + 1) * BS % part == 0:
+                at = pl.ds((g + 1) * BS - part, part)
+                copy = pltpu.make_async_copy(live_ref.at[at], live_hbm.at[at], sems.at[6 + (g + 1) * BS // part])
+                copy.start()
+                leaving.append(copy)
+        for copy in leaving:
+            copy.wait()
 
     return call(
         kernel,
@@ -98,10 +110,14 @@
             pltpu.VMEM((deep, wide), jnp.bfloat16),
             pltpu.VMEM((deep // BS, wide // BS), jnp.int32),
             pltpu.SMEM((tiles,), jnp.int32),
-            pltpu.VMEM((deep, wide), jnp.bfloat16),
-            pltpu.SemaphoreType.DMA((5,)),
+            pltpu.VMEM((deep // BS, wide), jnp.float32),
+            pltpu.VMEM((rows, cols), jnp.bfloat16),
+            pltpu.VMEM((count * deep, share), jnp.bfloat16),
+            pltpu.VMEM((count * deep, share), jnp.bfloat16),
+            pltpu.SemaphoreType.DMA((9,)),
         ],
         limit=56 * 1024 * 1024,
+        out_space=pltpu.HBM,
     )
 
 
@@ -132,7 +148,6 @@
 
 def dots(three, dens, jobs, cost=0):
     deep, share = 8 * 128, dens.shape[1]
-    tile = 256
     arrays = []
     for array, _ in three:
         if not any(array is other for other in arrays):
@@ -143,6 +158,7 @@
         ins, dens_ref, outs = refs[: len(arrays)], refs[len(arrays)], list(refs[len(arrays) + 1 :])
         for rows, picked, kinds in jobs:
             right = jnp.concatenate([dens_ref[j * deep : (j + 1) * deep, :] for j in picked], axis=1)
+            tile = rows // -(-rows // 512)
             for m in range(0, rows, tile):
                 left = jnp.concatenate([ins[w][base + m : base + m + tile, :] for w, base in three_at], axis=1)
                 total = jnp.dot(left, right, preferred_element_type=jnp.float32)
@@ -187,7 +203,8 @@
     live, own, other = masked(three_center, three_mask, density, density_mask, nu_sizes)
     bf16, f32 = jnp.bfloat16, jnp.float32
     n, deep = live.shape[0], 128
-    half, both = n // 2, own.shape[0]
+    rows_a = n * 16 // 32
+    rows_b = n - rows_a
 
     a_back = opposed(live, "row", 1)
     dens = jnp.concatenate([own, other_core(other)])
@@ -205,7 +222,7 @@
             (x, at) for x in (live, live_other, a_front, back_other, a_far, far_other, a_back, front_other)
         ]
 
-    three_a, three_b = three(0), three(half)
+    three_a, three_b = three(0), three(rows_a)
     dens = in_order((dens, b_front, b_far, b_back))
 
     def later(pieces, done):
@@ -215,31 +232,31 @@
     def plus(near, arrived):
         return (near + arrived.astype(f32)).astype(bf16)
 
-    (lb4,) = dots(three_b, dens, [(half, (4,), (bf16,))], COST)
+    (lb4,) = dots(three_b, dens, [(rows_b, (4,), (bf16,))], COST)
     lb = along_z(lb4, -1)
-    (ra4,) = dots(later(three_a, lb4), dens, [(half, (4,), (bf16,))], COST)
+    (ra4,) = dots(later(three_a, lb4), dens, [(rows_a, (4,), (bf16,))], COST)
     ra = along_z(ra4, 1)
-    la3, ra3 = dots(later(three_a, ra4), dens, [(half, (5, 3), (bf16, f32))], COST)
+    la3, ra3 = dots(later(three_a, ra4), dens, [(rows_a, (5, 3), (bf16, f32))], COST)
     la = along_z(la3, -1)
-    rb3, lb3 = dots(later(three_b, la3), dens, [(half, (3, 5), (bf16, f32))], COST)
+    rb3, lb3 = dots(later(three_b, la3), dens, [(rows_b, (3, 5), (bf16, f32))], COST)
     rb = along_z(rb3, 1)
     sa = plus(ra3, ra)
     sb = plus(lb3, lb)
     ra, lb = along_z(sa, 1), along_z(sb, -1)
-    ra2, la2 = dots(later(three_a, sa), dens, [(half, (2, 6), (f32, f32))])
-    rb2, lb2 = dots(later(three_b, sb), dens, [(half, (2, 6), (f32, f32))])
+    ra2, la2 = dots(later(three_a, sa), dens, [(rows_a, (2, 6), (f32, f32))])
+    rb2, lb2 = dots(later(three_b, sb), dens, [(rows_b, (2, 6), (f32, f32))])
     la, rb = along_z(plus(la2, la), -1), along_z(plus(rb2, rb), 1)
     sa = plus(ra2, ra)
     sb = plus(lb2, lb)
     ra, lb = along_z(sa, 1), along_z(sb, -1)
-    ra1, la1 = dots(later(three_a, sa), dens, [(half, (1, 7), (f32, f32))])
-    rb1, lb1 = dots(later(three_b, sb), dens, [(half, (1, 7), (f32, f32))])
+    ra1, la1 = dots(later(three_a, sa), dens, [(rows_a, (1, 7), (f32, f32))])
+    rb1, lb1 = dots(later(three_b, sb), dens, [(rows_b, (1, 7), (f32, f32))])
     la, rb = along_z(plus(la1, la), -1), along_z(plus(rb1, rb), 1)
     sa = plus(ra1, ra)
     sb = plus(lb1, lb)
     ra, lb = along_z(sa, 1), along_z(sb, -1)
-    (enda,) = dots(later(three_a, sa), dens, [(half, (0,), (f32,))])
-    (endb,) = dots(later(three_b, sb), dens, [(half, (0,), (f32,))])
+    (enda,) = dots(later(three_a, sa), dens, [(rows_a, (0,), (f32,))])
+    (endb,) = dots(later(three_b, sb), dens, [(rows_b, (0,), (f32,))])
     top = enda + la.astype(f32) + ra.astype(f32)
     bottom = endb + rb.astype(f32) + lb.astype(f32)
     return jnp.concatenate([top.astype(bf16), bottom.astype(bf16)])

time: 80.5 us -> 80.2 us (level)
  no operation moved by 1% of the time
where the time goes in v5:
time: 80.2 us; the launch traced here: 79.9 us
  waiting for transfers between devices  35.4 us (44%)
  starting transfers between devices  32.2 us (40%)
  Pallas kernels  9.39 us (12%)
  other arithmetic  1.64 us (2%)
  local copies, waits for them, and re-layouts  1.01 us (1%)
    ppermute x14, starting transfers between devices, along_z(): return lax.ppermute(block, 'depth', route)  24 us
    ppermute x14, waiting for transfers between devices, along_z(): return lax.ppermute(block, 'depth', route)  18.9 us
    ppermute x6, waiting for transfers between devices, opposed(): return lax.ppermute(block, (axis, 'depth'), route)  16.5 us
    pallas_call x12, Pallas kernels, call(): pl.pallas_call(kernel, out_shape=outs, in_specs=in_specs, out_specs=[pl.B...  9.39 us
    ppermute x6, starting transfers between devices, opposed(): return lax.ppermute(block, (axis, 'depth'), route)  7.35 us
  transfers between devices with their start and end apart: 25, of which 15 were waited for; matrix products, arithmetic and copies ran while one was open for 2% of the time, Pallas kernels for 8%

profile of v5, /device:TPU:24, one launch (start us, length us, event | category | flops | bytes accessed | tf_op | source)
XLA Modules:
  0.0 79.9 jit_solution(4296024152173566573)
XLA Ops:
  0.0 2.2 %shard_map.55 = (bf16[2048,128]{1,0:T(8,128)(2,1)}, bf16[1024,128]{1,0:T(8,128)(2,1)}, bf16[1024,128]{1,0:T(8,128)(2,1)}) custom-call(bf16[2048,128]{1,0:T(8,128)(2,1)} %three_hbm.1, s32[4,64]{1,0:T(4,128)} %bitcast.1, bf16[128,2048]{1,0:T(8,128)(2,1)} %dens_hbm.1, s32[4,64]{1,0:T(4,128)} %maskd_hbm.1, s32[4]{0:T(128)} %sizes_hbm.1), custom_call_target="tpu_custom_call" | custom-call | tf_op jit(solution)/shard_map/pallas_call | solution.py:19
  2.3 1.6 %collective-permute-start.4 = (bf16[2048,128]{1,0:T(8,128)(2,1)}, bf16[2048,128]{1,0:T(8,128)(2,1)S(1)}, u32[]{:S(2)}, u32[]{:S(2)}) collective-permute-start(bf16[2048,128]{1,0:T(8,128)(2,1)} %get-tuple-element.45.refs_0_), channel_id=1, source_target_pairs={{0,64},{1,193},{2,66},{3,195},{4,68},{5,197},{6,70},{7,199},{8,72}... | collective-permute-start | bytes 1572872 | tf_op jit(solution)/shard_map/ppermute | solution.py:195
  3.9 1.0 %constant_dynamic-update-slice_fusion.1 = bf16[2048,128]{1,0:T(8,128)(2,1)S(1)} fusion(bf16[1024,128]{1,0:T(8,128)(2,1)} %get-tuple-element.33), kind=kLoop, calls=%fused_computation.14 | loop fusion | bytes 524288
  4.9 1.2 %collective-permute-start.9 = (bf16[2048,128]{1,0:T(8,128)(2,1)S(1)}, bf16[2048,128]{1,0:T(8,128)(2,1)S(1)}, u32[]{:S(2)}, u32[]{:S(2)}) collective-permute-start(bf16[2048,128]{1,0:T(8,128)(2,1)S(1)} %constant_dynamic-update-slice_fusion.refs_0_), channel_id=1, source_target_pairs={{0,16},{1,49},{2,18},{3,51},{4,20},{5,53},{6,22},{7,55},{8,24},{9,... | collective-permute-start | bytes 1572872 | tf_op jit(solution)/shard_map/ppermute | solution.py:195
  6.1 0.7 collective-permute-start.3
  6.9 1.8 %collective-permute-start = (bf16[2048,128]{1,0:T(8,128)(2,1)}, bf16[2048,128]{1,0:T(8,128)(2,1)S(1)}, u32[]{:S(2)}, u32[]{:S(2)}) collective-permute-start(bf16[2048,128]{1,0:T(8,128)(2,1)} %get-tuple-element.45.refs_0_), channel_id=1, source_target_pairs={{0,192},{1,65},{2,194},{3,67},{4,196},{5,69},{6,198},{7,71},{8,200... | collective-permute-start | bytes 1572872 | tf_op jit(solution)/shard_map/ppermute | solution.py:195
  8.7 0.3 collective-permute-start.2
  9.0 6.1 %collective-permute-done.4.refs_6_ = bf16[2048,128]{1,0:T(8,128)(2,1)S(1)} collective-permute-done((bf16[2048,128]{1,0:T(8,128)(2,1)}, bf16[2048,128]{1,0:T(8,128)(2,1)S(1)}, u32[]{:S(2)}, u32[]{:S(2)}) %collective-permute-start.4) | collective-permute-done | bytes 524320 | tf_op jit(solution)/shard_map/ppermute | solution.py:195
  15.0 1.4 %collective-permute-start.6 = (bf16[2048,128]{1,0:T(8,128)(2,1)S(1)}, bf16[2048,128]{1,0:T(8,128)(2,1)S(1)}, u32[]{:S(2)}, u32[]{:S(2)}) collective-permute-start(bf16[2048,128]{1,0:T(8,128)(2,1)S(1)} %collective-permute-done.4.refs_6_), channel_id=1, source_target_pairs={{0,64},{1,193},{2,66},{3,195},{4,68},{5,197},{6,70},{7,199},{8,72}... | collective-permute-start | bytes 1572872 | tf_op jit(solution)/shard_map/ppermute | solution.py:195
  16.5 2.3 %collective-permute-done.9.refs_3_ = bf16[2048,128]{1,0:T(8,128)(2,1)S(1)} collective-permute-done((bf16[2048,128]{1,0:T(8,128)(2,1)S(1)}, bf16[2048,128]{1,0:T(8,128)(2,1)S(1)}, u32[]{:S(2)}, u32[]{:S(2)}) %collective-permute-start.9) | collective-permute-done | bytes 524320 | tf_op jit(solution)/shard_map/ppermute | solution.py:195
  18.8 1.1 %collective-permute-start.10 = (bf16[2048,128]{1,0:T(8,128)(2,1)S(1)}, bf16[2048,128]{1,0:T(8,128)(2,1)S(1)}, u32[]{:S(2)}, u32[]{:S(2)}) collective-permute-start(bf16[2048,128]{1,0:T(8,128)(2,1)S(1)} %collective-permute-done.9.refs_3_), channel_id=1, source_target_pairs={{0,16},{1,49},{2,18},{3,51},{4,20},{5,53},{6,22},{7,55},{8,24},{9,... | collective-permute-start | bytes 1572872 | tf_op jit(solution)/shard_map/ppermute | solution.py:195
  19.8 1.6 %collective-permute-done.2.refs_1_ = bf16[2048,128]{1,0:T(8,128)(2,1)S(1)} collective-permute-done((bf16[2048,128]{1,0:T(8,128)(2,1)S(1)}, bf16[2048,128]{1,0:T(8,128)(2,1)S(1)}, u32[]{:S(2)}, u32[]{:S(2)}) %collective-permute-start.2) | collective-permute-done | bytes 524320 | tf_op jit(solution)/shard_map/ppermute | solution.py:195
  21.5 4.0 %collective-permute-done.6.refs_4_ = bf16[2048,128]{1,0:T(8,128)(2,1)S(1)} collective-permute-done((bf16[2048,128]{1,0:T(8,128)(2,1)S(1)}, bf16[2048,128]{1,0:T(8,128)(2,1)S(1)}, u32[]{:S(2)}, u32[]{:S(2)}) %collective-permute-start.6) | collective-permute-done | bytes 524320 | tf_op jit(solution)/shard_map/ppermute | solution.py:195
  25.4 2.5 %collective-permute-done.10.refs_2_ = bf16[2048,128]{1,0:T(8,128)(2,1)S(1)} collective-permute-done((bf16[2048,128]{1,0:T(8,128)(2,1)S(1)}, bf16[2048,128]{1,0:T(8,128)(2,1)S(1)}, u32[]{:S(2)}, u32[]{:S(2)}) %collective-permute-start.10) | collective-permute-done | bytes 524320 | tf_op jit(solution)/shard_map/ppermute | solution.py:195
  28.0 0.2 shard_map.56.refs_8_
  28.2 0.7 shard_map.57
  28.9 5.9 %collective-permute-start.18 = (bf16[1024,128]{1,0:T(8,128)(2,1)S(1)}, bf16[1024,128]{1,0:T(8,128)(2,1)S(1)}, u32[]{:S(2)}, u32[]{:S(2)}) collective-permute-start(bf16[1024,128]{1,0:T(8,128)(2,1)S(1)} %shard_map.57), channel_id=1, source_target_pairs={{0,14},{1,15},{2,0},{3,1},{4,2},{5,3},{6,4},{7,5},{8,6},{9,7},{10,... | collective-permute-start | bytes 786440 | tf_op jit(solution)/shard_map/ppermute | solution.py:181
  34.8 0.7 shard_map.58
  35.6 0.7 shard_map.59
  36.3 3.3 %collective-permute-start.14 = (bf16[1024,128]{1,0:T(8,128)(2,1)S(1)}, bf16[1024,128]{1,0:T(8,128)(2,1)S(1)}, u32[]{:S(2)}, u32[]{:S(2)}) collective-permute-start(bf16[1024,128]{1,0:T(8,128)(2,1)S(1)} %get-tuple-element.48), channel_id=1, source_target_pairs={{0,14},{1,15},{2,0},{3,1},{4,2},{5,3},{6,4},{7,5},{8,6},{9,7},{10,... | collective-permute-start | bytes 786440 | tf_op jit(solution)/shard_map/ppermute | solution.py:181
  39.6 0.7 shard_map.63
  40.3 0.3 collective-permute-start.21
  40.6 0.8 %collective-permute-done.18 = bf16[1024,128]{1,0:T(8,128)(2,1)S(1)} collective-permute-done((bf16[1024,128]{1,0:T(8,128)(2,1)S(1)}, bf16[1024,128]{1,0:T(8,128)(2,1)S(1)}, u32[]{:S(2)}, u32[]{:S(2)}) %collective-permute-start.18) | collective-permute-done | bytes 262176 | tf_op jit(solution)/shard_map/ppermute | solution.py:181
  41.5 3.8 %collective-permute-start.19 = (bf16[1024,128]{1,0:T(8,128)(2,1)S(1)}, bf16[1024,128]{1,0:T(8,128)(2,1)S(1)}, u32[]{:S(2)}, u32[]{:S(2)}) collective-permute-start(bf16[1024,128]{1,0:T(8,128)(2,1)S(1)} %add_convert_fusion.5), channel_id=1, source_target_pairs={{0,14},{1,15},{2,0},{3,1},{4,2},{5,3},{6,4},{7,5},{8,6},{9,7},{10,... | collective-permute-start | bytes 786440 | tf_op jit(solution)/shard_map/ppermute | solution.py:181
  45.2 0.7 collective-permute-done.11
  46.1 0.7 shard_map.64
  46.8 4.7 %collective-permute-done.21 = bf16[1024,128]{1,0:T(8,128)(2,1)S(1)} collective-permute-done((bf16[1024,128]{1,0:T(8,128)(2,1)S(1)}, bf16[1024,128]{1,0:T(8,128)(2,1)S(1)}, u32[]{:S(2)}, u32[]{:S(2)}) %collective-permute-start.21) | collective-permute-done | bytes 262176 | tf_op jit(solution)/shard_map/ppermute | solution.py:181
  51.7 0.7 shard_map.60
  52.5 3.3 %collective-permute-start.15 = (bf16[1024,128]{1,0:T(8,128)(2,1)S(1)}, bf16[1024,128]{1,0:T(8,128)(2,1)S(1)}, u32[]{:S(2)}, u32[]{:S(2)}) collective-permute-start(bf16[1024,128]{1,0:T(8,128)(2,1)S(1)} %add_convert_fusion.8), channel_id=1, source_target_pairs={{0,14},{1,15},{2,0},{3,1},{4,2},{5,3},{6,4},{7,5},{8,6},{9,7},{10,... | collective-permute-start | bytes 786440 | tf_op jit(solution)/shard_map/ppermute | solution.py:181
  55.9 0.3 collective-permute-start.20
  56.1 1.0 %collective-permute-done.12 = bf16[1024,128]{1,0:T(8,128)(2,1)S(1)} collective-permute-done((bf16[1024,128]{1,0:T(8,128)(2,1)S(1)}, bf16[1024,128]{1,0:T(8,128)(2,1)S(1)}, u32[]{:S(2)}, u32[]{:S(2)}) %collective-permute-start.12) | collective-permute-done | bytes 262176 | tf_op jit(solution)/shard_map/ppermute | solution.py:181
  57.2 0.9 %collective-permute-start.13 = (bf16[1024,128]{1,0:T(8,128)(2,1)S(1)}, bf16[1024,128]{1,0:T(8,128)(2,1)S(1)}, u32[]{:S(2)}, u32[]{:S(2)}) collective-permute-start(bf16[1024,128]{1,0:T(8,128)(2,1)S(1)} %add_convert_fusion.10), channel_id=1, source_target_pairs={{0,2},{1,3},{2,4},{3,5},{4,6},{5,7},{6,8},{7,9},{8,10},{9,11},{10,... | collective-permute-start | bytes 786440 | tf_op jit(solution)/shard_map/ppermute | solution.py:181
  58.1 0.7 shard_map.65
  58.8 4.0 %collective-permute-done.22 = bf16[1024,128]{1,0:T(8,128)(2,1)S(1)} collective-permute-done((bf16[1024,128]{1,0:T(8,128)(2,1)S(1)}, bf16[1024,128]{1,0:T(8,128)(2,1)S(1)}, u32[]{:S(2)}, u32[]{:S(2)}) %collective-permute-start.22) | collective-permute-done | bytes 262176 | tf_op jit(solution)/shard_map/ppermute | solution.py:181
  62.9 0.7 shard_map.61
  63.6 2.0 %collective-permute-done.20 = bf16[1024,128]{1,0:T(8,128)(2,1)S(1)} collective-permute-done((bf16[1024,128]{1,0:T(8,128)(2,1)S(1)}, bf16[1024,128]{1,0:T(8,128)(2,1)S(1)}, u32[]{:S(2)}, u32[]{:S(2)}) %collective-permute-start.20) | collective-permute-done | bytes 262176 | tf_op jit(solution)/shard_map/ppermute | solution.py:181
  65.7 3.8 %collective-permute-start.24 = (bf16[1024,128]{1,0:T(8,128)(2,1)S(1)}, bf16[1024,128]{1,0:T(8,128)(2,1)S(1)}, u32[]{:S(2)}, u32[]{:S(2)}) collective-permute-start(bf16[1024,128]{1,0:T(8,128)(2,1)S(1)} %add_convert_fusion.3), channel_id=1, source_target_pairs={{0,14},{1,15},{2,0},{3,1},{4,2},{5,3},{6,4},{7,5},{8,6},{9,7},{10,... | collective-permute-start | bytes 786440 | tf_op jit(solution)/shard_map/ppermute | solution.py:181
  69.5 0.1 collective-permute-start.16
  69.7 2.1 %collective-permute-start.17 = (bf16[1024,128]{1,0:T(8,128)(2,1)S(1)}, bf16[1024,128]{1,0:T(8,128)(2,1)S(1)}, u32[]{:S(2)}, u32[]{:S(2)}) collective-permute-start(bf16[1024,128]{1,0:T(8,128)(2,1)S(1)} %add_convert_fusion.9), channel_id=1, source_target_pairs={{0,2},{1,3},{2,4},{3,5},{4,6},{5,7},{6,8},{7,9},{8,10},{9,11},{10,... | collective-permute-start | bytes 786440 | tf_op jit(solution)/shard_map/ppermute | solution.py:181
  71.8 0.7 shard_map.66
  72.5 0.7 shard_map.62
  73.2 0.9 %collective-permute-done.23 = bf16[1024,128]{1,0:T(8,128)(2,1)S(1)} collective-permute-done((bf16[1024,128]{1,0:T(8,128)(2,1)S(1)}, bf16[1024,128]{1,0:T(8,128)(2,1)S(1)}, u32[]{:S(2)}, u32[]{:S(2)}) %collective-permute-start.23) | collective-permute-done | bytes 262176 | tf_op jit(solution)/shard_map/ppermute | solution.py:181
  74.0 1.5 %collective-permute-done.24 = bf16[1024,128]{1,0:T(8,128)(2,1)S(1)} collective-permute-done((bf16[1024,128]{1,0:T(8,128)(2,1)S(1)}, bf16[1024,128]{1,0:T(8,128)(2,1)S(1)}, u32[]{:S(2)}, u32[]{:S(2)}) %collective-permute-start.24) | collective-permute-done | bytes 262176 | tf_op jit(solution)/shard_map/ppermute | solution.py:181
  75.5 0.1 add_convert_fusion
  75.6 2.7 %collective-permute-done.16 = bf16[1024,128]{1,0:T(8,128)(2,1)S(1)} collective-permute-done((bf16[1024,128]{1,0:T(8,128)(2,1)S(1)}, bf16[1024,128]{1,0:T(8,128)(2,1)S(1)}, u32[]{:S(2)}, u32[]{:S(2)}) %collective-permute-start.16) | collective-permute-done | bytes 262176 | tf_op jit(solution)/shard_map/ppermute | solution.py:181
  78.4 0.6 collective-permute-done.17
  79.0 0.1 add_convert_fusion.6
  79.1 0.8 %pad_maximum_fusion = bf16[2048,128]{1,0:T(8,128)(2,1)} fusion(bf16[1024,128]{1,0:T(8,128)(2,1)S(1)} %add_convert_fusion, bf16[1024,128]{1,0:T(8,128)(2,1)S(1)} %add_convert_fusion.6), kind=kLoop, calls=%fused_computation | loop fusion | flops 1048576 | bytes 1048576 | tf_op jit(solution)/shard_map/concatenate | solution.py:262
  (31 shorter events, 1.1 us)
Async XLA Ops:
  2.2 2.6 %collective-permute-start.1 = (bf16[1024,128]{1,0:T(8,128)(2,1)}, bf16[1024,128]{1,0:T(8,128)(2,1)S(1)}, u32[]{:S(2)}, u32[]{:S(2)}) collective-permute-start(bf16[1024,128]{1,0:T(8,128)(2,1)} %get-tuple-element.34), channel_id=1, source_target_pairs={{0,1},{1,0},{2,3},{3,2},{4,5},{5,4},{6,7},{7,6},{8,9},{9,8},{10,11... | collective-permute-start | bytes 786440 | tf_op jit(solution)/shard_map/ppermute | solution.py:185
  2.3 12.7 %collective-permute-start.4 = (bf16[2048,128]{1,0:T(8,128)(2,1)}, bf16[2048,128]{1,0:T(8,128)(2,1)S(1)}, u32[]{:S(2)}, u32[]{:S(2)}) collective-permute-start(bf16[2048,128]{1,0:T(8,128)(2,1)} %get-tuple-element.45.refs_0_), channel_id=1, source_target_pairs={{0,64},{1,193},{2,66},{3,195},{4,68},{5,197},{6,70},{7,199},{8,72}... | collective-permute-start | bytes 1572872 | tf_op jit(solution)/shard_map/ppermute | solution.py:195
  4.9 23.2 %copy-start = (bf16[2048,128]{1,0:T(8,128)(2,1)S(1)}, bf16[2048,128]{1,0:T(8,128)(2,1)}, u32[]{:S(2)}) copy-start(bf16[2048,128]{1,0:T(8,128)(2,1)} %get-tuple-element.45.refs_0_) | copy-start | bytes 1572868
  4.9 13.8 %collective-permute-start.9 = (bf16[2048,128]{1,0:T(8,128)(2,1)S(1)}, bf16[2048,128]{1,0:T(8,128)(2,1)S(1)}, u32[]{:S(2)}, u32[]{:S(2)}) collective-permute-start(bf16[2048,128]{1,0:T(8,128)(2,1)S(1)} %constant_dynamic-update-slice_fusion.refs_0_), channel_id=1, source_target_pairs={{0,16},{1,49},{2,18},{3,51},{4,20},{5,53},{6,22},{7,55},{8,24},{9,... | collective-permute-start | bytes 1572872 | tf_op jit(solution)/shard_map/ppermute | solution.py:195
  6.1 13.7 %collective-permute-start.3 = (bf16[2048,128]{1,0:T(8,128)(2,1)}, bf16[2048,128]{1,0:T(8,128)(2,1)S(1)}, u32[]{:S(2)}, u32[]{:S(2)}) collective-permute-start(bf16[2048,128]{1,0:T(8,128)(2,1)} %get-tuple-element.45.refs_0_), channel_id=1, source_target_pairs={{0,1},{1,0},{2,3},{3,2},{4,5},{5,4},{6,7},{7,6},{8,9},{9,8},{10,11... | collective-permute-start | bytes 1572872 | tf_op jit(solution)/shard_map/ppermute | solution.py:185
  6.9 13.0 %collective-permute-start = (bf16[2048,128]{1,0:T(8,128)(2,1)}, bf16[2048,128]{1,0:T(8,128)(2,1)S(1)}, u32[]{:S(2)}, u32[]{:S(2)}) collective-permute-start(bf16[2048,128]{1,0:T(8,128)(2,1)} %get-tuple-element.45.refs_0_), channel_id=1, source_target_pairs={{0,192},{1,65},{2,194},{3,67},{4,196},{5,69},{6,198},{7,71},{8,200... | collective-permute-start | bytes 1572872 | tf_op jit(solution)/shard_map/ppermute | solution.py:195
  8.7 12.7 %collective-permute-start.2 = (bf16[2048,128]{1,0:T(8,128)(2,1)S(1)}, bf16[2048,128]{1,0:T(8,128)(2,1)S(1)}, u32[]{:S(2)}, u32[]{:S(2)}) collective-permute-start(bf16[2048,128]{1,0:T(8,128)(2,1)S(1)} %constant_dynamic-update-slice_fusion.refs_0_), channel_id=1, source_target_pairs={{0,48},{1,17},{2,50},{3,19},{4,52},{5,21},{6,54},{7,23},{8,56},{9,... | collective-permute-start | bytes 1572872 | tf_op jit(solution)/shard_map/ppermute | solution.py:195
  15.0 10.4 %collective-permute-start.6 = (bf16[2048,128]{1,0:T(8,128)(2,1)S(1)}, bf16[2048,128]{1,0:T(8,128)(2,1)S(1)}, u32[]{:S(2)}, u32[]{:S(2)}) collective-permute-start(bf16[2048,128]{1,0:T(8,128)(2,1)S(1)} %collective-permute-done.4.refs_6_), channel_id=1, source_target_pairs={{0,64},{1,193},{2,66},{3,195},{4,68},{5,197},{6,70},{7,199},{8,72}... | collective-permute-start | bytes 1572872 | tf_op jit(solution)/shard_map/ppermute | solution.py:195
  18.8 9.2 %collective-permute-start.10 = (bf16[2048,128]{1,0:T(8,128)(2,1)S(1)}, bf16[2048,128]{1,0:T(8,128)(2,1)S(1)}, u32[]{:S(2)}, u32[]{:S(2)}) collective-permute-start(bf16[2048,128]{1,0:T(8,128)(2,1)S(1)} %collective-permute-done.9.refs_3_), channel_id=1, source_target_pairs={{0,16},{1,49},{2,18},{3,51},{4,20},{5,53},{6,22},{7,55},{8,24},{9,... | collective-permute-start | bytes 1572872 | tf_op jit(solution)/shard_map/ppermute | solution.py:195
  19.8 8.3 %collective-permute-start.5 = (bf16[2048,128]{1,0:T(8,128)(2,1)S(1)}, bf16[2048,128]{1,0:T(8,128)(2,1)S(1)}, u32[]{:S(2)}, u32[]{:S(2)}) collective-permute-start(bf16[2048,128]{1,0:T(8,128)(2,1)S(1)} %collective-permute-done.4.refs_6_), channel_id=1, source_target_pairs={{0,1},{1,0},{2,3},{3,2},{4,5},{5,4},{6,7},{7,6},{8,9},{9,8},{10,11... | collective-permute-start | bytes 1572872 | tf_op jit(solution)/shard_map/ppermute | solution.py:185
  21.5 6.7 %collective-permute-start.8 = (bf16[2048,128]{1,0:T(8,128)(2,1)S(1)}, bf16[2048,128]{1,0:T(8,128)(2,1)S(1)}, u32[]{:S(2)}, u32[]{:S(2)}) collective-permute-start(bf16[2048,128]{1,0:T(8,128)(2,1)S(1)} %collective-permute-done.refs_2_), channel_id=1, source_target_pairs={{0,1},{1,0},{2,3},{3,2},{4,5},{5,4},{6,7},{7,6},{8,9},{9,8},{10,11... | collective-permute-start | bytes 1572872 | tf_op jit(solution)/shard_map/ppermute | solution.py:185
  25.4 2.7 %collective-permute-start.7 = (bf16[2048,128]{1,0:T(8,128)(2,1)S(1)}, bf16[2048,128]{1,0:T(8,128)(2,1)S(1)}, u32[]{:S(2)}, u32[]{:S(2)}) collective-permute-start(bf16[2048,128]{1,0:T(8,128)(2,1)S(1)} %collective-permute-done.6.refs_4_), channel_id=1, source_target_pairs={{0,1},{1,0},{2,3},{3,2},{4,5},{5,4},{6,7},{7,6},{8,9},{9,8},{10,11... | collective-permute-start | bytes 1572872 | tf_op jit(solution)/shard_map/ppermute | solution.py:185
  28.9 12.5 %collective-permute-start.18 = (bf16[1024,128]{1,0:T(8,128)(2,1)S(1)}, bf16[1024,128]{1,0:T(8,128)(2,1)S(1)}, u32[]{:S(2)}, u32[]{:S(2)}) collective-permute-start(bf16[1024,128]{1,0:T(8,128)(2,1)S(1)} %shard_map.57), channel_id=1, source_target_pairs={{0,14},{1,15},{2,0},{3,1},{4,2},{5,3},{6,4},{7,5},{8,6},{9,7},{10,... | collective-permute-start | bytes 786440 | tf_op jit(solution)/shard_map/ppermute | solution.py:181
  35.5 10.4 %collective-permute-start.11 = (bf16[1024,128]{1,0:T(8,128)(2,1)S(1)}, bf16[1024,128]{1,0:T(8,128)(2,1)S(1)}, u32[]{:S(2)}, u32[]{:S(2)}) collective-permute-start(bf16[1024,128]{1,0:T(8,128)(2,1)S(1)} %shard_map.58), channel_id=1, source_target_pairs={{0,2},{1,3},{2,4},{3,5},{4,6},{5,7},{6,8},{7,9},{8,10},{9,11},{10,... | collective-permute-start | bytes 786440 | tf_op jit(solution)/shard_map/ppermute | solution.py:181
  36.3 16.1 %collective-permute-start.14 = (bf16[1024,128]{1,0:T(8,128)(2,1)S(1)}, bf16[1024,128]{1,0:T(8,128)(2,1)S(1)}, u32[]{:S(2)}, u32[]{:S(2)}) collective-permute-start(bf16[1024,128]{1,0:T(8,128)(2,1)S(1)} %get-tuple-element.48), channel_id=1, source_target_pairs={{0,14},{1,15},{2,0},{3,1},{4,2},{5,3},{6,4},{7,5},{8,6},{9,7},{10,... | collective-permute-start | bytes 786440 | tf_op jit(solution)/shard_map/ppermute | solution.py:181
  40.3 11.2 %collective-permute-start.21 = (bf16[1024,128]{1,0:T(8,128)(2,1)S(1)}, bf16[1024,128]{1,0:T(8,128)(2,1)S(1)}, u32[]{:S(2)}, u32[]{:S(2)}) collective-permute-start(bf16[1024,128]{1,0:T(8,128)(2,1)S(1)} %get-tuple-element.58), channel_id=1, source_target_pairs={{0,2},{1,3},{2,4},{3,5},{4,6},{5,7},{6,8},{7,9},{8,10},{9,11},{10,... | collective-permute-start | bytes 786440 | tf_op jit(solution)/shard_map/ppermute | solution.py:181
  41.5 14.3 %collective-permute-start.19 = (bf16[1024,128]{1,0:T(8,128)(2,1)S(1)}, bf16[1024,128]{1,0:T(8,128)(2,1)S(1)}, u32[]{:S(2)}, u32[]{:S(2)}) collective-permute-start(bf16[1024,128]{1,0:T(8,128)(2,1)S(1)} %add_convert_fusion.5), channel_id=1, source_target_pairs={{0,14},{1,15},{2,0},{3,1},{4,2},{5,3},{6,4},{7,5},{8,6},{9,7},{10,... | collective-permute-start | bytes 786440 | tf_op jit(solution)/shard_map/ppermute | solution.py:181
  46.0 11.2 %collective-permute-start.12 = (bf16[1024,128]{1,0:T(8,128)(2,1)S(1)}, bf16[1024,128]{1,0:T(8,128)(2,1)S(1)}, u32[]{:S(2)}, u32[]{:S(2)}) collective-permute-start(bf16[1024,128]{1,0:T(8,128)(2,1)S(1)} %add_convert_fusion.11), channel_id=1, source_target_pairs={{0,2},{1,3},{2,4},{3,5},{4,6},{5,7},{6,8},{7,9},{8,10},{9,11},{10,... | collective-permute-start | bytes 786440 | tf_op jit(solution)/shard_map/ppermute | solution.py:181
  51.6 11.2 %collective-permute-start.22 = (bf16[1024,128]{1,0:T(8,128)(2,1)S(1)}, bf16[1024,128]{1,0:T(8,128)(2,1)S(1)}, u32[]{:S(2)}, u32[]{:S(2)}) collective-permute-start(bf16[1024,128]{1,0:T(8,128)(2,1)S(1)} %add_convert_fusion.2), channel_id=1, source_target_pairs={{0,2},{1,3},{2,4},{3,5},{4,6},{5,7},{6,8},{7,9},{8,10},{9,11},{10,... | collective-permute-start | bytes 786440 | tf_op jit(solution)/shard_map/ppermute | solution.py:181
  52.5 17.0 %collective-permute-start.15 = (bf16[1024,128]{1,0:T(8,128)(2,1)S(1)}, bf16[1024,128]{1,0:T(8,128)(2,1)S(1)}, u32[]{:S(2)}, u32[]{:S(2)}) collective-permute-start(bf16[1024,128]{1,0:T(8,128)(2,1)S(1)} %add_convert_fusion.8), channel_id=1, source_target_pairs={{0,14},{1,15},{2,0},{3,1},{4,2},{5,3},{6,4},{7,5},{8,6},{9,7},{10,... | collective-permute-start | bytes 786440 | tf_op jit(solution)/shard_map/ppermute | solution.py:181
  55.9 9.7 %collective-permute-start.20 = (bf16[1024,128]{1,0:T(8,128)(2,1)S(1)}, bf16[1024,128]{1,0:T(8,128)(2,1)S(1)}, u32[]{:S(2)}, u32[]{:S(2)}) collective-permute-start(bf16[1024,128]{1,0:T(8,128)(2,1)S(1)} %add_convert_fusion.4), channel_id=1, source_target_pairs={{0,14},{1,15},{2,0},{3,1},{4,2},{5,3},{6,4},{7,5},{8,6},{9,7},{10,... | collective-permute-start | bytes 786440 | tf_op jit(solution)/shard_map/ppermute | solution.py:181
  57.2 12.4 %collective-permute-start.13 = (bf16[1024,128]{1,0:T(8,128)(2,1)S(1)}, bf16[1024,128]{1,0:T(8,128)(2,1)S(1)}, u32[]{:S(2)}, u32[]{:S(2)}) collective-permute-start(bf16[1024,128]{1,0:T(8,128)(2,1)S(1)} %add_convert_fusion.10), channel_id=1, source_target_pairs={{0,2},{1,3},{2,4},{3,5},{4,6},{5,7},{6,8},{7,9},{8,10},{9,11},{10,... | collective-permute-start | bytes 786440 | tf_op jit(solution)/shard_map/ppermute | solution.py:181
  62.8 11.2 %collective-permute-start.23 = (bf16[1024,128]{1,0:T(8,128)(2,1)S(1)}, bf16[1024,128]{1,0:T(8,128)(2,1)S(1)}, u32[]{:S(2)}, u32[]{:S(2)}) collective-permute-start(bf16[1024,128]{1,0:T(8,128)(2,1)S(1)} %add_convert_fusion.1), channel_id=1, source_target_pairs={{0,2},{1,3},{2,4},{3,5},{4,6},{5,7},{6,8},{7,9},{8,10},{9,11},{10,... | collective-permute-start | bytes 786440 | tf_op jit(solution)/shard_map/ppermute | solution.py:181
  65.7 9.9 %collective-permute-start.24 = (bf16[1024,128]{1,0:T(8,128)(2,1)S(1)}, bf16[1024,128]{1,0:T(8,128)(2,1)S(1)}, u32[]{:S(2)}, u32[]{:S(2)}) collective-permute-start(bf16[1024,128]{1,0:T(8,128)(2,1)S(1)} %add_convert_fusion.3), channel_id=1, source_target_pairs={{0,14},{1,15},{2,0},{3,1},{4,2},{5,3},{6,4},{7,5},{8,6},{9,7},{10,... | collective-permute-start | bytes 786440 | tf_op jit(solution)/shard_map/ppermute | solution.py:181
  69.5 8.8 %collective-permute-start.16 = (bf16[1024,128]{1,0:T(8,128)(2,1)S(1)}, bf16[1024,128]{1,0:T(8,128)(2,1)S(1)}, u32[]{:S(2)}, u32[]{:S(2)}) collective-permute-start(bf16[1024,128]{1,0:T(8,128)(2,1)S(1)} %add_convert_fusion.7), channel_id=1, source_target_pairs={{0,14},{1,15},{2,0},{3,1},{4,2},{5,3},{6,4},{7,5},{8,6},{9,7},{10,... | collective-permute-start | bytes 786440 | tf_op jit(solution)/shard_map/ppermute | solution.py:181
  69.7 9.3 %collective-permute-start.17 = (bf16[1024,128]{1,0:T(8,128)(2,1)S(1)}, bf16[1024,128]{1,0:T(8,128)(2,1)S(1)}, u32[]{:S(2)}, u32[]{:S(2)}) collective-permute-start(bf16[1024,128]{1,0:T(8,128)(2,1)S(1)} %add_convert_fusion.9), channel_id=1, source_target_pairs={{0,2},{1,3},{2,4},{3,5},{4,6},{5,7},{6,8},{7,9},{8,10},{9,11},{10,... | collective-permute-start | bytes 786440 | tf_op jit(solution)/shard_map/ppermute | solution.py:181

commit v6 on v5

--- a/solution.py
+++ b/solution.py
@@ -15,13 +15,14 @@
 vmem = functools.partial(pl.BlockSpec, memory_space=pltpu.VMEM)
 
 
-def call(kernel, outs, operands, in_specs, scratch=(), flops=0, limit=VMEM_BYTES, out_space=pltpu.VMEM):
+def call(kernel, outs, operands, in_specs, scratch=(), flops=0, limit=VMEM_BYTES, out_space=pltpu.VMEM, aliases={}):
     return pl.pallas_call(
         kernel,
         out_shape=outs,
         in_specs=in_specs,
         out_specs=[pl.BlockSpec(memory_space=out_space)] * len(outs),
         scratch_shapes=list(scratch),
+        input_output_aliases=aliases,
         compiler_params=pltpu.CompilerParams(vmem_limit_bytes=limit),
         cost_estimate=pl.CostEstimate(flops=flops, bytes_accessed=0, transcendentals=0),
     )(*operands)
@@ -175,6 +176,35 @@
     )
 
 
+def finished(terms, total, first, result=None):
+    rows, share = terms[0].shape
+    part = rows // 2
+
+    def kernel(near_ref, right_ref, left_ref, *refs):
+        out, held, sems = refs[-3:]
+        copies = []
+        for i in range(2):
+            at = pl.ds(i * part, part)
+            added = near_ref[at, :] + right_ref[at, :].astype(jnp.float32) + left_ref[at, :].astype(jnp.float32)
+            held[at, :] = added.astype(held.dtype)
+            place = pl.ds(first + i * part, part)
+            copies.append(pltpu.make_async_copy(held.at[at], out.at[place], sems.at[i]))
+            copies[-1].start()
+        for copy in copies:
+            copy.wait()
+
+    earlier = () if result is None else (result,)
+    return call(
+        kernel,
+        [jax.ShapeDtypeStruct((total, share), jnp.bfloat16)],
+        (*terms, *earlier),
+        [vmem()] * 3 + [pl.BlockSpec(memory_space=pltpu.HBM)] * len(earlier),
+        [pltpu.VMEM((rows, share), jnp.bfloat16), pltpu.SemaphoreType.DMA((2,))],
+        out_space=pltpu.HBM,
+        aliases={3: 0} if earlier else {},
+    )[0]
+
+
 def along_z(block, distance):
     count = lax.axis_size("depth") // 2
     route = [(z * 2 + c, (z + distance) % count * 2 + c) for z in range(count) for c in range(2)]
@@ -257,9 +287,8 @@
     ra, lb = along_z(sa, 1), along_z(sb, -1)
     (enda,) = dots(later(three_a, sa), dens, [(rows_a, (0,), (f32,))])
     (endb,) = dots(later(three_b, sb), dens, [(rows_b, (0,), (f32,))])
-    top = enda + la.astype(f32) + ra.astype(f32)
-    bottom = endb + rb.astype(f32) + lb.astype(f32)
-    return jnp.concatenate([top.astype(bf16), bottom.astype(bf16)])
+    lower = finished((endb, rb, lb), n, rows_a)
+    return finished((enda, ra, la), n, 0, lower)
 
 
 def solution(mesh):

time: 80.2 us -> 80 us (level)
  Pallas kernels: 9.39 us -> 10.9 us
  other arithmetic: 1.64 us -> 0.6 us
    pallas_call x12 -> x14, Pallas kernels: 9.39 us -> 10.9 us  [call(): pl.pallas_call(kernel, out_shape=outs, in_specs=in_specs, out_specs=[pl.B...]
    concatenate x1 -> x0, other arithmetic: 0.83 us -> none  [on_device(): return jnp.concatenate([top.astype(bf16), bottom.astype(bf16)])]
  transfers between devices with their start and end apart: 25 -> 25, of which waited for: 15 -> 13; matrix products, arithmetic and copies ran while one was open for 2% -> 2% of each run, Pallas kernels for 8% -> 9%
where the time goes in v6:
time: 80 us; the launch traced here: 79.9 us
  waiting for transfers between devices  34.9 us (44%)
  starting transfers between devices  32 us (40%)
  Pallas kernels  10.9 us (14%)
  local copies, waits for them, and re-layouts  1.01 us (1%)
    ppermute x14, starting transfers between devices, along_z(): return lax.ppermute(block, 'depth', route)  23.8 us
    ppermute x14, waiting for transfers between devices, along_z(): return lax.ppermute(block, 'depth', route)  18.4 us
    ppermute x6, waiting for transfers between devices, opposed(): return lax.ppermute(block, (axis, 'depth'), route)  16.5 us
    pallas_call x14, Pallas kernels, call(): pl.pallas_call(kernel, out_shape=outs, in_specs=in_specs, out_specs=[pl.B...  10.9 us
    ppermute x6, starting transfers between devices, opposed(): return lax.ppermute(block, (axis, 'depth'), route)  7.35 us
  transfers between devices with their start and end apart: 25, of which 13 were waited for; matrix products, arithmetic and copies ran while one was open for 2% of the time, Pallas kernels for 9%

profile of v6, /device:TPU:24, one launch (start us, length us, event | category | flops | bytes accessed | tf_op | source)
XLA Modules:
  0.0 79.9 jit_solution(9682160764631502543)
XLA Ops:
  0.0 2.2 %shard_map.55 = (bf16[2048,128]{1,0:T(8,128)(2,1)}, bf16[1024,128]{1,0:T(8,128)(2,1)}, bf16[1024,128]{1,0:T(8,128)(2,1)}) custom-call(bf16[2048,128]{1,0:T(8,128)(2,1)} %three_hbm.1, s32[4,64]{1,0:T(4,128)} %bitcast.1, bf16[128,2048]{1,0:T(8,128)(2,1)} %dens_hbm.1, s32[4,64]{1,0:T(4,128)} %maskd_hbm.1, s32[4]{0:T(128)} %sizes_hbm.1), custom_call_target="tpu_custom_call" | custom-call | tf_op jit(solution)/shard_map/pallas_call | solution.py:19
  2.2 0.1 collective-permute-start.1
  2.3 1.6 %collective-permute-start.4 = (bf16[2048,128]{1,0:T(8,128)(2,1)}, bf16[2048,128]{1,0:T(8,128)(2,1)S(1)}, u32[]{:S(2)}, u32[]{:S(2)}) collective-permute-start(bf16[2048,128]{1,0:T(8,128)(2,1)} %get-tuple-element.55.refs_0_), channel_id=1, source_target_pairs={{0,64},{1,193},{2,66},{3,195},{4,68},{5,197},{6,70},{7,199},{8,72}... | collective-permute-start | bytes 1572872 | tf_op jit(solution)/shard_map/ppermute | solution.py:225
  3.9 1.0 %constant_dynamic-update-slice_fusion.1 = bf16[2048,128]{1,0:T(8,128)(2,1)S(1)} fusion(bf16[1024,128]{1,0:T(8,128)(2,1)} %get-tuple-element.33), kind=kLoop, calls=%fused_computation.11 | loop fusion | bytes 524288
  4.9 1.2 %collective-permute-start.9 = (bf16[2048,128]{1,0:T(8,128)(2,1)S(1)}, bf16[2048,128]{1,0:T(8,128)(2,1)S(1)}, u32[]{:S(2)}, u32[]{:S(2)}) collective-permute-start(bf16[2048,128]{1,0:T(8,128)(2,1)S(1)} %constant_dynamic-update-slice_fusion.refs_0_), channel_id=1, source_target_pairs={{0,16},{1,49},{2,18},{3,51},{4,20},{5,53},{6,22},{7,55},{8,24},{9,... | collective-permute-start | bytes 1572872 | tf_op jit(solution)/shard_map/ppermute | solution.py:225
  6.1 0.7 collective-permute-start.3
  6.9 1.8 %collective-permute-start = (bf16[2048,128]{1,0:T(8,128)(2,1)}, bf16[2048,128]{1,0:T(8,128)(2,1)S(1)}, u32[]{:S(2)}, u32[]{:S(2)}) collective-permute-start(bf16[2048,128]{1,0:T(8,128)(2,1)} %get-tuple-element.55.refs_0_), channel_id=1, source_target_pairs={{0,192},{1,65},{2,194},{3,67},{4,196},{5,69},{6,198},{7,71},{8,200... | collective-permute-start | bytes 1572872 | tf_op jit(solution)/shard_map/ppermute | solution.py:225
  8.7 0.3 collective-permute-start.2
  9.0 6.1 %collective-permute-done.4.refs_6_ = bf16[2048,128]{1,0:T(8,128)(2,1)S(1)} collective-permute-done((bf16[2048,128]{1,0:T(8,128)(2,1)}, bf16[2048,128]{1,0:T(8,128)(2,1)S(1)}, u32[]{:S(2)}, u32[]{:S(2)}) %collective-permute-start.4) | collective-permute-done | bytes 524320 | tf_op jit(solution)/shard_map/ppermute | solution.py:225
  15.0 1.4 %collective-permute-start.6 = (bf16[2048,128]{1,0:T(8,128)(2,1)S(1)}, bf16[2048,128]{1,0:T(8,128)(2,1)S(1)}, u32[]{:S(2)}, u32[]{:S(2)}) collective-permute-start(bf16[2048,128]{1,0:T(8,128)(2,1)S(1)} %collective-permute-done.4.refs_6_), channel_id=1, source_target_pairs={{0,64},{1,193},{2,66},{3,195},{4,68},{5,197},{6,70},{7,199},{8,72}... | collective-permute-start | bytes 1572872 | tf_op jit(solution)/shard_map/ppermute | solution.py:225
  16.5 2.3 %collective-permute-done.9.refs_3_ = bf16[2048,128]{1,0:T(8,128)(2,1)S(1)} collective-permute-done((bf16[2048,128]{1,0:T(8,128)(2,1)S(1)}, bf16[2048,128]{1,0:T(8,128)(2,1)S(1)}, u32[]{:S(2)}, u32[]{:S(2)}) %collective-permute-start.9) | collective-permute-done | bytes 524320 | tf_op jit(solution)/shard_map/ppermute | solution.py:225
  18.8 1.1 %collective-permute-start.10 = (bf16[2048,128]{1,0:T(8,128)(2,1)S(1)}, bf16[2048,128]{1,0:T(8,128)(2,1)S(1)}, u32[]{:S(2)}, u32[]{:S(2)}) collective-permute-start(bf16[2048,128]{1,0:T(8,128)(2,1)S(1)} %collective-permute-done.9.refs_3_), channel_id=1, source_target_pairs={{0,16},{1,49},{2,18},{3,51},{4,20},{5,53},{6,22},{7,55},{8,24},{9,... | collective-permute-start | bytes 1572872 | tf_op jit(solution)/shard_map/ppermute | solution.py:225
  19.8 1.6 %collective-permute-done.2.refs_1_ = bf16[2048,128]{1,0:T(8,128)(2,1)S(1)} collective-permute-done((bf16[2048,128]{1,0:T(8,128)(2,1)S(1)}, bf16[2048,128]{1,0:T(8,128)(2,1)S(1)}, u32[]{:S(2)}, u32[]{:S(2)}) %collective-permute-start.2) | collective-permute-done | bytes 524320 | tf_op jit(solution)/shard_map/ppermute | solution.py:225
  21.5 4.0 %collective-permute-done.6.refs_4_ = bf16[2048,128]{1,0:T(8,128)(2,1)S(1)} collective-permute-done((bf16[2048,128]{1,0:T(8,128)(2,1)S(1)}, bf16[2048,128]{1,0:T(8,128)(2,1)S(1)}, u32[]{:S(2)}, u32[]{:S(2)}) %collective-permute-start.6) | collective-permute-done | bytes 524320 | tf_op jit(solution)/shard_map/ppermute | solution.py:225
  25.4 2.5 %collective-permute-done.10.refs_2_ = bf16[2048,128]{1,0:T(8,128)(2,1)S(1)} collective-permute-done((bf16[2048,128]{1,0:T(8,128)(2,1)S(1)}, bf16[2048,128]{1,0:T(8,128)(2,1)S(1)}, u32[]{:S(2)}, u32[]{:S(2)}) %collective-permute-start.10) | collective-permute-done | bytes 524320 | tf_op jit(solution)/shard_map/ppermute | solution.py:225
  28.0 0.2 shard_map.56.refs_8_
  28.2 0.7 shard_map.57
  28.9 5.9 %collective-permute-start.18 = (bf16[1024,128]{1,0:T(8,128)(2,1)S(1)}, bf16[1024,128]{1,0:T(8,128)(2,1)S(1)}, u32[]{:S(2)}, u32[]{:S(2)}) collective-permute-start(bf16[1024,128]{1,0:T(8,128)(2,1)S(1)} %shard_map.57), channel_id=1, source_target_pairs={{0,14},{1,15},{2,0},{3,1},{4,2},{5,3},{6,4},{7,5},{8,6},{9,7},{10,... | collective-permute-start | bytes 786440 | tf_op jit(solution)/shard_map/ppermute | solution.py:211
  34.8 0.7 shard_map.58
  35.5 0.1 collective-permute-start.11
  35.6 0.7 shard_map.59
  36.3 3.3 %collective-permute-start.15 = (bf16[1024,128]{1,0:T(8,128)(2,1)S(1)}, bf16[1024,128]{1,0:T(8,128)(2,1)S(1)}, u32[]{:S(2)}, u32[]{:S(2)}) collective-permute-start(bf16[1024,128]{1,0:T(8,128)(2,1)S(1)} %get-tuple-element.48), channel_id=1, source_target_pairs={{0,14},{1,15},{2,0},{3,1},{4,2},{5,3},{6,4},{7,5},{8,6},{9,7},{10,... | collective-permute-start | bytes 786440 | tf_op jit(solution)/shard_map/ppermute | solution.py:211
  39.6 0.7 shard_map.63
  40.3 0.3 collective-permute-start.21
  40.6 0.8 %collective-permute-done.18 = bf16[1024,128]{1,0:T(8,128)(2,1)S(1)} collective-permute-done((bf16[1024,128]{1,0:T(8,128)(2,1)S(1)}, bf16[1024,128]{1,0:T(8,128)(2,1)S(1)}, u32[]{:S(2)}, u32[]{:S(2)}) %collective-permute-start.18) | collective-permute-done | bytes 262176 | tf_op jit(solution)/shard_map/ppermute | solution.py:211
  41.5 3.8 %collective-permute-start.19 = (bf16[1024,128]{1,0:T(8,128)(2,1)S(1)}, bf16[1024,128]{1,0:T(8,128)(2,1)S(1)}, u32[]{:S(2)}, u32[]{:S(2)}) collective-permute-start(bf16[1024,128]{1,0:T(8,128)(2,1)S(1)} %add_convert_fusion.4), channel_id=1, source_target_pairs={{0,14},{1,15},{2,0},{3,1},{4,2},{5,3},{6,4},{7,5},{8,6},{9,7},{10,... | collective-permute-start | bytes 786440 | tf_op jit(solution)/shard_map/ppermute | solution.py:211
  45.2 0.7 collective-permute-done.11
  46.0 0.1 collective-permute-start.12
  46.1 0.7 shard_map.64
  46.8 4.7 %collective-permute-done.21 = bf16[1024,128]{1,0:T(8,128)(2,1)S(1)} collective-permute-done((bf16[1024,128]{1,0:T(8,128)(2,1)S(1)}, bf16[1024,128]{1,0:T(8,128)(2,1)S(1)}, u32[]{:S(2)}, u32[]{:S(2)}) %collective-permute-start.21) | collective-permute-done | bytes 262176 | tf_op jit(solution)/shard_map/ppermute | solution.py:211
  51.6 0.1 collective-permute-start.22
  51.7 0.7 shard_map.60
  52.5 3.3 %collective-permute-start.16 = (bf16[1024,128]{1,0:T(8,128)(2,1)S(1)}, bf16[1024,128]{1,0:T(8,128)(2,1)S(1)}, u32[]{:S(2)}, u32[]{:S(2)}) collective-permute-start(bf16[1024,128]{1,0:T(8,128)(2,1)S(1)} %add_convert_fusion.6), channel_id=1, source_target_pairs={{0,14},{1,15},{2,0},{3,1},{4,2},{5,3},{6,4},{7,5},{8,6},{9,7},{10,... | collective-permute-start | bytes 786440 | tf_op jit(solution)/shard_map/ppermute | solution.py:211
  55.9 0.3 collective-permute-start.20
  56.1 1.0 %collective-permute-done.12 = bf16[1024,128]{1,0:T(8,128)(2,1)S(1)} collective-permute-done((bf16[1024,128]{1,0:T(8,128)(2,1)S(1)}, bf16[1024,128]{1,0:T(8,128)(2,1)S(1)}, u32[]{:S(2)}, u32[]{:S(2)}) %collective-permute-start.12) | collective-permute-done | bytes 262176 | tf_op jit(solution)/shard_map/ppermute | solution.py:211
  57.2 0.9 %collective-permute-start.13 = (bf16[1024,128]{1,0:T(8,128)(2,1)S(1)}, bf16[1024,128]{1,0:T(8,128)(2,1)S(1)}, u32[]{:S(2)}, u32[]{:S(2)}) collective-permute-start(bf16[1024,128]{1,0:T(8,128)(2,1)S(1)} %add_convert_fusion.8), channel_id=1, source_target_pairs={{0,2},{1,3},{2,4},{3,5},{4,6},{5,7},{6,8},{7,9},{8,10},{9,11},{10,... | collective-permute-start | bytes 786440 | tf_op jit(solution)/shard_map/ppermute | solution.py:211
  58.1 0.7 shard_map.65
  58.8 4.0 %collective-permute-done.22 = bf16[1024,128]{1,0:T(8,128)(2,1)S(1)} collective-permute-done((bf16[1024,128]{1,0:T(8,128)(2,1)S(1)}, bf16[1024,128]{1,0:T(8,128)(2,1)S(1)}, u32[]{:S(2)}, u32[]{:S(2)}) %collective-permute-start.22) | collective-permute-done | bytes 262176 | tf_op jit(solution)/shard_map/ppermute | solution.py:211
  62.9 0.7 shard_map.61
  63.7 3.3 %collective-permute-start.17 = (bf16[1024,128]{1,0:T(8,128)(2,1)S(1)}, bf16[1024,128]{1,0:T(8,128)(2,1)S(1)}, u32[]{:S(2)}, u32[]{:S(2)}) collective-permute-start(bf16[1024,128]{1,0:T(8,128)(2,1)S(1)} %add_convert_fusion.5), channel_id=1, source_target_pairs={{0,14},{1,15},{2,0},{3,1},{4,2},{5,3},{6,4},{7,5},{8,6},{9,7},{10,... | collective-permute-start | bytes 786440 | tf_op jit(solution)/shard_map/ppermute | solution.py:211
  67.1 2.4 %collective-permute-start.24 = (bf16[1024,128]{1,0:T(8,128)(2,1)S(1)}, bf16[1024,128]{1,0:T(8,128)(2,1)S(1)}, u32[]{:S(2)}, u32[]{:S(2)}) collective-permute-start(bf16[1024,128]{1,0:T(8,128)(2,1)S(1)} %add_convert_fusion.2), channel_id=1, source_target_pairs={{0,14},{1,15},{2,0},{3,1},{4,2},{5,3},{6,4},{7,5},{8,6},{9,7},{10,... | collective-permute-start | bytes 786440 | tf_op jit(solution)/shard_map/ppermute | solution.py:211
  69.6 0.7 shard_map.66.near_ref
  70.3 0.7 shard_map.62.near_ref
  71.0 3.0 %collective-permute-done.23.right_ref = bf16[1024,128]{1,0:T(8,128)(2,1)S(1)} collective-permute-done((bf16[1024,128]{1,0:T(8,128)(2,1)S(1)}, bf16[1024,128]{1,0:T(8,128)(2,1)S(1)}, u32[]{:S(2)}, u32[]{:S(2)}) %collective-permute-start.23) | collective-permute-done | bytes 262176 | tf_op jit(solution)/shard_map/ppermute | solution.py:211
  74.0 2.8 %collective-permute-done.24.left_ref = bf16[1024,128]{1,0:T(8,128)(2,1)S(1)} collective-permute-done((bf16[1024,128]{1,0:T(8,128)(2,1)S(1)}, bf16[1024,128]{1,0:T(8,128)(2,1)S(1)}, u32[]{:S(2)}, u32[]{:S(2)}) %collective-permute-start.24) | collective-permute-done | bytes 262176 | tf_op jit(solution)/shard_map/ppermute | solution.py:211
  76.8 0.8 shard_map.67.refs_0_
  77.6 1.3 %collective-permute-done.14.right_ref = bf16[1024,128]{1,0:T(8,128)(2,1)S(1)} collective-permute-done((bf16[1024,128]{1,0:T(8,128)(2,1)S(1)}, bf16[1024,128]{1,0:T(8,128)(2,1)S(1)}, u32[]{:S(2)}, u32[]{:S(2)}) %collective-permute-start.14) | collective-permute-done | bytes 262176 | tf_op jit(solution)/shard_map/ppermute | solution.py:211
  79.0 0.8 shard_map.68
  (30 shorter events, 0.9 us)
Async XLA Ops:
  2.2 2.6 %collective-permute-start.1 = (bf16[1024,128]{1,0:T(8,128)(2,1)}, bf16[1024,128]{1,0:T(8,128)(2,1)S(1)}, u32[]{:S(2)}, u32[]{:S(2)}) collective-permute-start(bf16[1024,128]{1,0:T(8,128)(2,1)} %get-tuple-element.34), channel_id=1, source_target_pairs={{0,1},{1,0},{2,3},{3,2},{4,5},{5,4},{6,7},{7,6},{8,9},{9,8},{10,11... | collective-permute-start | bytes 786440 | tf_op jit(solution)/shard_map/ppermute | solution.py:215
  2.3 12.7 %collective-permute-start.4 = (bf16[2048,128]{1,0:T(8,128)(2,1)}, bf16[2048,128]{1,0:T(8,128)(2,1)S(1)}, u32[]{:S(2)}, u32[]{:S(2)}) collective-permute-start(bf16[2048,128]{1,0:T(8,128)(2,1)} %get-tuple-element.55.refs_0_), channel_id=1, source_target_pairs={{0,64},{1,193},{2,66},{3,195},{4,68},{5,197},{6,70},{7,199},{8,72}... | collective-permute-start | bytes 1572872 | tf_op jit(solution)/shard_map/ppermute | solution.py:225
  4.9 23.2 %copy-start = (bf16[2048,128]{1,0:T(8,128)(2,1)S(1)}, bf16[2048,128]{1,0:T(8,128)(2,1)}, u32[]{:S(2)}) copy-start(bf16[2048,128]{1,0:T(8,128)(2,1)} %get-tuple-element.55.refs_0_) | copy-start | bytes 1572868
  4.9 13.8 %collective-permute-start.9 = (bf16[2048,128]{1,0:T(8,128)(2,1)S(1)}, bf16[2048,128]{1,0:T(8,128)(2,1)S(1)}, u32[]{:S(2)}, u32[]{:S(2)}) collective-permute-start(bf16[2048,128]{1,0:T(8,128)(2,1)S(1)} %constant_dynamic-update-slice_fusion.refs_0_), channel_id=1, source_target_pairs={{0,16},{1,49},{2,18},{3,51},{4,20},{5,53},{6,22},{7,55},{8,24},{9,... | collective-permute-start | bytes 1572872 | tf_op jit(solution)/shard_map/ppermute | solution.py:225
  6.1 13.7 %collective-permute-start.3 = (bf16[2048,128]{1,0:T(8,128)(2,1)}, bf16[2048,128]{1,0:T(8,128)(2,1)S(1)}, u32[]{:S(2)}, u32[]{:S(2)}) collective-permute-start(bf16[2048,128]{1,0:T(8,128)(2,1)} %get-tuple-element.55.refs_0_), channel_id=1, source_target_pairs={{0,1},{1,0},{2,3},{3,2},{4,5},{5,4},{6,7},{7,6},{8,9},{9,8},{10,11... | collective-permute-start | bytes 1572872 | tf_op jit(solution)/shard_map/ppermute | solution.py:215
  6.9 13.0 %collective-permute-start = (bf16[2048,128]{1,0:T(8,128)(2,1)}, bf16[2048,128]{1,0:T(8,128)(2,1)S(1)}, u32[]{:S(2)}, u32[]{:S(2)}) collective-permute-start(bf16[2048,128]{1,0:T(8,128)(2,1)} %get-tuple-element.55.refs_0_), channel_id=1, source_target_pairs={{0,192},{1,65},{2,194},{3,67},{4,196},{5,69},{6,198},{7,71},{8,200... | collective-permute-start | bytes 1572872 | tf_op jit(solution)/shard_map/ppermute | solution.py:225
  8.7 12.7 %collective-permute-start.2 = (bf16[2048,128]{1,0:T(8,128)(2,1)S(1)}, bf16[2048,128]{1,0:T(8,128)(2,1)S(1)}, u32[]{:S(2)}, u32[]{:S(2)}) collective-permute-start(bf16[2048,128]{1,0:T(8,128)(2,1)S(1)} %constant_dynamic-update-slice_fusion.refs_0_), channel_id=1, source_target_pairs={{0,48},{1,17},{2,50},{3,19},{4,52},{5,21},{6,54},{7,23},{8,56},{9,... | collective-permute-start | bytes 1572872 | tf_op jit(solution)/shard_map/ppermute | solution.py:225
  15.0 10.4 %collective-permute-start.6 = (bf16[2048,128]{1,0:T(8,128)(2,1)S(1)}, bf16[2048,128]{1,0:T(8,128)(2,1)S(1)}, u32[]{:S(2)}, u32[]{:S(2)}) collective-permute-start(bf16[2048,128]{1,0:T(8,128)(2,1)S(1)} %collective-permute-done.4.refs_6_), channel_id=1, source_target_pairs={{0,64},{1,193},{2,66},{3,195},{4,68},{5,197},{6,70},{7,199},{8,72}... | collective-permute-start | bytes 1572872 | tf_op jit(solution)/shard_map/ppermute | solution.py:225
  18.8 9.2 %collective-permute-start.10 = (bf16[2048,128]{1,0:T(8,128)(2,1)S(1)}, bf16[2048,128]{1,0:T(8,128)(2,1)S(1)}, u32[]{:S(2)}, u32[]{:S(2)}) collective-permute-start(bf16[2048,128]{1,0:T(8,128)(2,1)S(1)} %collective-permute-done.9.refs_3_), channel_id=1, source_target_pairs={{0,16},{1,49},{2,18},{3,51},{4,20},{5,53},{6,22},{7,55},{8,24},{9,... | collective-permute-start | bytes 1572872 | tf_op jit(solution)/shard_map/ppermute | solution.py:225
  19.8 8.3 %collective-permute-start.5 = (bf16[2048,128]{1,0:T(8,128)(2,1)S(1)}, bf16[2048,128]{1,0:T(8,128)(2,1)S(1)}, u32[]{:S(2)}, u32[]{:S(2)}) collective-permute-start(bf16[2048,128]{1,0:T(8,128)(2,1)S(1)} %collective-permute-done.4.refs_6_), channel_id=1, source_target_pairs={{0,1},{1,0},{2,3},{3,2},{4,5},{5,4},{6,7},{7,6},{8,9},{9,8},{10,11... | collective-permute-start | bytes 1572872 | tf_op jit(solution)/shard_map/ppermute | solution.py:215
  21.5 6.7 %collective-permute-start.8 = (bf16[2048,128]{1,0:T(8,128)(2,1)S(1)}, bf16[2048,128]{1,0:T(8,128)(2,1)S(1)}, u32[]{:S(2)}, u32[]{:S(2)}) collective-permute-start(bf16[2048,128]{1,0:T(8,128)(2,1)S(1)} %collective-permute-done.refs_2_), channel_id=1, source_target_pairs={{0,1},{1,0},{2,3},{3,2},{4,5},{5,4},{6,7},{7,6},{8,9},{9,8},{10,11... | collective-permute-start | bytes 1572872 | tf_op jit(solution)/shard_map/ppermute | solution.py:215
  25.4 2.7 %collective-permute-start.7 = (bf16[2048,128]{1,0:T(8,128)(2,1)S(1)}, bf16[2048,128]{1,0:T(8,128)(2,1)S(1)}, u32[]{:S(2)}, u32[]{:S(2)}) collective-permute-start(bf16[2048,128]{1,0:T(8,128)(2,1)S(1)} %collective-permute-done.6.refs_4_), channel_id=1, source_target_pairs={{0,1},{1,0},{2,3},{3,2},{4,5},{5,4},{6,7},{7,6},{8,9},{9,8},{10,11... | collective-permute-start | bytes 1572872 | tf_op jit(solution)/shard_map/ppermute | solution.py:215
  28.9 12.5 %collective-permute-start.18 = (bf16[1024,128]{1,0:T(8,128)(2,1)S(1)}, bf16[1024,128]{1,0:T(8,128)(2,1)S(1)}, u32[]{:S(2)}, u32[]{:S(2)}) collective-permute-start(bf16[1024,128]{1,0:T(8,128)(2,1)S(1)} %shard_map.57), channel_id=1, source_target_pairs={{0,14},{1,15},{2,0},{3,1},{4,2},{5,3},{6,4},{7,5},{8,6},{9,7},{10,... | collective-permute-start | bytes 786440 | tf_op jit(solution)/shard_map/ppermute | solution.py:211
  35.5 10.4 %collective-permute-start.11 = (bf16[1024,128]{1,0:T(8,128)(2,1)S(1)}, bf16[1024,128]{1,0:T(8,128)(2,1)S(1)}, u32[]{:S(2)}, u32[]{:S(2)}) collective-permute-start(bf16[1024,128]{1,0:T(8,128)(2,1)S(1)} %shard_map.58), channel_id=1, source_target_pairs={{0,2},{1,3},{2,4},{3,5},{4,6},{5,7},{6,8},{7,9},{8,10},{9,11},{10,... | collective-permute-start | bytes 786440 | tf_op jit(solution)/shard_map/ppermute | solution.py:211
  36.3 16.1 %collective-permute-start.15 = (bf16[1024,128]{1,0:T(8,128)(2,1)S(1)}, bf16[1024,128]{1,0:T(8,128)(2,1)S(1)}, u32[]{:S(2)}, u32[]{:S(2)}) collective-permute-start(bf16[1024,128]{1,0:T(8,128)(2,1)S(1)} %get-tuple-element.48), channel_id=1, source_target_pairs={{0,14},{1,15},{2,0},{3,1},{4,2},{5,3},{6,4},{7,5},{8,6},{9,7},{10,... | collective-permute-start | bytes 786440 | tf_op jit(solution)/shard_map/ppermute | solution.py:211
  40.3 11.2 %collective-permute-start.21 = (bf16[1024,128]{1,0:T(8,128)(2,1)S(1)}, bf16[1024,128]{1,0:T(8,128)(2,1)S(1)}, u32[]{:S(2)}, u32[]{:S(2)}) collective-permute-start(bf16[1024,128]{1,0:T(8,128)(2,1)S(1)} %get-tuple-element.58), channel_id=1, source_target_pairs={{0,2},{1,3},{2,4},{3,5},{4,6},{5,7},{6,8},{7,9},{8,10},{9,11},{10,... | collective-permute-start | bytes 786440 | tf_op jit(solution)/shard_map/ppermute | solution.py:211
  41.5 14.3 %collective-permute-start.19 = (bf16[1024,128]{1,0:T(8,128)(2,1)S(1)}, bf16[1024,128]{1,0:T(8,128)(2,1)S(1)}, u32[]{:S(2)}, u32[]{:S(2)}) collective-permute-start(bf16[1024,128]{1,0:T(8,128)(2,1)S(1)} %add_convert_fusion.4), channel_id=1, source_target_pairs={{0,14},{1,15},{2,0},{3,1},{4,2},{5,3},{6,4},{7,5},{8,6},{9,7},{10,... | collective-permute-start | bytes 786440 | tf_op jit(solution)/shard_map/ppermute | solution.py:211
  46.0 11.2 %collective-permute-start.12 = (bf16[1024,128]{1,0:T(8,128)(2,1)S(1)}, bf16[1024,128]{1,0:T(8,128)(2,1)S(1)}, u32[]{:S(2)}, u32[]{:S(2)}) collective-permute-start(bf16[1024,128]{1,0:T(8,128)(2,1)S(1)} %add_convert_fusion.9), channel_id=1, source_target_pairs={{0,2},{1,3},{2,4},{3,5},{4,6},{5,7},{6,8},{7,9},{8,10},{9,11},{10,... | collective-permute-start | bytes 786440 | tf_op jit(solution)/shard_map/ppermute | solution.py:211
  51.6 11.2 %collective-permute-start.22 = (bf16[1024,128]{1,0:T(8,128)(2,1)S(1)}, bf16[1024,128]{1,0:T(8,128)(2,1)S(1)}, u32[]{:S(2)}, u32[]{:S(2)}) collective-permute-start(bf16[1024,128]{1,0:T(8,128)(2,1)S(1)} %add_convert_fusion.1), channel_id=1, source_target_pairs={{0,2},{1,3},{2,4},{3,5},{4,6},{5,7},{6,8},{7,9},{8,10},{9,11},{10,... | collective-permute-start | bytes 786440 | tf_op jit(solution)/shard_map/ppermute | solution.py:211
  52.5 11.2 %collective-permute-start.16 = (bf16[1024,128]{1,0:T(8,128)(2,1)S(1)}, bf16[1024,128]{1,0:T(8,128)(2,1)S(1)}, u32[]{:S(2)}, u32[]{:S(2)}) collective-permute-start(bf16[1024,128]{1,0:T(8,128)(2,1)S(1)} %add_convert_fusion.6), channel_id=1, source_target_pairs={{0,14},{1,15},{2,0},{3,1},{4,2},{5,3},{6,4},{7,5},{8,6},{9,7},{10,... | collective-permute-start | bytes 786440 | tf_op jit(solution)/shard_map/ppermute | solution.py:211
  55.9 11.2 %collective-permute-start.20 = (bf16[1024,128]{1,0:T(8,128)(2,1)S(1)}, bf16[1024,128]{1,0:T(8,128)(2,1)S(1)}, u32[]{:S(2)}, u32[]{:S(2)}) collective-permute-start(bf16[1024,128]{1,0:T(8,128)(2,1)S(1)} %add_convert_fusion.3), channel_id=1, source_target_pairs={{0,14},{1,15},{2,0},{3,1},{4,2},{5,3},{6,4},{7,5},{8,6},{9,7},{10,... | collective-permute-start | bytes 786440 | tf_op jit(solution)/shard_map/ppermute | solution.py:211
  57.2 12.2 %collective-permute-start.13 = (bf16[1024,128]{1,0:T(8,128)(2,1)S(1)}, bf16[1024,128]{1,0:T(8,128)(2,1)S(1)}, u32[]{:S(2)}, u32[]{:S(2)}) collective-permute-start(bf16[1024,128]{1,0:T(8,128)(2,1)S(1)} %add_convert_fusion.8), channel_id=1, source_target_pairs={{0,2},{1,3},{2,4},{3,5},{4,6},{5,7},{6,8},{7,9},{8,10},{9,11},{10,... | collective-permute-start | bytes 786440 | tf_op jit(solution)/shard_map/ppermute | solution.py:211
  62.8 11.2 %collective-permute-start.23 = (bf16[1024,128]{1,0:T(8,128)(2,1)S(1)}, bf16[1024,128]{1,0:T(8,128)(2,1)S(1)}, u32[]{:S(2)}, u32[]{:S(2)}) collective-permute-start(bf16[1024,128]{1,0:T(8,128)(2,1)S(1)} %add_convert_fusion), channel_id=1, source_target_pairs={{0,2},{1,3},{2,4},{3,5},{4,6},{5,7},{6,8},{7,9},{8,10},{9,11},{10,... | collective-permute-start | bytes 786440 | tf_op jit(solution)/shard_map/ppermute | solution.py:211
  63.7 13.9 %collective-permute-start.17 = (bf16[1024,128]{1,0:T(8,128)(2,1)S(1)}, bf16[1024,128]{1,0:T(8,128)(2,1)S(1)}, u32[]{:S(2)}, u32[]{:S(2)}) collective-permute-start(bf16[1024,128]{1,0:T(8,128)(2,1)S(1)} %add_convert_fusion.5), channel_id=1, source_target_pairs={{0,14},{1,15},{2,0},{3,1},{4,2},{5,3},{6,4},{7,5},{8,6},{9,7},{10,... | collective-permute-start | bytes 786440 | tf_op jit(solution)/shard_map/ppermute | solution.py:211
  67.1 9.7 %collective-permute-start.24 = (bf16[1024,128]{1,0:T(8,128)(2,1)S(1)}, bf16[1024,128]{1,0:T(8,128)(2,1)S(1)}, u32[]{:S(2)}, u32[]{:S(2)}) collective-permute-start(bf16[1024,128]{1,0:T(8,128)(2,1)S(1)} %add_convert_fusion.2), channel_id=1, source_target_pairs={{0,14},{1,15},{2,0},{3,1},{4,2},{5,3},{6,4},{7,5},{8,6},{9,7},{10,... | collective-permute-start | bytes 786440 | tf_op jit(solution)/shard_map/ppermute | solution.py:211
  69.5 9.4 %collective-permute-start.14 = (bf16[1024,128]{1,0:T(8,128)(2,1)S(1)}, bf16[1024,128]{1,0:T(8,128)(2,1)S(1)}, u32[]{:S(2)}, u32[]{:S(2)}) collective-permute-start(bf16[1024,128]{1,0:T(8,128)(2,1)S(1)} %add_convert_fusion.7), channel_id=1, source_target_pairs={{0,2},{1,3},{2,4},{3,5},{4,6},{5,7},{6,8},{7,9},{8,10},{9,11},{10,... | collective-permute-start | bytes 786440 | tf_op jit(solution)/shard_map/ppermute | solution.py:211
